TPU v7x, 512 devices: a whole 4x4x16 slice. The times are simulated.
512 devices in a mesh: outer: 16 (over y, x), inner: 32 (over z, core).
Axes of the slice: x: 4, y: 4, z: 16, core: 2. Of those that a mesh axis runs over, the one named last changes fastest.
Arguments:
- start_state: float32 [192, 512], replicated, may hold values from -6 to 6
- guess: float32 [512, 192, 512], P(('outer', 'inner')), may hold values from -6 to 6
- weight_in: bfloat16 [1024, 512, 1024], P(('outer', 'inner')), may hold values from -0.25 to 0.25
- weight_out: bfloat16 [1024, 1024, 512], P(('outer', 'inner')), may hold values from -0.1875 to 0.1875
- norm_gain: float32 [1024, 512], P(('outer', 'inner')), may hold values from 0.1 to 1.9
- coarse_gain: float32 [16, 512], P('outer'), may hold values from 0.6 to 1
Outputs:
- final_states: float32 [512, 192, 512], P(('outer', 'inner'))
All inputs are finite; a program needn't handle non-finite values.
Results may differ from a plain program's by a relative error of at most 0.006.
Values sent between devices are 32-bit elements; how exact they have to be, the bound alone decides.
No kernel may reach another device: no remote copies, remote signals or barrier semaphores. Data moves between devices by JAX's collectives and lax.ppermute only.
A program may use at most 64 MiB of HBM per device.

v0:
```python
import jax
import jax.numpy as jnp
from jax import lax
from jax.sharding import PartitionSpec as P

step_size = 0.5


def shifted(value, axis, by):
    peers = lax.axis_size(axis)
    pairs = [(i, i + by) for i in range(peers) if 0 <= i + by < peers]
    return lax.ppermute(value, axis, pairs)


def in_blocks(value, dim, peers):
    dims = value.shape
    parts = value.reshape(*dims[:dim], peers, dims[dim] // peers, *dims[dim + 1 :])
    return jnp.moveaxis(parts, dim, 0)


def summed_on_arrival(value, axis, dim):
    peers = lax.axis_size(axis)
    parts = lax.all_to_all(in_blocks(value, dim, peers), axis, 0, 0, tiled=True)
    return jnp.sum(parts, axis=0)


def in_one_piece(arrays, axis, dim, along):
    ends, at = ([], 0)
    for a in arrays[:-1]:
        at += a.shape[along]
        ends.append(at)
    both = jnp.concatenate(arrays, axis=along)
    return tuple(jnp.split(lax.all_gather(both, axis, axis=dim, tiled=True), ends, axis=along))


def layer(state, weight_in, weight_out, gain):
    meansq = jnp.mean(state * state, axis=-1, keepdims=True)
    normed = (state * lax.rsqrt(meansq + 1e-06) * gain).astype(jnp.bfloat16)
    hidden = jax.nn.gelu(jnp.dot(normed, weight_in, preferred_element_type=jnp.float32)).astype(
        jnp.bfloat16
    )
    return state + step_size * jnp.dot(hidden, weight_out, preferred_element_type=jnp.float32)


def coarse(gain, defect_part):
    gains, terms = (
        lax.all_gather(gain, "outer", axis=0, tiled=True),
        lax.all_gather(defect_part, "outer", axis=0, tiled=True),
    )
    groups = gains.shape[0]
    terms = terms.reshape(groups, defect_part.shape[0], defect_part.shape[1])
    group = lax.axis_index("outer")

    def advance(index, carry):
        running, saved = carry
        saved = jnp.where(index == group, running, saved)
        running = gains[index][None] * running + terms[index]
        return (running, saved)

    zeros = jnp.zeros_like(defect_part)
    unused, earlier = lax.fori_loop(0, groups, advance, (zeros, zeros))
    current = gain * earlier + defect_part
    return (earlier, current)


def per_device(start_state, guess, weight_in, weight_out, norm_gain, coarse_gain):
    is_first = lax.axis_index(("outer", "inner")) == 0

    def relax(states):
        received = shifted(states, ("outer", "inner"), 1)
        state = jnp.where(is_first, start_state, received)
        for level in range(weight_in.shape[0]):
            state = layer(state, weight_in[level], weight_out[level], norm_gain[level])
        return state

    first = relax(guess[0])
    second = relax(first)
    third = relax(second)
    defect = third - second
    inner_count = lax.axis_size("inner")
    summed = summed_on_arrival(defect, "inner", 0) / inner_count
    part_early, part_now = coarse(coarse_gain, summed)
    earlier, current = in_one_piece((part_early, part_now), "inner", 0, 1)
    weight = (lax.axis_index("inner") + 1).astype(jnp.float32) / inner_count
    corrected = third + weight * current + (1.0 - weight) * earlier
    return relax(corrected)[None]


def solution(mesh):
    placed = (
        P(),
        P(("outer", "inner"), None, None),
        P(("outer", "inner"), None, None),
        P(("outer", "inner"), None, None),
        P(("outer", "inner"), None),
        P("outer", None),
    )
    return jax.shard_map(
        per_device,
        mesh=mesh,
        in_specs=placed,
        out_specs=P(("outer", "inner"), None, None),
        check_vma=False,
    )
```

profile of v0, /device:TPU:1, one launch (start us, length us, event | category | flops | bytes accessed | tf_op | source)
XLA Modules:
  0.0 170.1 jit_solution(5017549568948448045)
XLA Ops:
  0.0 4.9 %collective-permute-start = (f32[192,512]{1,0:T(8,128)}, f32[192,512]{1,0:T(8,128)S(1)}, u32[]{:S(2)}, u32[]{:S(2)}) collective-permute-start(f32[192,512]{1,0:T(8,128)} %bitcast.135), channel_id=1, source_target_pairs={{0,1},{1,2},{2,3},{3,4},{4,5},{5,6},{6,7},{7,8},{8,9},{9,10},{10,1... | collective-permute-start | bytes 1179656 | tf_op jit(solution)/shard_map/ppermute | solution.py:12
  4.9 0.8 fusion.267
  5.7 4.2 %collective-permute-done = f32[192,512]{1,0:T(8,128)S(1)} collective-permute-done((f32[192,512]{1,0:T(8,128)}, f32[192,512]{1,0:T(8,128)S(1)}, u32[]{:S(2)}, u32[]{:S(2)}) %collective-permute-start) | collective-permute-done | bytes 393248 | tf_op jit(solution)/shard_map/ppermute | solution.py:12
  9.9 0.2 multiply_reduce_fusion.7
  10.1 0.0 copy-start.2
  10.1 3.3 %multiply_reduce_fusion.6 = (f32[192]{0:T(256)S(1)}, f32[192,512]{1,0:T(8,128)}) fusion(bf16[2,1024,512]{2,1,0:T(8,128)(2,1)} %param.11, bf16[2,512,1024]{2,1,0:T(8,128)(2,1)} %param.10, f32[512]{0:T(512)S(1)} %bitcast.131, f32[192]{0:T(256)S(1)} %add_rsqrt_fusion.7, f32[192,512]{1,0:T(8,128)} %param.8, f32[192,512]{1,0:T(8,128)S(1)} %collective-permute-done, ...), kind=kOutput, calls=%fused_computation.149 | convolution fusion | flops 405307200 | bytes 4068096 | tf_op jit(solution)/shard_map/dot_general | solution.py:42
  13.5 0.0 copy-done.2
  13.5 0.0 copy-start
  13.5 2.2 %fusion.1 = f32[192,512]{1,0:T(8,128)S(1)} fusion(f32[192,512]{1,0:T(8,128)} %get-tuple-element.153, bf16[2,1024,512]{2,1,0:T(8,128)(2,1)S(1)} %copy-done.2, bf16[2,512,1024]{2,1,0:T(8,128)(2,1)} %param.10, f32[512]{0:T(512)S(1)} %bitcast.127, f32[192]{0:T(256)S(1)} %add_rsqrt_fusion.6), kind=kOutput, calls=%fused_computation.12 | convolution fusion | flops 404914176 | bytes 3279872 | tf_op jit(solution)/shard_map/dot_general | solution.py:42
  15.7 4.3 %collective-permute-start.1 = (f32[192,512]{1,0:T(8,128)S(1)}, f32[192,512]{1,0:T(8,128)S(1)}, u32[]{:S(2)}, u32[]{:S(2)}) collective-permute-start(f32[192,512]{1,0:T(8,128)S(1)} %fusion.1), channel_id=1, source_target_pairs={{0,1},{1,2},{2,3},{3,4},{4,5},{5,6},{6,7},{7,8},{8,9},{9,10},{10,1... | collective-permute-start | bytes 1179656 | tf_op jit(solution)/shard_map/ppermute | solution.py:12
  20.0 4.7 %collective-permute-done.1 = f32[192,512]{1,0:T(8,128)S(1)} collective-permute-done((f32[192,512]{1,0:T(8,128)S(1)}, f32[192,512]{1,0:T(8,128)S(1)}, u32[]{:S(2)}, u32[]{:S(2)}) %collective-permute-start.1) | collective-permute-done | bytes 393248 | tf_op jit(solution)/shard_map/ppermute | solution.py:12
  24.7 0.0 copy-done
  24.7 0.1 multiply_reduce_fusion.5
  24.8 2.8 %multiply_reduce_fusion.4 = (f32[192]{0:T(256)S(1)}, f32[192,512]{1,0:T(8,128)}) fusion(bf16[2,1024,512]{2,1,0:T(8,128)(2,1)S(1)} %copy-done.2, bf16[2,512,1024]{2,1,0:T(8,128)(2,1)} %param.10, f32[192]{0:T(256)S(1)} %add_rsqrt_fusion.5, f32[512]{0:T(512)S(1)} %bitcast.132, f32[192,512]{1,0:T(8,128)S(1)} %copy-done, ...), kind=kOutput, calls=%fused_computation.145 | convolution fusion | flops 405307200 | bytes 4068096 | tf_op jit(solution)/shard_map/dot_general | solution.py:42
  27.6 2.2 %fusion.3 = f32[192,512]{1,0:T(8,128)S(1)} fusion(f32[192,512]{1,0:T(8,128)} %get-tuple-element.155, bf16[2,1024,512]{2,1,0:T(8,128)(2,1)S(1)} %copy-done.2, bf16[2,512,1024]{2,1,0:T(8,128)(2,1)} %param.10, f32[192]{0:T(256)S(1)} %add_rsqrt_fusion.4, f32[512]{0:T(512)S(1)} %bitcast.128), kind=kOutput, calls=%fused_computation.14 | convolution fusion | flops 404914176 | bytes 3279872 | tf_op jit(solution)/shard_map/dot_general | solution.py:42
  29.8 0.0 copy-start.4
  29.8 4.4 %collective-permute-start.2 = (f32[192,512]{1,0:T(8,128)S(1)}, f32[192,512]{1,0:T(8,128)S(1)}, u32[]{:S(2)}, u32[]{:S(2)}) collective-permute-start(f32[192,512]{1,0:T(8,128)S(1)} %fusion.3), channel_id=1, source_target_pairs={{0,1},{1,2},{2,3},{3,4},{4,5},{5,6},{6,7},{7,8},{8,9},{9,10},{10,1... | collective-permute-start | bytes 1179656 | tf_op jit(solution)/shard_map/ppermute | solution.py:12
  34.2 4.7 %collective-permute-done.2 = f32[192,512]{1,0:T(8,128)S(1)} collective-permute-done((f32[192,512]{1,0:T(8,128)S(1)}, f32[192,512]{1,0:T(8,128)S(1)}, u32[]{:S(2)}, u32[]{:S(2)}) %collective-permute-start.2) | collective-permute-done | bytes 393248 | tf_op jit(solution)/shard_map/ppermute | solution.py:12
  38.9 0.0 copy-done.4
  38.9 0.1 multiply_reduce_fusion.3
  39.0 2.8 %multiply_reduce_fusion.2 = (f32[192]{0:T(256)S(1)}, f32[192,512]{1,0:T(8,128)}) fusion(bf16[2,1024,512]{2,1,0:T(8,128)(2,1)S(1)} %copy-done.2, bf16[2,512,1024]{2,1,0:T(8,128)(2,1)} %param.10, f32[192]{0:T(256)S(1)} %add_rsqrt_fusion.3, f32[512]{0:T(512)S(1)} %bitcast.133, f32[192,512]{1,0:T(8,128)S(1)} %copy-done, ...), kind=kOutput, calls=%fused_computation.141 | convolution fusion | flops 405307200 | bytes 4068096 | tf_op jit(solution)/shard_map/dot_general | solution.py:42
  41.8 0.0 copy-start.1
  41.8 2.3 %fusion.274 = (f32[192,512]{1,0:T(8,128)S(1)}, f32[192,512]{1,0:T(8,128)S(1)}) fusion(f32[192,512]{1,0:T(8,128)} %copy-done.4, f32[192,512]{1,0:T(8,128)} %get-tuple-element.157, bf16[2,1024,512]{2,1,0:T(8,128)(2,1)S(1)} %copy-done.2, bf16[2,512,1024]{2,1,0:T(8,128)(2,1)} %param.10, f32[192]{0:T(256)S(1)} %add_rsqrt_fusion.2, f32[512]{0:T(512)S(1)} %bitcast.129), kind=kOutput, calls=%fused_computation.249 | convolution fusion | flops 405012480 | bytes 4066304 | tf_op jit(solution)/shard_map/dot_general | solution.py:42
  44.1 0.8 reshape.70
  45.0 19.8 %all-to-all-start = ((f32[32,6,512]{2,1,0:T(8,128)}), f32[32,6,512]{2,1,0:T(8,128)S(1)}, u32[]{:S(2)}, u32[]{:S(2)}) async-start(f32[32,6,512]{2,1,0:T(8,128)} %reshape.70), calls=%async_computation | async-start | bytes 1048576 | tf_op jit(solution)/shard_map/all_to_all | solution.py:23
  64.8 0.0 copy-done.1
  64.9 22.2 %all-gather = f32[16,1,512]{2,1,0:T(1,128)S(1)} all-gather(f32[1,1,512]{2,1,0:T(1,128)S(1)} %bitcast.125), channel_id=1, replica_groups=mesh['outer'=16,'inner'=32] {'outer'}, dimensions={0}, use_global_device_ids=true | all-gather | bytes 34816 | tf_op jit(solution)/shard_map/all_gather | solution.py:47
  87.1 11.2 %all-to-all-done = f32[32,6,512]{2,1,0:T(8,128)S(1)} async-done(((f32[32,6,512]{2,1,0:T(8,128)}), f32[32,6,512]{2,1,0:T(8,128)S(1)}, u32[]{:S(2)}, u32[]{:S(2)}) %all-to-all-start) | async-done | bytes 393248 | tf_op jit(solution)/shard_map/all_to_all | solution.py:23
  98.3 0.1 reduce_sum.87
  98.4 20.9 %all-gather.1 = f32[16,6,512]{2,1,0:T(8,128)S(1)} all-gather(f32[1,6,512]{2,1,0:T(8,128)S(1)} %multiply_bitcast_fusion), channel_id=1, replica_groups=mesh['outer'=16,'inner'=32] {'outer'}, dimensions={0}, use_global_device_ids=true | all-gather | bytes 208896 | tf_op jit(solution)/shard_map/all_gather | solution.py:48
  119.3 0.9 while.16
  120.3 35.9 %all-gather.2 = f32[32,6,1024]{2,1,0:T(8,128)S(1)} all-gather(f32[1,6,1024]{2,1,0:T(8,128)S(1)} %maximum_bitcast_fusion), channel_id=1, replica_groups=mesh['outer'=16,'inner'=32] {'inner'}, dimensions={0}, use_global_device_ids=true | all-gather | bytes 811008 | tf_op jit(solution)/shard_map/all_gather | solution.py:33
  156.2 0.1 reshape.77
  156.3 0.1 fusion.169
  156.5 3.5 %collective-permute-start.3 = (f32[192,512]{1,0:T(8,128)S(1)}, f32[192,512]{1,0:T(8,128)S(1)}, u32[]{:S(2)}, u32[]{:S(2)}) collective-permute-start(f32[192,512]{1,0:T(8,128)S(1)} %fusion.169), channel_id=1, source_target_pairs={{0,1},{1,2},{2,3},{3,4},{4,5},{5,6},{6,7},{7,8},{8,9},{9,10},{10,1... | collective-permute-start | bytes 1179656 | tf_op jit(solution)/shard_map/ppermute | solution.py:12
  160.0 4.7 %collective-permute-done.3 = f32[192,512]{1,0:T(8,128)S(1)} collective-permute-done((f32[192,512]{1,0:T(8,128)S(1)}, f32[192,512]{1,0:T(8,128)S(1)}, u32[]{:S(2)}, u32[]{:S(2)}) %collective-permute-start.3) | collective-permute-done | bytes 393248 | tf_op jit(solution)/shard_map/ppermute | solution.py:12
  164.7 0.1 multiply_reduce_fusion.1
  164.8 0.0 copy-start.3
  164.8 2.6 %multiply_reduce_fusion = (f32[192]{0:T(256)S(1)}, f32[192,512]{1,0:T(8,128)S(1)}) fusion(bf16[2,1024,512]{2,1,0:T(8,128)(2,1)} %param.11, bf16[2,512,1024]{2,1,0:T(8,128)(2,1)} %param.10, f32[192]{0:T(256)S(1)} %add_rsqrt_fusion.1, f32[512]{0:T(512)S(1)} %bitcast.134, f32[192,512]{1,0:T(8,128)S(1)} %copy-done, f32[192,512]{1,0:T(8,128)S(1)} %collective-permute-done.3, ...), kind=kOutput, calls=%fused_computation.137 | convolution fusion | flops 405307200 | bytes 4068096 | tf_op jit(solution)/shard_map/dot_general | solution.py:42
  167.4 0.0 copy-done.3
  167.4 2.7 %fusion.8 = f32[1,192,512]{2,1,0:T(8,128)} fusion(f32[192,512]{1,0:T(8,128)S(1)} %get-tuple-element.161, bf16[2,1024,512]{2,1,0:T(8,128)(2,1)S(1)} %copy-done.3, bf16[2,512,1024]{2,1,0:T(8,128)(2,1)} %param.10, f32[192]{0:T(256)S(1)} %add_rsqrt_fusion, f32[512]{0:T(512)S(1)} %bitcast.130), kind=kOutput, calls=%fused_computation.19 | convolution fusion | flops 404914176 | bytes 3279872 | tf_op jit(solution)/shard_map/dot_general | solution.py:42
  (46 shorter events, 0.4 us)
Async XLA Ops:
  0.0 9.9 %collective-permute-start = (f32[192,512]{1,0:T(8,128)}, f32[192,512]{1,0:T(8,128)S(1)}, u32[]{:S(2)}, u32[]{:S(2)}) collective-permute-start(f32[192,512]{1,0:T(8,128)} %bitcast.135), channel_id=1, source_target_pairs={{0,1},{1,2},{2,3},{3,4},{4,5},{5,6},{6,7},{7,8},{8,9},{9,10},{10,1... | collective-permute-start | bytes 1179656 | tf_op jit(solution)/shard_map/ppermute | solution.py:12
  10.1 3.3 %copy-start.2 = (bf16[2,1024,512]{2,1,0:T(8,128)(2,1)S(1)}, bf16[2,1024,512]{2,1,0:T(8,128)(2,1)}, u32[]{:S(2)}) copy-start(bf16[2,1024,512]{2,1,0:T(8,128)(2,1)} %param.11) | copy-start | bytes 6291460
  13.5 11.2 %copy-start = (f32[192,512]{1,0:T(8,128)S(1)}, f32[192,512]{1,0:T(8,128)}, u32[]{:S(2)}) copy-start(f32[192,512]{1,0:T(8,128)} %param.8) | copy-start | bytes 1179652
  15.7 9.0 %collective-permute-start.1 = (f32[192,512]{1,0:T(8,128)S(1)}, f32[192,512]{1,0:T(8,128)S(1)}, u32[]{:S(2)}, u32[]{:S(2)}) collective-permute-start(f32[192,512]{1,0:T(8,128)S(1)} %fusion.1), channel_id=1, source_target_pairs={{0,1},{1,2},{2,3},{3,4},{4,5},{5,6},{6,7},{7,8},{8,9},{9,10},{10,1... | collective-permute-start | bytes 1179656 | tf_op jit(solution)/shard_map/ppermute | solution.py:12
  29.8 9.1 %copy-start.4 = (f32[192,512]{1,0:T(8,128)}, f32[192,512]{1,0:T(8,128)S(1)}, u32[]{:S(2)}) copy-start(f32[192,512]{1,0:T(8,128)S(1)} %fusion.3) | copy-start | bytes 1179652
  29.8 9.1 %collective-permute-start.2 = (f32[192,512]{1,0:T(8,128)S(1)}, f32[192,512]{1,0:T(8,128)S(1)}, u32[]{:S(2)}, u32[]{:S(2)}) collective-permute-start(f32[192,512]{1,0:T(8,128)S(1)} %fusion.3), channel_id=1, source_target_pairs={{0,1},{1,2},{2,3},{3,4},{4,5},{5,6},{6,7},{7,8},{8,9},{9,10},{10,1... | collective-permute-start | bytes 1179656 | tf_op jit(solution)/shard_map/ppermute | solution.py:12
  41.8 23.0 %copy-start.1 = (f32[1,512]{1,0:T(1,128)S(1)}, f32[1,512]{1,0:T(1,128)}, u32[]{:S(2)}) copy-start(f32[1,512]{1,0:T(1,128)} %param.13) | copy-start | bytes 6148
  45.0 53.3 %all-to-all-start = ((f32[32,6,512]{2,1,0:T(8,128)}), f32[32,6,512]{2,1,0:T(8,128)S(1)}, u32[]{:S(2)}, u32[]{:S(2)}) async-start(f32[32,6,512]{2,1,0:T(8,128)} %reshape.70), calls=%async_computation | async-start | bytes 1048576 | tf_op jit(solution)/shard_map/all_to_all | solution.py:23
  156.5 8.2 %collective-permute-start.3 = (f32[192,512]{1,0:T(8,128)S(1)}, f32[192,512]{1,0:T(8,128)S(1)}, u32[]{:S(2)}, u32[]{:S(2)}) collective-permute-start(f32[192,512]{1,0:T(8,128)S(1)} %fusion.169), channel_id=1, source_target_pairs={{0,1},{1,2},{2,3},{3,4},{4,5},{5,6},{6,7},{7,8},{8,9},{9,10},{10,1... | collective-permute-start | bytes 1179656 | tf_op jit(solution)/shard_map/ppermute | solution.py:12
  164.8 2.6 %copy-start.3 = (bf16[2,1024,512]{2,1,0:T(8,128)(2,1)S(1)}, bf16[2,1024,512]{2,1,0:T(8,128)(2,1)}, u32[]{:S(2)}) copy-start(bf16[2,1024,512]{2,1,0:T(8,128)(2,1)} %param.11) | copy-start | bytes 6291460
where the time goes:
time: 173 us; the launch traced here: 170 us
  blocking collectives  79.1 us (46%)
  starting transfers between devices  36.9 us (21%)
  waiting for transfers between devices  29.6 us (17%)
  matrix products  20.9 us (12%)
  local copies, waits for them, and re-layouts  1.91 us (1%)
    all_gather x1, blocking collectives, in_one_piece(): lax.all_gather(both, axis, axis=dim, tiled=True)  35.9 us
    all_gather x1, blocking collectives, coarse(): lax.all_gather(gain, 'outer', axis=0, tiled=True)  22.2 us
    all_gather x1, blocking collectives, coarse(): lax.all_gather(defect_part, 'outer', axis=0, tiled=True)  20.9 us
    dot_general x8, matrix products, layer(): jnp.dot(hidden, weight_out, preferred_element_type=jnp.float32)  20.9 us
    all_to_all x1, starting transfers between devices, summed_on_arrival(): parts = lax.all_to_all(in_blocks(value, dim, peers), axis, 0, 0, tiled=True)  19.8 us
    ppermute x4, waiting for transfers between devices, shifted(): return lax.ppermute(value, axis, pairs)  18.3 us
    ppermute x4, starting transfers between devices, shifted(): return lax.ppermute(value, axis, pairs)  17.1 us
    all_to_all x1, waiting for transfers between devices, summed_on_arrival(): parts = lax.all_to_all(in_blocks(value, dim, peers), axis, 0, 0, tiled=True)  11.2 us
  transfers between devices with their start and end apart: 5, of which 5 were waited for; matrix products, arithmetic and copies ran while one was open for 0% of the time, Pallas kernels for 0%

commit v1 on v0

v1 whole, which is shorter than its diff:
```python
import jax
import jax.numpy as jnp
from jax import lax
from jax.sharding import Mesh, PartitionSpec as P

step_size = 0.5
ALL = ("outer", "z", "core")


def from_odd(value):
    peers = lax.axis_size(ALL)
    return lax.ppermute(value, ALL, [(i, i + 1) for i in range(1, peers - 1, 2)])


def from_pair(value):
    return lax.all_gather(value, "core", axis=0)


def to_each(value, axis):
    peers = lax.axis_size(axis)
    copies = jnp.broadcast_to(value[None], (peers,) + value.shape)
    return lax.all_to_all(copies, axis, 0, 0, tiled=True)


def layer(state, weight_in, weight_out, gain):
    meansq = jnp.mean(state * state, axis=-1, keepdims=True)
    normed = (state * lax.rsqrt(meansq + 1e-06) * gain).astype(jnp.bfloat16)
    hidden = jax.nn.gelu(jnp.dot(normed, weight_in, preferred_element_type=jnp.float32)).astype(
        jnp.bfloat16
    )
    return state + step_size * jnp.dot(hidden, weight_out, preferred_element_type=jnp.float32)


def coarse(gain, part):
    places = lax.axis_size("z")
    groups = lax.axis_size("outer")
    count = places * lax.axis_size("core")
    rows = part.shape[0] // places
    blocks = part.reshape(places, rows, part.shape[1])
    own = jnp.sum(lax.all_to_all(blocks, "z", 0, 0, tiled=True), axis=0) / count
    heard = to_each(jnp.concatenate([own, gain], axis=0), "outer")
    group = lax.axis_index("outer")
    running = jnp.zeros_like(own)
    earlier = jnp.zeros_like(own)
    for index in range(groups):
        earlier = jnp.where(index == group, running, earlier)
        running = heard[index, rows:] * running + heard[index, :rows]
    current = gain * earlier + own
    both = jnp.concatenate([earlier, current], axis=1)
    both = lax.all_gather(both, "z", axis=0, tiled=True)
    both = lax.all_gather(both, "core", axis=0, tiled=True)
    return jnp.split(both, 2, axis=1)


def per_device(start_state, guess, weight_in, weight_out, norm_gain, coarse_gain):
    core = lax.axis_index("core")
    is_first = lax.axis_index(ALL) == 0
    is_odd = core == 1
    tokens = start_state.shape[0]

    def block(state):
        for level in range(weight_in.shape[0]):
            state = layer(state, weight_in[level], weight_out[level], norm_gain[level])
        return state

    def arrived(value):
        return jnp.where(is_first, start_state, value)

    guess_z = from_odd(guess[0])
    guess_pair = from_pair(guess[0])
    first = block(jnp.where(is_odd, guess_pair[0], arrived(guess_z)))
    first_z = from_odd(first)
    first_pair = from_pair(first)
    second_odd = block(first_pair[0])
    second_z = from_odd(second_odd)
    second_even = block(arrived(first_z))
    second_pair = from_pair(jnp.where(is_odd, second_odd, second_even))
    third = block(jnp.where(is_odd, second_pair[0], arrived(second_z)))
    third_pair = from_pair(third)
    third_z = from_odd(third)

    half = tokens // 2

    def mine(value):
        return lax.dynamic_slice_in_dim(value, core * half, half, 1)

    defects = mine(third_pair) - mine(second_pair)
    earlier, current = coarse(coarse_gain, defects[0] + defects[1])
    count = lax.axis_size("z") * lax.axis_size("core")
    weight = lax.axis_index(("z", "core")).astype(jnp.float32) / count
    moved = jnp.where(is_odd, third_pair[0], third_z)
    corrected = moved + weight * current + (1.0 - weight) * earlier
    return block(arrived(corrected))[None]


def solution(mesh):
    groups, inner = mesh.devices.shape
    fine = Mesh(mesh.devices.reshape(groups, inner // 2, 2), ALL)
    split = P(ALL, None, None)
    return jax.shard_map(
        per_device,
        mesh=fine,
        in_specs=(P(), split, split, split, P(ALL, None), P("outer", None)),
        out_specs=split,
        check_vma=False,
    )
```

time: 173 us -> 135 us (0.78); the launches traced: 170 us -> 134 us
  waiting for transfers between devices: 29.6 us -> 0.01 us
  starting transfers between devices: 36.9 us -> 27.6 us
  matrix products: 20.9 us -> 24 us
    all_to_all x0 -> x1, blocking collectives: none -> 27.5 us  [coarse(): own = jnp.sum(lax.all_to_all(blocks, 'z', 0, 0, tiled=True), axis=0) / count]
    all_gather x3 -> x6, blocking collectives: 79.1 us -> 52.3 us  [the longest x1 26.6 us: coarse(): both = lax.all_gather(both, 'z', axis=0, tiled=True)]
    ppermute x4, waiting for transfers between devices: 18.3 us -> 0.01 us  [from_odd(): lax.ppermute(value, ALL, [(i, i + 1) for i in range(1, peers - 1, 2)])]
    all_to_all x1, starting transfers between devices: 19.8 us -> 6.76 us  [to_each(): return lax.all_to_all(copies, axis, 0, 0, tiled=True)]
    all_to_all x1, waiting for transfers between devices: 11.2 us -> 0.01 us  [to_each(): return lax.all_to_all(copies, axis, 0, 0, tiled=True)]
    ppermute x4, starting transfers between devices: 17.1 us -> 20.9 us  [from_odd(): lax.ppermute(value, ALL, [(i, i + 1) for i in range(1, peers - 1, 2)])]
    dot_general x8 -> x10, matrix products: 20.9 us -> 24 us  [layer(): jnp.dot(hidden, weight_out, preferred_element_type=jnp.float32)]
  transfers between devices with their start and end apart: 5 -> 5, of which waited for: 5 -> 0; matrix products, arithmetic and copies ran while one was open for 0% -> 8% of each run, Pallas kernels for 0% -> 0%
where the time goes in v1:
time: 135 us; the launch traced here: 134 us
  blocking collectives  79.7 us (59%)
  starting transfers between devices  27.6 us (20%)
  matrix products  24 us (18%)
  local copies, waits for them, and re-layouts  1.6 us (1%)
    all_to_all x1, blocking collectives, coarse(): own = jnp.sum(lax.all_to_all(blocks, 'z', 0, 0, tiled=True), axis=0) / count  27.5 us
    all_gather x1, blocking collectives, coarse(): both = lax.all_gather(both, 'z', axis=0, tiled=True)  26.6 us
    dot_general x10, matrix products, layer(): jnp.dot(hidden, weight_out, preferred_element_type=jnp.float32)  24 us
    ppermute x4, starting transfers between devices, from_odd(): lax.ppermute(value, ALL, [(i, i + 1) for i in range(1, peers - 1, 2)])  20.9 us
    all_gather x1, blocking collectives, coarse(): both = lax.all_gather(both, 'core', axis=0, tiled=True)  13.8 us
    all_gather x4, blocking collectives, from_pair(): return lax.all_gather(value, 'core', axis=0)  11.9 us
    all_to_all x1, starting transfers between devices, to_each(): return lax.all_to_all(copies, axis, 0, 0, tiled=True)  6.76 us
  transfers between devices with their start and end apart: 5, of which 0 were waited for; matrix products, arithmetic and copies ran while one was open for 8% of the time, Pallas kernels for 0%

profile of v1, /device:TPU:1, one launch (start us, length us, event | category | flops | bytes accessed | tf_op | source)
XLA Modules:
  0.0 134.4 jit_solution(8898435849523209769)
XLA Ops:
  0.0 0.0 copy-start.2
  0.0 5.1 %collective-permute-start = (f32[192,512]{1,0:T(8,128)}, f32[192,512]{1,0:T(8,128)S(1)}, u32[]{:S(2)}, u32[]{:S(2)}) collective-permute-start(f32[192,512]{1,0:T(8,128)} %bitcast.279), channel_id=1, source_target_pairs={{1,2},{3,4},{5,6},{7,8},{9,10},{11,12},{13,14},{15,16},{17,18},{19... | collective-permute-start | bytes 1179656 | tf_op jit(solution)/shard_map/ppermute | solution.py:12
  5.1 4.8 %all_gather.27 = f32[2,192,512]{2,1,0:T(8,128)S(1)} all-gather(f32[1,192,512]{2,1,0:T(8,128)} %param.7), channel_id=1, replica_groups=mesh['outer'=16,'z'=16,'core'=2] {'core'}, dimensions={0}, use_global_device_ids=true | all-gather | bytes 1179648 | tf_op jit(solution)/shard_map/all_gather | solution.py:16
  9.9 0.8 fusion.361
  10.7 0.0 collective-permute-done
  10.7 0.2 multiply_reduce_fusion.9
  10.9 0.0 copy-done.2
  10.9 2.1 %multiply_reduce_fusion.8 = (f32[192]{0:T(256)S(1)}, f32[192,512]{1,0:T(8,128)S(1)}) fusion(f32[192,512]{1,0:T(8,128)S(1)} %get-tuple-element.12, bf16[2,1024,512]{2,1,0:T(8,128)(2,1)S(1)} %copy-done.2, bf16[2,512,1024]{2,1,0:T(8,128)(2,1)} %param.8, f32[512]{0:T(512)S(1)} %bitcast.301, f32[192]{0:T(256)S(1)} %add_rsqrt_fusion.9), kind=kOutput, calls=%fused_computation.191 | convolution fusion | flops 405110592 | bytes 3280640 | tf_op jit(solution)/shard_map/dot_general | solution.py:31
  13.0 2.3 %fusion.1 = f32[192,512]{1,0:T(8,128)S(1)} fusion(f32[192,512]{1,0:T(8,128)S(1)} %get-tuple-element.31, bf16[2,1024,512]{2,1,0:T(8,128)(2,1)} %param.9, bf16[2,512,1024]{2,1,0:T(8,128)(2,1)} %param.8, f32[512]{0:T(512)S(1)} %bitcast.296, f32[192]{0:T(256)S(1)} %add_rsqrt_fusion.8), kind=kOutput, calls=%fused_computation.11 | convolution fusion | flops 404914176 | bytes 3279872 | tf_op jit(solution)/shard_map/dot_general | solution.py:31
  15.3 3.7 %collective-permute-start.1 = (f32[192,512]{1,0:T(8,128)S(1)}, f32[192,512]{1,0:T(8,128)S(1)}, u32[]{:S(2)}, u32[]{:S(2)}) collective-permute-start(f32[192,512]{1,0:T(8,128)S(1)} %fusion.1), channel_id=1, source_target_pairs={{1,2},{3,4},{5,6},{7,8},{9,10},{11,12},{13,14},{15,16},{17,18},{19... | collective-permute-start | bytes 1179656 | tf_op jit(solution)/shard_map/ppermute | solution.py:12
  19.0 2.4 %all-gather = f32[384,512]{1,0:T(8,128)S(1)} all-gather(f32[192,512]{1,0:T(8,128)S(1)} %fusion.1), channel_id=2, replica_groups=mesh['outer'=16,'z'=16,'core'=2] {'core'}, dimensions={0}, use_global_device_ids=true | all-gather | bytes 1179648 | tf_op jit(solution)/shard_map/all_gather | solution.py:16
  21.4 0.1 multiply_reduce_fusion.7
  21.5 2.4 %multiply_reduce_fusion.6 = (f32[192]{0:T(256)S(1)}, f32[192,512]{1,0:T(8,128)S(1)}) fusion(bf16[2,1024,512]{2,1,0:T(8,128)(2,1)} %param.9, bf16[2,512,1024]{2,1,0:T(8,128)(2,1)} %param.8, f32[384,512]{1,0:T(8,128)S(1)} %all-gather, f32[512]{0:T(512)S(1)} %bitcast.302, f32[192]{0:T(256)S(1)} %add_rsqrt_fusion.7), kind=kOutput, calls=%fused_computation.188 | convolution fusion | flops 405110592 | bytes 3280384 | tf_op jit(solution)/shard_map/dot_general | solution.py:31
  23.9 0.0 copy-start
  23.9 2.3 %fusion.3 = f32[192,512]{1,0:T(8,128)S(1)} fusion(f32[192,512]{1,0:T(8,128)S(1)} %get-tuple-element.33, bf16[2,1024,512]{2,1,0:T(8,128)(2,1)} %param.9, bf16[2,512,1024]{2,1,0:T(8,128)(2,1)} %param.8, f32[192]{0:T(256)S(1)} %add_rsqrt_fusion.6, f32[512]{0:T(512)S(1)} %bitcast.297), kind=kOutput, calls=%fused_computation.13 | convolution fusion | flops 404914176 | bytes 3279872 | tf_op jit(solution)/shard_map/dot_general | solution.py:31
  26.3 3.6 %collective-permute-start.2 = (f32[192,512]{1,0:T(8,128)S(1)}, f32[192,512]{1,0:T(8,128)S(1)}, u32[]{:S(2)}, u32[]{:S(2)}) collective-permute-start(f32[192,512]{1,0:T(8,128)S(1)} %fusion.3), channel_id=1, source_target_pairs={{1,2},{3,4},{5,6},{7,8},{9,10},{11,12},{13,14},{15,16},{17,18},{19... | collective-permute-start | bytes 1179656 | tf_op jit(solution)/shard_map/ppermute | solution.py:12
  29.8 0.0 collective-permute-done.1
  29.9 0.0 copy-done
  29.9 0.1 multiply_reduce_fusion.5
  30.0 2.4 %multiply_reduce_fusion.4 = (f32[192]{0:T(256)S(1)}, f32[192,512]{1,0:T(8,128)S(1)}) fusion(bf16[2,1024,512]{2,1,0:T(8,128)(2,1)} %param.9, bf16[2,512,1024]{2,1,0:T(8,128)(2,1)} %param.8, f32[192]{0:T(256)S(1)} %add_rsqrt_fusion.5, f32[512]{0:T(512)S(1)} %bitcast.303, f32[192,512]{1,0:T(8,128)S(1)} %copy-done, f32[192,512]{1,0:T(8,128)S(1)} %collective-permute-done.1, ...), kind=kOutput, calls=%fused_computation.184 | convolution fusion | flops 405307200 | bytes 4068096 | tf_op jit(solution)/shard_map/dot_general | solution.py:31
  32.5 2.3 %fusion.6 = f32[192,512]{1,0:T(8,128)S(1)} fusion(f32[192,512]{1,0:T(8,128)S(1)} %fusion.3, f32[192,512]{1,0:T(8,128)S(1)} %get-tuple-element.35, bf16[2,1024,512]{2,1,0:T(8,128)(2,1)} %param.9, bf16[2,512,1024]{2,1,0:T(8,128)(2,1)} %param.8, f32[192]{0:T(256)S(1)} %add_rsqrt_fusion.4, f32[512]{0:T(512)S(1)} %bitcast.298, pred[]{:T(512)S(6)} %eq.53), kind=kOutput, calls=%fused_computation.16 | convolution fusion | flops 405012480 | bytes 3673089 | tf_op jit(solution)/shard_map/dot_general | solution.py:31
  34.8 2.4 %all-gather.1 = f32[384,512]{1,0:T(8,128)S(1)} all-gather(f32[192,512]{1,0:T(8,128)S(1)} %fusion.6), channel_id=3, replica_groups=mesh['outer'=16,'z'=16,'core'=2] {'core'}, dimensions={0}, use_global_device_ids=true | all-gather | bytes 1179648 | tf_op jit(solution)/shard_map/all_gather | solution.py:16
  37.1 0.0 collective-permute-done.2
  37.1 0.1 multiply_reduce_fusion.3
  37.3 2.4 %multiply_reduce_fusion.2 = (f32[192]{0:T(256)S(1)}, f32[192,512]{1,0:T(8,128)S(1)}) fusion(f32[192,512]{1,0:T(8,128)S(1)} %get-tuple-element.10, bf16[2,1024,512]{2,1,0:T(8,128)(2,1)} %param.9, bf16[2,512,1024]{2,1,0:T(8,128)(2,1)} %param.8, f32[192]{0:T(256)S(1)} %add_rsqrt_fusion.3, f32[512]{0:T(512)S(1)} %bitcast.304), kind=kOutput, calls=%fused_computation.180 | convolution fusion | flops 405110592 | bytes 3280640 | tf_op jit(solution)/shard_map/dot_general | solution.py:31
  39.7 2.3 %fusion.8 = f32[192,512]{1,0:T(8,128)S(1)} fusion(f32[192,512]{1,0:T(8,128)S(1)} %get-tuple-element.37, bf16[2,1024,512]{2,1,0:T(8,128)(2,1)} %param.9, bf16[2,512,1024]{2,1,0:T(8,128)(2,1)} %param.8, f32[192]{0:T(256)S(1)} %add_rsqrt_fusion.2, f32[512]{0:T(512)S(1)} %bitcast.299), kind=kOutput, calls=%fused_computation.18 | convolution fusion | flops 404914176 | bytes 3279872 | tf_op jit(solution)/shard_map/dot_general | solution.py:31
  42.0 0.0 copy-start.1
  42.0 2.4 %all-gather.2 = f32[384,512]{1,0:T(8,128)S(1)} all-gather(f32[192,512]{1,0:T(8,128)S(1)} %fusion.8), channel_id=4, replica_groups=mesh['outer'=16,'z'=16,'core'=2] {'core'}, dimensions={0}, use_global_device_ids=true | all-gather | bytes 1179648 | tf_op jit(solution)/shard_map/all_gather | solution.py:16
  44.4 0.1 dynamic-slice_subtract_fusion
  44.5 27.5 %all_to_all.10 = f32[16,6,512]{2,1,0:T(8,128)S(1)} all-to-all(f32[16,6,512]{2,1,0:T(8,128)S(1)} %add.278), channel_id=1, replica_groups=mesh['outer'=16,'z'=16,'core'=2] {'z'}, dimensions={0} | all-to-all | bytes 393216 | tf_op jit(solution)/shard_map/all_to_all | solution.py:40
  72.0 0.0 copy-done.1
  72.1 0.7 broadcast_in_dim.4
  72.8 6.8 %all-to-all-start.1 = ((f32[16,7,512]{2,1,0:T(8,128)}), f32[16,7,512]{2,1,0:T(8,128)S(1)}, u32[]{:S(2)}, u32[]{:S(2)}) async-start(f32[16,7,512]{2,1,0:T(8,128)} %broadcast_in_dim.4), calls=%async_computation.1 | async-start | bytes 524288 | tf_op jit(solution)/shard_map/all_to_all | solution.py:22
  79.6 8.5 %collective-permute-start.3 = (f32[192,512]{1,0:T(8,128)S(1)}, f32[192,512]{1,0:T(8,128)S(1)}, u32[]{:S(2)}, u32[]{:S(2)}) collective-permute-start(f32[192,512]{1,0:T(8,128)S(1)} %fusion.8), channel_id=1, source_target_pairs={{1,2},{3,4},{5,6},{7,8},{9,10},{11,12},{13,14},{15,16},{17,18},{19... | collective-permute-start | bytes 1179656 | tf_op jit(solution)/shard_map/ppermute | solution.py:12
  88.1 0.0 all-to-all-done.1
  88.2 0.1 multiply_add_fusion
  88.3 26.6 %all-gather.3 = f32[16,6,1024]{2,1,0:T(8,128)S(1)} all-gather(f32[1,6,1024]{2,1,0:T(8,128)S(1)} %maximum_bitcast_fusion), channel_id=1, replica_groups=mesh['outer'=16,'z'=16,'core'=2] {'z'}, dimensions={0}, use_global_device_ids=true | all-gather | bytes 417792 | tf_op jit(solution)/shard_map/all_gather | solution.py:50
  114.9 0.1 reshape.126
  114.9 13.8 %all_gather.35 = f32[192,1024]{1,0:T(8,128)S(1)} all-gather(f32[96,1024]{1,0:T(8,128)S(1)} %reshape.126), channel_id=1, replica_groups=mesh['outer'=16,'z'=16,'core'=2] {'core'}, dimensions={0}, use_global_device_ids=true | all-gather | bytes 1179648 | tf_op jit(solution)/shard_map/all_gather | solution.py:51
  128.7 0.0 collective-permute-done.3
  128.7 0.2 multiply_reduce_fusion.1
  128.9 2.4 %multiply_reduce_fusion = (f32[192]{0:T(256)S(1)}, f32[192,512]{1,0:T(8,128)S(1)}) fusion(f32[192,512]{1,0:T(8,128)S(1)} %get-tuple-element.6, bf16[2,1024,512]{2,1,0:T(8,128)(2,1)} %param.9, bf16[2,512,1024]{2,1,0:T(8,128)(2,1)} %param.8, f32[192]{0:T(256)S(1)} %add_rsqrt_fusion.1, f32[512]{0:T(512)S(1)} %bitcast.305), kind=kOutput, calls=%fused_computation.175 | convolution fusion | flops 405110592 | bytes 3280640 | tf_op jit(solution)/shard_map/dot_general | solution.py:31
  131.3 3.0 %fusion.11 = f32[1,192,512]{2,1,0:T(8,128)} fusion(f32[192,512]{1,0:T(8,128)S(1)} %get-tuple-element.39, bf16[2,1024,512]{2,1,0:T(8,128)(2,1)} %param.9, bf16[2,512,1024]{2,1,0:T(8,128)(2,1)} %param.8, f32[192]{0:T(256)S(1)} %add_rsqrt_fusion, f32[512]{0:T(512)S(1)} %bitcast.300), kind=kOutput, calls=%fused_computation.21 | convolution fusion | flops 404914176 | bytes 3279872 | tf_op jit(solution)/shard_map/dot_general | solution.py:31
  (17 shorter events, 0.2 us)
Async XLA Ops:
  0.0 10.9 %copy-start.2 = (bf16[2,1024,512]{2,1,0:T(8,128)(2,1)S(1)}, bf16[2,1024,512]{2,1,0:T(8,128)(2,1)}, u32[]{:S(2)}) copy-start(bf16[2,1024,512]{2,1,0:T(8,128)(2,1)} %param.9) | copy-start | bytes 6291460
  0.0 10.7 %collective-permute-start = (f32[192,512]{1,0:T(8,128)}, f32[192,512]{1,0:T(8,128)S(1)}, u32[]{:S(2)}, u32[]{:S(2)}) collective-permute-start(f32[192,512]{1,0:T(8,128)} %bitcast.279), channel_id=1, source_target_pairs={{1,2},{3,4},{5,6},{7,8},{9,10},{11,12},{13,14},{15,16},{17,18},{19... | collective-permute-start | bytes 1179656 | tf_op jit(solution)/shard_map/ppermute | solution.py:12
  15.3 14.6 %collective-permute-start.1 = (f32[192,512]{1,0:T(8,128)S(1)}, f32[192,512]{1,0:T(8,128)S(1)}, u32[]{:S(2)}, u32[]{:S(2)}) collective-permute-start(f32[192,512]{1,0:T(8,128)S(1)} %fusion.1), channel_id=1, source_target_pairs={{1,2},{3,4},{5,6},{7,8},{9,10},{11,12},{13,14},{15,16},{17,18},{19... | collective-permute-start | bytes 1179656 | tf_op jit(solution)/shard_map/ppermute | solution.py:12
  23.9 6.0 %copy-start = (f32[192,512]{1,0:T(8,128)S(1)}, f32[192,512]{1,0:T(8,128)}, u32[]{:S(2)}) copy-start(f32[192,512]{1,0:T(8,128)} %param.6) | copy-start | bytes 1179652
  26.3 10.9 %collective-permute-start.2 = (f32[192,512]{1,0:T(8,128)S(1)}, f32[192,512]{1,0:T(8,128)S(1)}, u32[]{:S(2)}, u32[]{:S(2)}) collective-permute-start(f32[192,512]{1,0:T(8,128)S(1)} %fusion.3), channel_id=1, source_target_pairs={{1,2},{3,4},{5,6},{7,8},{9,10},{11,12},{13,14},{15,16},{17,18},{19... | collective-permute-start | bytes 1179656 | tf_op jit(solution)/shard_map/ppermute | solution.py:12
  42.0 30.0 %copy-start.1 = (f32[1,512]{1,0:T(1,128)S(1)}, f32[1,512]{1,0:T(1,128)}, u32[]{:S(2)}) copy-start(f32[1,512]{1,0:T(1,128)} %param.11) | copy-start | bytes 6148
  72.8 15.3 %all-to-all-start.1 = ((f32[16,7,512]{2,1,0:T(8,128)}), f32[16,7,512]{2,1,0:T(8,128)S(1)}, u32[]{:S(2)}, u32[]{:S(2)}) async-start(f32[16,7,512]{2,1,0:T(8,128)} %broadcast_in_dim.4), calls=%async_computation.1 | async-start | bytes 524288 | tf_op jit(solution)/shard_map/all_to_all | solution.py:22
  79.6 49.1 %collective-permute-start.3 = (f32[192,512]{1,0:T(8,128)S(1)}, f32[192,512]{1,0:T(8,128)S(1)}, u32[]{:S(2)}, u32[]{:S(2)}) collective-permute-start(f32[192,512]{1,0:T(8,128)S(1)} %fusion.8), channel_id=1, source_target_pairs={{1,2},{3,4},{5,6},{7,8},{9,10},{11,12},{13,14},{15,16},{17,18},{19... | collective-permute-start | bytes 1179656 | tf_op jit(solution)/shard_map/ppermute | solution.py:12

commit v2 on v1

v2 whole, which is shorter than its diff:
```python
import functools

import jax
import jax.numpy as jnp
from jax import lax
from jax.experimental import pallas as pl
from jax.experimental.pallas import tpu as pltpu
from jax.sharding import Mesh, PartitionSpec as P

step_size = 0.5
ALL = ("outer", "z", "core")
LANES = 128


def from_odd(value):
    peers = lax.axis_size(ALL)
    return lax.ppermute(value, ALL, [(i, i + 1) for i in range(1, peers - 1, 2)])


def from_pair(value):
    return lax.all_gather(value, "core", axis=0)


def gelu(value):
    root = 0.7978845608028654
    inner = value * (root + (root * 0.044715) * (value * value))
    half = 0.5 * value
    return half + half * jnp.tanh(inner)


def layers(state, weight_in, weight_out, norm_gain):
    for level in range(weight_in.shape[0]):
        meansq = jnp.mean(state * state, axis=-1, keepdims=True)
        normed = (state * lax.rsqrt(meansq + 1e-06) * norm_gain[level : level + 1, :]).astype(
            jnp.bfloat16
        )
        hidden = jnp.dot(normed, weight_in[level], preferred_element_type=jnp.float32)
        hidden = gelu(hidden).astype(jnp.bfloat16)
        state = state + step_size * jnp.dot(
            hidden, weight_out[level], preferred_element_type=jnp.float32
        )
    return state


def call(body, out_shape, args, name, flops=0):
    return pl.pallas_call(
        body,
        out_shape=jax.ShapeDtypeStruct(out_shape, jnp.float32),
        in_specs=[pl.BlockSpec(memory_space=pltpu.VMEM)] * len(args),
        out_specs=pl.BlockSpec(memory_space=pltpu.VMEM),
        compiler_params=pltpu.CompilerParams(vmem_limit_bytes=16 << 20),
        cost_estimate=pl.CostEstimate(
            flops=flops, bytes_accessed=sum(a.size * 4 for a in args), transcendentals=0
        ),
        name=name,
    )(*args)


def load_kernel(*refs):
    count = len(refs) // 3
    copies = [
        pltpu.make_async_copy(refs[at], refs[count + at], refs[2 * count + at])
        for at in range(count)
    ]
    for copy in copies:
        copy.start()
    for copy in copies:
        copy.wait()


def loaded(args):
    return pl.pallas_call(
        load_kernel,
        out_shape=[jax.ShapeDtypeStruct(a.shape, a.dtype) for a in args],
        in_specs=[pl.BlockSpec(memory_space=pl.ANY)] * len(args),
        out_specs=[pl.BlockSpec(memory_space=pltpu.VMEM)] * len(args),
        scratch_shapes=[pltpu.SemaphoreType.DMA(())] * len(args),
        compiler_params=pltpu.CompilerParams(vmem_limit_bytes=16 << 20),
        cost_estimate=pl.CostEstimate(
            flops=0,
            bytes_accessed=sum(a.size * a.dtype.itemsize for a in args),
            transcendentals=0,
        ),
        name="load",
    )(*args)


def is_odd():
    return lax.axis_index("core") == 1


def is_first():
    return lax.axis_index(ALL) == 0


def choose_kernel(pair, hop, start, weight_in, weight_out, norm_gain, out):
    even = jnp.where(is_first(), start[...], hop[...])
    state = jnp.where(is_odd(), pair[0], even)
    out[...] = layers(state, weight_in, weight_out, norm_gain)


def odd_kernel(pair, weight_in, weight_out, norm_gain, out):
    out[...] = layers(pair[0], weight_in, weight_out, norm_gain)


def even_kernel(ready, hop, start, weight_in, weight_out, norm_gain, out):
    even = jnp.where(is_first(), start[...], hop[...])
    state = layers(even, weight_in, weight_out, norm_gain)
    out[...] = jnp.where(is_odd(), ready[...], state)


def part_kernel(third, second, out):
    places, rows, lanes = out.shape
    tokens, width = third.shape[1:]
    half = width // 2
    across = half // lanes

    def piece(ref, which, at, right):
        down = pl.ds(at // across * rows, rows)
        side = pl.ds(right * half + at % across * lanes, lanes)
        return ref[which, down, side]

    for at in range(places):
        sums = []
        for right in range(2):
            sums.append(
                (piece(third, 0, at, right) - piece(second, 0, at, right))
                + (piece(third, 1, at, right) - piece(second, 1, at, right))
            )
        out[at] = jnp.where(is_odd(), sums[1], sums[0])


def gain_piece(gain, lanes):
    pieces = gain.shape[1] // lanes
    across = pieces // 2
    place = lax.axis_index("core") * across + lax.rem(lax.axis_index("z"), across)
    value = gain[:, 0:lanes]
    for at in range(1, pieces):
        value = jnp.where(place == at, gain[:, at * lanes : (at + 1) * lanes], value)
    return value


def own_kernel(count, parts, gain, out):
    places, rows, lanes = parts.shape
    own = parts[0]
    for at in range(1, places):
        own = own + parts[at]
    own = own / count
    spare = out.shape[1] - rows
    tail = jnp.broadcast_to(gain_piece(gain, lanes), (spare, lanes))
    for group in range(out.shape[0]):
        out[group, 0:rows, :] = own
        out[group, rows:, :] = tail


def scan_kernel(heard, out):
    groups = heard.shape[0]
    rows, lanes = out.shape[1:]
    group = lax.axis_index("outer")
    running = jnp.zeros((rows, lanes), jnp.float32)
    earlier, current = running, running
    for index in range(groups):
        earlier = jnp.where(index == group, running, earlier)
        running = heard[index, rows : rows + 1, :] * running + heard[index, 0:rows, :]
        current = jnp.where(index == group, running, current)
    out[0] = earlier
    out[1] = current


def last_kernel(both, pair, hop, start, weight_in, weight_out, norm_gain, out):
    cores, places, kinds, rows, lanes = both.shape
    count = places * cores
    place = lax.axis_index("z") * cores + lax.axis_index("core")
    weight = place.astype(jnp.float32) / count
    across = hop.shape[1] // lanes // cores
    columns = []
    for core in range(cores):
        for side in range(across):
            pieces = []
            for down in range(places // across):
                at = down * across + side
                pieces.append(weight * both[core, at, 1] + (1.0 - weight) * both[core, at, 0])
            columns.append(jnp.concatenate(pieces, axis=0))
    moved = jnp.where(is_odd(), pair[0], hop[...])
    state = moved + jnp.concatenate(columns, axis=1)
    state = jnp.where(is_first(), start[...], state)
    out[0] = layers(state, weight_in, weight_out, norm_gain)


def per_device(start_state, guess, weight_in, weight_out, norm_gain, coarse_gain):
    tokens, width = start_state.shape
    places, groups = lax.axis_size("z"), lax.axis_size("outer")
    cores = lax.axis_size("core")
    *params, start_state, coarse_gain = loaded(
        (weight_in, weight_out, norm_gain, start_state, coarse_gain)
    )
    params = tuple(params)
    flops = 4 * tokens * weight_in.size

    def block(body, args, name):
        return call(body, (tokens, width), args + params, name, flops)

    guess_z = from_odd(guess[0])
    guess_pair = from_pair(guess[0])
    first = block(choose_kernel, (guess_pair, guess_z, start_state), "first")
    first_z = from_odd(first)
    first_pair = from_pair(first)
    second_odd = block(odd_kernel, (first_pair,), "second_odd")
    second_z = from_odd(second_odd)
    second = block(even_kernel, (second_odd, first_z, start_state), "second")
    second_pair = from_pair(second)
    third = block(choose_kernel, (second_pair, second_z, start_state), "third")
    third_pair = from_pair(third)
    third_z = from_odd(third)

    rows = tokens * width // LANES // places // cores
    part = call(part_kernel, (places, rows, LANES), (third_pair, second_pair), "part")
    parts = lax.all_to_all(part, "z", 0, 0, tiled=True)
    own = call(
        functools.partial(own_kernel, places * cores),
        (groups, rows + 8, LANES),
        (parts, coarse_gain),
        "own",
    )
    heard = lax.all_to_all(own, "outer", 0, 0, tiled=True)
    both = call(scan_kernel, (2, rows, LANES), (heard,), "scan")
    both = lax.all_gather(lax.all_gather(both, "z", axis=0), "core", axis=0)
    return call(
        last_kernel,
        (1, tokens, width),
        (both, third_pair, third_z, start_state) + params,
        "last",
        flops,
    )


def solution(mesh):
    groups, inner = mesh.devices.shape
    fine = Mesh(mesh.devices.reshape(groups, inner // 2, 2), ALL)
    split = P(ALL, None, None)
    return jax.shard_map(
        per_device,
        mesh=fine,
        in_specs=(P(), split, split, split, P(ALL, None), P("outer", None)),
        out_specs=split,
        check_vma=False,
    )
```

time: 135 us -> 122 us (0.904)
  matrix products: 24 us -> 0 us
  Pallas kernels: 0 us -> 10.5 us
  local copies, waits for them, and re-layouts: 1.6 us -> 7.61 us
  starting transfers between devices: 27.6 us -> 25.1 us
  blocking collectives: 79.7 us -> 77.7 us
    dot_general x10 -> x0, matrix products: 24 us -> none  [layer(): jnp.dot(hidden, weight_out, preferred_element_type=jnp.float32)]
    pallas_call x0 -> x9, Pallas kernels: none -> 10.5 us  [the longest x8 9.98 us: call(): pl.pallas_call(body, out_shape=jax.ShapeDtypeStruct(out_shape, jnp.float3...]
    unnamed x7 -> x18, local copies, waits for them, and re-layouts: 0.07 us -> 7.61 us
    ppermute x4, starting transfers between devices: 20.9 us -> 18.3 us  [from_odd(): lax.ppermute(value, ALL, [(i, i + 1) for i in range(1, peers - 1, 2)])]
    all_gather x2, blocking collectives: 40.4 us -> 38.4 us  [per_device(): both = lax.all_gather(lax.all_gather(both, 'z', axis=0), 'core', axis=0)]
  transfers between devices with their start and end apart: 5 -> 5, of which waited for: 0 -> 1; matrix products, arithmetic and copies ran while one was open for 8% -> 0% of each run, Pallas kernels for 0% -> 3%
where the time goes in v2:
time: 122 us
  blocking collectives  77.7 us (64%)
  starting transfers between devices  25.1 us (21%)
  Pallas kernels  10.5 us (9%)
  local copies, waits for them, and re-layouts  7.61 us (6%)
    all_gather x2, blocking collectives, per_device(): both = lax.all_gather(lax.all_gather(both, 'z', axis=0), 'core', axis=0)  38.4 us
    all_to_all x1, blocking collectives, per_device(): parts = lax.all_to_all(part, 'z', 0, 0, tiled=True)  27.6 us
    ppermute x4, starting transfers between devices, from_odd(): lax.ppermute(value, ALL, [(i, i + 1) for i in range(1, peers - 1, 2)])  18.3 us
    all_gather x4, blocking collectives, from_pair(): return lax.all_gather(value, 'core', axis=0)  11.7 us
    pallas_call x8, Pallas kernels, call(): pl.pallas_call(body, out_shape=jax.ShapeDtypeStruct(out_shape, jnp.float3...  9.98 us
    unnamed x18, local copies, waits for them, and re-layouts  7.61 us
    all_to_all x1, starting transfers between devices, per_device(): heard = lax.all_to_all(own, 'outer', 0, 0, tiled=True)  6.77 us
  transfers between devices with their start and end apart: 5, of which 1 were waited for; matrix products, arithmetic and copies ran while one was open for 0% of the time, Pallas kernels for 3%

profile of v2, /device:TPU:1, one launch (start us, length us, event | category | flops | bytes accessed | tf_op | source)
XLA Modules:
  0.0 121.8 jit_solution(2975182876846745234)
XLA Ops:
  0.0 4.9 %collective-permute-start = (f32[192,512]{1,0:T(8,128)}, f32[192,512]{1,0:T(8,128)S(1)}, u32[]{:S(2)}, u32[]{:S(2)}) collective-permute-start(f32[192,512]{1,0:T(8,128)} %bitcast.13), channel_id=1, source_target_pairs={{1,2},{3,4},{5,6},{7,8},{9,10},{11,12},{13,14},{15,16},{17,18},{19... | collective-permute-start | bytes 1179656 | tf_op jit(solution)/shard_map/ppermute | solution.py:17
  5.0 0.0 copy-start.2
  5.0 1.6 %copy-done.2 = bf16[2,512,1024]{2,1,0:T(8,128)(2,1)S(1)} copy-done((bf16[2,512,1024]{2,1,0:T(8,128)(2,1)S(1)}, bf16[2,512,1024]{2,1,0:T(8,128)(2,1)}, u32[]{:S(2)}) %copy-start.2) | copy-done | bytes 2097176
  6.5 0.0 copy-start.3
  6.5 1.6 %copy-done.3 = bf16[2,1024,512]{2,1,0:T(8,128)(2,1)S(1)} copy-done((bf16[2,1024,512]{2,1,0:T(8,128)(2,1)S(1)}, bf16[2,1024,512]{2,1,0:T(8,128)(2,1)}, u32[]{:S(2)}) %copy-start.3) | copy-done | bytes 2097176
  8.1 0.0 copy-start.5
  8.1 1.0 copy-done.5
  9.1 0.0 copy-start.6
  9.1 0.7 copy-done.6
  9.8 0.0 copy-start.7
  9.8 0.7 copy-done.7
  10.5 0.0 copy-start.8
  10.5 0.5 load.1
  11.0 0.5 copy-done.8
  11.5 0.0 copy-start
  11.5 4.6 %all_gather.33.pair = f32[2,192,512]{2,1,0:T(8,128)S(1)} all-gather(f32[1,192,512]{2,1,0:T(8,128)S(1)} %copy-done.8), channel_id=1, replica_groups=mesh['outer'=16,'z'=16,'core'=2] {'core'}, dimensions={0}, use_global_device_ids=true | all-gather | bytes 1179648 | tf_op jit(solution)/shard_map/all_gather | solution.py:21
  16.1 0.0 collective-permute-done.hop
  16.1 1.5 %first.1 = f32[192,512]{1,0:T(8,128)S(1)} custom-call(f32[2,192,512]{2,1,0:T(8,128)S(1)} %all_gather.33.pair, f32[192,512]{1,0:T(8,128)S(1)} %collective-permute-done.hop, f32[192,512]{1,0:T(8,128)S(1)} %get-tuple-element.10.start, bf16[2,512,1024]{2,1,0:T(8,128)(2,1)S(1)} %get-tuple-element.11.weight_in, ...), custom_call_target="tpu_custom_call" | custom-call | flops 805306368 | bytes 9965568 | tf_op jit(solution)/shard_map/first/pallas_call | solution.py:46
  17.6 1.4 %collective-permute-start.1 = (f32[192,512]{1,0:T(8,128)S(1)}, f32[192,512]{1,0:T(8,128)S(1)}, u32[]{:S(2)}, u32[]{:S(2)}) collective-permute-start(f32[192,512]{1,0:T(8,128)S(1)} %first.1), channel_id=1, source_target_pairs={{1,2},{3,4},{5,6},{7,8},{9,10},{11,12},{13,14},{15,16},{17,18},{19... | collective-permute-start | bytes 1179656 | tf_op jit(solution)/shard_map/ppermute | solution.py:17
  18.9 2.4 %all-gather = f32[384,512]{1,0:T(8,128)S(1)} all-gather(f32[192,512]{1,0:T(8,128)S(1)} %first.1), channel_id=2, replica_groups=mesh['outer'=16,'z'=16,'core'=2] {'core'}, dimensions={0}, use_global_device_ids=true | all-gather | bytes 1179648 | tf_op jit(solution)/shard_map/all_gather | solution.py:21
  21.3 1.4 %second_odd.1.ready = f32[192,512]{1,0:T(8,128)S(1)} custom-call(f32[2,192,512]{2,1,0:T(8,128)S(1)} %bitcast.11, bf16[2,512,1024]{2,1,0:T(8,128)(2,1)S(1)} %get-tuple-element.11.weight_in, bf16[2,1024,512]{2,1,0:T(8,128)(2,1)S(1)} %get-tuple-element.12.weight_out, f32[2,512]{1,0:T(2,128)S(1)} %get-tuple-element.13.norm_gain), custom_call_target="tpu_custom_call" | custom-call | flops 805306368 | bytes 9179136 | tf_op jit(solution)/shard_map/second_odd/pallas_call | solution.py:46
  22.8 3.6 %collective-permute-start.2 = (f32[192,512]{1,0:T(8,128)S(1)}, f32[192,512]{1,0:T(8,128)S(1)}, u32[]{:S(2)}, u32[]{:S(2)}) collective-permute-start(f32[192,512]{1,0:T(8,128)S(1)} %second_odd.1.ready), channel_id=1, source_target_pairs={{1,2},{3,4},{5,6},{7,8},{9,10},{11,12},{13,14},{15,16},{17,18},{19... | collective-permute-start | bytes 1179656 | tf_op jit(solution)/shard_map/ppermute | solution.py:17
  26.3 0.0 collective-permute-done.1.hop
  26.4 1.5 %second.1 = f32[192,512]{1,0:T(8,128)S(1)} custom-call(f32[192,512]{1,0:T(8,128)S(1)} %second_odd.1.ready, f32[192,512]{1,0:T(8,128)S(1)} %collective-permute-done.1.hop, f32[192,512]{1,0:T(8,128)S(1)} %get-tuple-element.10.start, bf16[2,512,1024]{2,1,0:T(8,128)(2,1)S(1)} %get-tuple-element.11.weight_in, ...), custom_call_target="tpu_custom_call" | custom-call | flops 805306368 | bytes 9572352 | tf_op jit(solution)/shard_map/second/pallas_call | solution.py:46
  27.8 2.4 %all-gather.1 = f32[384,512]{1,0:T(8,128)S(1)} all-gather(f32[192,512]{1,0:T(8,128)S(1)} %second.1), channel_id=3, replica_groups=mesh['outer'=16,'z'=16,'core'=2] {'core'}, dimensions={0}, use_global_device_ids=true | all-gather | bytes 1179648 | tf_op jit(solution)/shard_map/all_gather | solution.py:21
  30.2 0.8 collective-permute-done.2.hop
  31.0 0.0 copy-done
  31.0 1.5 %third.1 = f32[192,512]{1,0:T(8,128)S(1)} custom-call(f32[2,192,512]{2,1,0:T(8,128)S(1)} %bitcast.8, f32[192,512]{1,0:T(8,128)S(1)} %collective-permute-done.2.hop, f32[192,512]{1,0:T(8,128)S(1)} %get-tuple-element.10.start, bf16[2,512,1024]{2,1,0:T(8,128)(2,1)S(1)} %get-tuple-element.11.weight_in, bf16[2,1024,512]{2,1,0:T(8,128)(2,1)S(1)} %get-tuple-element.12.weight_out, ...), custom_call_target="tpu_custom_call" | custom-call | flops 805306368 | bytes 9965568 | tf_op jit(solution)/shard_map/third/pallas_call | solution.py:46
  32.5 0.0 copy-start.4
  32.5 2.4 %all-gather.2 = f32[384,512]{1,0:T(8,128)S(1)} all-gather(f32[192,512]{1,0:T(8,128)S(1)} %third.1), channel_id=4, replica_groups=mesh['outer'=16,'z'=16,'core'=2] {'core'}, dimensions={0}, use_global_device_ids=true | all-gather | bytes 1179648 | tf_op jit(solution)/shard_map/all_gather | solution.py:21
  34.9 0.1 part.1
  35.0 0.0 copy-done.4
  35.0 27.6 %all_to_all.10.parts = f32[16,24,128]{2,1,0:T(8,128)S(1)} all-to-all(f32[16,24,128]{2,1,0:T(8,128)S(1)} %part.1), channel_id=1, replica_groups=mesh['outer'=16,'z'=16,'core'=2] {'z'}, dimensions={0} | all-to-all | bytes 393216 | tf_op jit(solution)/shard_map/all_to_all | solution.py:218
  62.6 0.7 own.1
  63.3 6.8 %all-to-all-start.1 = ((f32[16,32,128]{2,1,0:T(8,128)}), f32[16,32,128]{2,1,0:T(8,128)S(1)}, u32[]{:S(2)}, u32[]{:S(2)}) async-start(f32[16,32,128]{2,1,0:T(8,128)} %own.1), calls=%async_computation.1 | async-start | bytes 524288 | tf_op jit(solution)/shard_map/all_to_all | solution.py:225
  70.1 8.4 %collective-permute-start.3 = (f32[192,512]{1,0:T(8,128)}, f32[192,512]{1,0:T(8,128)}, u32[]{:S(2)}, u32[]{:S(2)}) collective-permute-start(f32[192,512]{1,0:T(8,128)} %copy-done.4), channel_id=1, source_target_pairs={{1,2},{3,4},{5,6},{7,8},{9,10},{11,12},{13,14},{15,16},{17,18},{19... | collective-permute-start | bytes 1179656 | tf_op jit(solution)/shard_map/ppermute | solution.py:17
  78.6 0.0 all-to-all-done.1.heard
  78.6 24.9 %all-gather.3 = f32[32,24,128]{2,1,0:T(8,128)S(1)} all-gather(f32[2,24,128]{2,1,0:T(8,128)S(1)} %scan.1), channel_id=5, replica_groups=mesh['outer'=16,'z'=16,'core'=2] {'z'}, dimensions={0}, use_global_device_ids=true | all-gather | bytes 417792 | tf_op jit(solution)/shard_map/all_gather | solution.py:227
  103.5 13.5 %all-gather.4 = f32[32,2,24,128]{3,2,1,0:T(8,128)S(1)} all-gather(f32[16,2,24,128]{3,2,1,0:T(8,128)S(1)} %bitcast.12), channel_id=6, replica_groups=mesh['outer'=16,'z'=16,'core'=2] {'core'}, dimensions={0}, use_global_device_ids=true | all-gather | bytes 1179648 | tf_op jit(solution)/shard_map/all_gather | solution.py:227
  117.0 0.0 collective-permute-done.3.hop
  117.0 0.0 copy-start.1
  117.0 1.6 %copy-done.1 = bf16[2,1024,512]{2,1,0:T(8,128)(2,1)S(1)} copy-done((bf16[2,1024,512]{2,1,0:T(8,128)(2,1)S(1)}, bf16[2,1024,512]{2,1,0:T(8,128)(2,1)}, u32[]{:S(2)}) %copy-start.1) | copy-done | bytes 2097176
  118.6 3.3 %last.1 = f32[1,192,512]{2,1,0:T(8,128)} custom-call(f32[2,16,2,24,128]{4,3,2,1,0:T(8,128)S(1)} %bitcast.10, f32[2,192,512]{2,1,0:T(8,128)S(1)} %bitcast.7, f32[192,512]{1,0:T(8,128)} %collective-permute-done.3.hop, f32[192,512]{1,0:T(8,128)S(1)} %get-tuple-element.10.start, bf16[2,512,1024]{2,1,0:T(8,128)(2,1)S(1)} %get-tuple-element.11.weight_in, ...), custom_call_target="tpu_custom_call" | custom-call | flops 805306368 | bytes 10752000 | tf_op jit(solution)/shard_map/last/pallas_call | solution.py:46
  (1 shorter events, 0.0 us)
Async XLA Ops:
  0.0 16.1 %collective-permute-start = (f32[192,512]{1,0:T(8,128)}, f32[192,512]{1,0:T(8,128)S(1)}, u32[]{:S(2)}, u32[]{:S(2)}) collective-permute-start(f32[192,512]{1,0:T(8,128)} %bitcast.13), channel_id=1, source_target_pairs={{1,2},{3,4},{5,6},{7,8},{9,10},{11,12},{13,14},{15,16},{17,18},{19... | collective-permute-start | bytes 1179656 | tf_op jit(solution)/shard_map/ppermute | solution.py:17
  5.0 1.6 %copy-start.2 = (bf16[2,512,1024]{2,1,0:T(8,128)(2,1)S(1)}, bf16[2,512,1024]{2,1,0:T(8,128)(2,1)}, u32[]{:S(2)}) copy-start(bf16[2,512,1024]{2,1,0:T(8,128)(2,1)} %refs_0_.1) | copy-start | bytes 6291460
  6.5 1.6 %copy-start.3 = (bf16[2,1024,512]{2,1,0:T(8,128)(2,1)S(1)}, bf16[2,1024,512]{2,1,0:T(8,128)(2,1)}, u32[]{:S(2)}) copy-start(bf16[2,1024,512]{2,1,0:T(8,128)(2,1)} %refs_1_.1) | copy-start | bytes 6291460
  8.1 1.0 copy-start.5
  9.1 0.7 copy-start.6
  9.8 0.7 copy-start.7
  10.5 1.0 copy-start.8
  11.5 19.5 %copy-start = (bf16[2,1024,512]{2,1,0:T(8,128)(2,1)}, bf16[2,1024,512]{2,1,0:T(8,128)(2,1)S(1)}, u32[]{:S(2)}) copy-start(bf16[2,1024,512]{2,1,0:T(8,128)(2,1)S(1)} %get-tuple-element.12.weight_out) | copy-start | bytes 6291460
  17.6 8.8 %collective-permute-start.1 = (f32[192,512]{1,0:T(8,128)S(1)}, f32[192,512]{1,0:T(8,128)S(1)}, u32[]{:S(2)}, u32[]{:S(2)}) collective-permute-start(f32[192,512]{1,0:T(8,128)S(1)} %first.1), channel_id=1, source_target_pairs={{1,2},{3,4},{5,6},{7,8},{9,10},{11,12},{13,14},{15,16},{17,18},{19... | collective-permute-start | bytes 1179656 | tf_op jit(solution)/shard_map/ppermute | solution.py:17
  22.8 8.3 %collective-permute-start.2 = (f32[192,512]{1,0:T(8,128)S(1)}, f32[192,512]{1,0:T(8,128)S(1)}, u32[]{:S(2)}, u32[]{:S(2)}) collective-permute-start(f32[192,512]{1,0:T(8,128)S(1)} %second_odd.1.ready), channel_id=1, source_target_pairs={{1,2},{3,4},{5,6},{7,8},{9,10},{11,12},{13,14},{15,16},{17,18},{19... | collective-permute-start | bytes 1179656 | tf_op jit(solution)/shard_map/ppermute | solution.py:17
  32.5 2.5 %copy-start.4 = (f32[192,512]{1,0:T(8,128)}, f32[192,512]{1,0:T(8,128)S(1)}, u32[]{:S(2)}) copy-start(f32[192,512]{1,0:T(8,128)S(1)} %third.1) | copy-start | bytes 1179652
  63.3 15.2 %all-to-all-start.1 = ((f32[16,32,128]{2,1,0:T(8,128)}), f32[16,32,128]{2,1,0:T(8,128)S(1)}, u32[]{:S(2)}, u32[]{:S(2)}) async-start(f32[16,32,128]{2,1,0:T(8,128)} %own.1), calls=%async_computation.1 | async-start | bytes 524288 | tf_op jit(solution)/shard_map/all_to_all | solution.py:225
  70.1 46.9 %collective-permute-start.3 = (f32[192,512]{1,0:T(8,128)}, f32[192,512]{1,0:T(8,128)}, u32[]{:S(2)}, u32[]{:S(2)}) collective-permute-start(f32[192,512]{1,0:T(8,128)} %copy-done.4), channel_id=1, source_target_pairs={{1,2},{3,4},{5,6},{7,8},{9,10},{11,12},{13,14},{15,16},{17,18},{19... | collective-permute-start | bytes 1179656 | tf_op jit(solution)/shard_map/ppermute | solution.py:17
  117.0 1.6 %copy-start.1 = (bf16[2,1024,512]{2,1,0:T(8,128)(2,1)S(1)}, bf16[2,1024,512]{2,1,0:T(8,128)(2,1)}, u32[]{:S(2)}) copy-start(bf16[2,1024,512]{2,1,0:T(8,128)(2,1)} %copy-done) | copy-start | bytes 6291460

commit v3 on v2

--- a/solution.py
+++ b/solution.py
@@ -42,18 +42,24 @@
     return state
 
 
-def call(body, out_shape, args, name, flops=0):
+def call(body, out_shape, args, name, flops=0, after=()):
+    count = len(args)
+
+    def with_after(*refs):
+        body(*refs[:count], refs[-1])
+
     return pl.pallas_call(
-        body,
+        with_after,
         out_shape=jax.ShapeDtypeStruct(out_shape, jnp.float32),
-        in_specs=[pl.BlockSpec(memory_space=pltpu.VMEM)] * len(args),
+        in_specs=[pl.BlockSpec(memory_space=pltpu.VMEM)] * count
+        + [pl.BlockSpec(memory_space=pl.ANY)] * len(after),
         out_specs=pl.BlockSpec(memory_space=pltpu.VMEM),
         compiler_params=pltpu.CompilerParams(vmem_limit_bytes=16 << 20),
         cost_estimate=pl.CostEstimate(
             flops=flops, bytes_accessed=sum(a.size * 4 for a in args), transcendentals=0
         ),
         name=name,
-    )(*args)
+    )(*args, *after)
 
 
 def load_kernel(*refs):
@@ -71,7 +77,7 @@
 def loaded(args):
     return pl.pallas_call(
         load_kernel,
-        out_shape=[jax.ShapeDtypeStruct(a.shape, a.dtype) for a in args],
+        out_shape=[pltpu.VMEM(a.shape, a.dtype) for a in args],
         in_specs=[pl.BlockSpec(memory_space=pl.ANY)] * len(args),
         out_specs=[pl.BlockSpec(memory_space=pltpu.VMEM)] * len(args),
         scratch_shapes=[pltpu.SemaphoreType.DMA(())] * len(args),
@@ -82,7 +88,7 @@
             transcendentals=0,
         ),
         name="load",
-    )(*args)
+    )(*[pltpu.with_memory_space_constraint(a, pltpu.HBM) for a in args])
 
 
 def is_odd():
@@ -155,7 +161,7 @@
 
 def scan_kernel(heard, out):
     groups = heard.shape[0]
-    rows, lanes = out.shape[1:]
+    rows, lanes = out.shape[1] // 2, out.shape[2]
     group = lax.axis_index("outer")
     running = jnp.zeros((rows, lanes), jnp.float32)
     earlier, current = running, running
@@ -163,12 +169,14 @@
         earlier = jnp.where(index == group, running, earlier)
         running = heard[index, rows : rows + 1, :] * running + heard[index, 0:rows, :]
         current = jnp.where(index == group, running, current)
-    out[0] = earlier
-    out[1] = current
+    for place in range(out.shape[0]):
+        out[place, 0:rows, :] = earlier
+        out[place, rows:, :] = current
 
 
 def last_kernel(both, pair, hop, start, weight_in, weight_out, norm_gain, out):
-    cores, places, kinds, rows, lanes = both.shape
+    cores, places = both.shape[:2]
+    rows, lanes = both.shape[2] // 2, both.shape[3]
     count = places * cores
     place = lax.axis_index("z") * cores + lax.axis_index("core")
     weight = place.astype(jnp.float32) / count
@@ -179,7 +187,8 @@
             pieces = []
             for down in range(places // across):
                 at = down * across + side
-                pieces.append(weight * both[core, at, 1] + (1.0 - weight) * both[core, at, 0])
+                earlier, current = both[core, at, 0:rows, :], both[core, at, rows:, :]
+                pieces.append(weight * current + (1.0 - weight) * earlier)
             columns.append(jnp.concatenate(pieces, axis=0))
     moved = jnp.where(is_odd(), pair[0], hop[...])
     state = moved + jnp.concatenate(columns, axis=1)
@@ -211,11 +220,12 @@
     second_pair = from_pair(second)
     third = block(choose_kernel, (second_pair, second_z, start_state), "third")
     third_pair = from_pair(third)
-    third_z = from_odd(third)
 
     rows = tokens * width // LANES // places // cores
     part = call(part_kernel, (places, rows, LANES), (third_pair, second_pair), "part")
     parts = lax.all_to_all(part, "z", 0, 0, tiled=True)
+    third, parts = lax.optimization_barrier((third, parts))
+    third_z = from_odd(third)
     own = call(
         functools.partial(own_kernel, places * cores),
         (groups, rows + 8, LANES),
@@ -223,8 +233,8 @@
         "own",
     )
     heard = lax.all_to_all(own, "outer", 0, 0, tiled=True)
-    both = call(scan_kernel, (2, rows, LANES), (heard,), "scan")
-    both = lax.all_gather(lax.all_gather(both, "z", axis=0), "core", axis=0)
+    both = call(scan_kernel, (places, 2 * rows, LANES), (heard,), "scan", after=(third_z,))
+    both = from_pair(lax.all_to_all(both, "z", 0, 0, tiled=True))
     return call(
         last_kernel,
         (1, tokens, width),

time: 122 us -> 117 us (0.959)
  blocking collectives: 77.7 us -> 86.4 us
  local copies, waits for them, and re-layouts: 7.61 us -> 0.01 us
  starting transfers between devices: 25.1 us -> 18.4 us
    all_gather x2 -> x0, blocking collectives: 38.4 us -> none  [per_device(): both = lax.all_gather(lax.all_gather(both, 'z', axis=0), 'core', axis=0)]
    all_to_all x0 -> x2, blocking collectives: none -> 36.4 us  [the longest x1 22.3 us: per_device(): both = from_pair(lax.all_to_all(both, 'z', 0, 0, tiled=True))]
    all_gather x4 -> x5, blocking collectives: 11.7 us -> 21.5 us  [from_pair(): return lax.all_gather(value, 'core', axis=0)]
    unnamed x18 -> x2, local copies, waits for them, and re-layouts: 7.61 us -> 0.01 us
    all_to_all x1 -> x0, starting transfers between devices: 6.77 us -> none  [per_device(): heard = lax.all_to_all(own, 'outer', 0, 0, tiled=True)]
  transfers between devices with their start and end apart: 5 -> 4, of which waited for: 1 -> 1; matrix products, arithmetic and copies ran while one was open for 0% -> 0% of each run, Pallas kernels for 3% -> 5%
where the time goes in v3:
time: 117 us
  blocking collectives  86.4 us (74%)
  starting transfers between devices  18.4 us (16%)
  Pallas kernels  10.8 us (9%)
    all_to_all x1, blocking collectives, per_device(): parts = lax.all_to_all(part, 'z', 0, 0, tiled=True)  28.5 us
    all_to_all x1, blocking collectives, per_device(): both = from_pair(lax.all_to_all(both, 'z', 0, 0, tiled=True))  22.3 us
    all_gather x5, blocking collectives, from_pair(): return lax.all_gather(value, 'core', axis=0)  21.5 us
    ppermute x4, starting transfers between devices, from_odd(): lax.ppermute(value, ALL, [(i, i + 1) for i in range(1, peers - 1, 2)])  18.4 us
    all_to_all x1, blocking collectives, per_device(): heard = lax.all_to_all(own, 'outer', 0, 0, tiled=True)  14.1 us
    pallas_call x8, Pallas kernels, call(): pl.pallas_call(with_after, out_shape=jax.ShapeDtypeStruct(out_shape, jnp....  8.5 us
  transfers between devices with their start and end apart: 4, of which 1 were waited for; matrix products, arithmetic and copies ran while one was open for 0% of the time, Pallas kernels for 5%

profile of v3, /device:TPU:1, one launch (start us, length us, event | category | flops | bytes accessed | tf_op | source)
XLA Modules:
  0.0 116.6 jit_solution(17159452345336708298)
XLA Ops:
  0.0 0.0 copy-start
  0.0 5.1 %collective-permute-start = (f32[192,512]{1,0:T(8,128)}, f32[192,512]{1,0:T(8,128)S(1)}, u32[]{:S(2)}, u32[]{:S(2)}) collective-permute-start(f32[192,512]{1,0:T(8,128)} %bitcast.11), channel_id=1, source_target_pairs={{1,2},{3,4},{5,6},{7,8},{9,10},{11,12},{13,14},{15,16},{17,18},{19... | collective-permute-start | bytes 1179656 | tf_op jit(solution)/shard_map/ppermute | solution.py:17
  5.1 2.3 %load.1 = (bf16[2,512,1024]{2,1,0:T(8,128)(2,1)S(1)}, bf16[2,1024,512]{2,1,0:T(8,128)(2,1)S(1)}, f32[2,512]{1,0:T(2,128)S(1)}, f32[192,512]{1,0:T(8,128)S(1)}, f32[1,512]{1,0:T(1,128)S(1)}) custom-call(bf16[2,512,1024]{2,1,0:T(8,128)(2,1)} %refs_0_.1, bf16[2,1024,512]{2,1,0:T(8,128)(2,1)} %refs_1_.1, f32[2,512]{1,0:T(2,128)} %refs_2_.1, f32[192,512]{1,0:T(8,128)} %refs_3_.1, ...), custom_call_target="tpu_custom_call" | custom-call | bytes 4593664 | tf_op jit(solution)/shard_map/load/pallas_call | solution.py:78
  7.4 0.0 copy-done
  7.4 4.6 %all_gather.27.refs_0_ = f32[2,192,512]{2,1,0:T(8,128)S(1)} all-gather(f32[1,192,512]{2,1,0:T(8,128)S(1)} %copy-done), channel_id=1, replica_groups=mesh['outer'=16,'z'=16,'core'=2] {'core'}, dimensions={0}, use_global_device_ids=true | all-gather | bytes 1179648 | tf_op jit(solution)/shard_map/all_gather | solution.py:21
  12.0 0.0 collective-permute-done.refs_1_
  12.0 1.5 %first.1 = f32[192,512]{1,0:T(8,128)S(1)} custom-call(f32[2,192,512]{2,1,0:T(8,128)S(1)} %all_gather.27.refs_0_, f32[192,512]{1,0:T(8,128)S(1)} %collective-permute-done.refs_1_, f32[192,512]{1,0:T(8,128)S(1)} %get-tuple-element.12.refs_2_.refs_3_, bf16[2,512,1024]{2,1,0:T(8,128)(2,1)S(1)} %get-tuple-element.13.refs_3_.refs_1_.refs_4_, ...), custom_call_target="tpu_custom_call" | custom-call | flops 805306368 | bytes 9965568 | tf_op jit(solution)/shard_map/first/pallas_call | solution.py:51
  13.5 2.3 %collective-permute-start.1 = (f32[192,512]{1,0:T(8,128)S(1)}, f32[192,512]{1,0:T(8,128)S(1)}, u32[]{:S(2)}, u32[]{:S(2)}) collective-permute-start(f32[192,512]{1,0:T(8,128)S(1)} %first.1), channel_id=1, source_target_pairs={{1,2},{3,4},{5,6},{7,8},{9,10},{11,12},{13,14},{15,16},{17,18},{19... | collective-permute-start | bytes 1179656 | tf_op jit(solution)/shard_map/ppermute | solution.py:17
  15.9 2.4 %all-gather = f32[384,512]{1,0:T(8,128)S(1)} all-gather(f32[192,512]{1,0:T(8,128)S(1)} %first.1), channel_id=2, replica_groups=mesh['outer'=16,'z'=16,'core'=2] {'core'}, dimensions={0}, use_global_device_ids=true | all-gather | bytes 1179648 | tf_op jit(solution)/shard_map/all_gather | solution.py:21
  18.3 1.5 %second_odd.1.refs_0_ = f32[192,512]{1,0:T(8,128)S(1)} custom-call(f32[2,192,512]{2,1,0:T(8,128)S(1)} %bitcast.10, bf16[2,512,1024]{2,1,0:T(8,128)(2,1)S(1)} %get-tuple-element.13.refs_3_.refs_1_.refs_4_, bf16[2,1024,512]{2,1,0:T(8,128)(2,1)S(1)} %get-tuple-element.14.refs_4_.refs_2_.refs_5_, f32[2,512]{1,0:T(2,128)S(1)} %get-tuple-element.15.refs_5_.refs_3_.refs_6_), custom_call_target="tpu_custom_call" | custom-call | flops 805306368 | bytes 9179136 | tf_op jit(solution)/shard_map/second_odd/pallas_call | solution.py:51
  19.8 3.6 %collective-permute-start.2 = (f32[192,512]{1,0:T(8,128)S(1)}, f32[192,512]{1,0:T(8,128)S(1)}, u32[]{:S(2)}, u32[]{:S(2)}) collective-permute-start(f32[192,512]{1,0:T(8,128)S(1)} %second_odd.1.refs_0_), channel_id=1, source_target_pairs={{1,2},{3,4},{5,6},{7,8},{9,10},{11,12},{13,14},{15,16},{17,18},{19... | collective-permute-start | bytes 1179656 | tf_op jit(solution)/shard_map/ppermute | solution.py:17
  23.4 0.0 collective-permute-done.1.refs_1_
  23.4 1.5 %second.1 = f32[192,512]{1,0:T(8,128)S(1)} custom-call(f32[192,512]{1,0:T(8,128)S(1)} %second_odd.1.refs_0_, f32[192,512]{1,0:T(8,128)S(1)} %collective-permute-done.1.refs_1_, f32[192,512]{1,0:T(8,128)S(1)} %get-tuple-element.12.refs_2_.refs_3_, bf16[2,512,1024]{2,1,0:T(8,128)(2,1)S(1)} %get-tuple-element.13.refs_3_.refs_1_.refs_4_, ...), custom_call_target="tpu_custom_call" | custom-call | flops 805306368 | bytes 9572352 | tf_op jit(solution)/shard_map/second/pallas_call | solution.py:51
  24.9 2.4 %all-gather.1 = f32[384,512]{1,0:T(8,128)S(1)} all-gather(f32[192,512]{1,0:T(8,128)S(1)} %second.1), channel_id=3, replica_groups=mesh['outer'=16,'z'=16,'core'=2] {'core'}, dimensions={0}, use_global_device_ids=true | all-gather | bytes 1179648 | tf_op jit(solution)/shard_map/all_gather | solution.py:21
  27.3 0.8 collective-permute-done.2.refs_1_
  28.0 1.5 %third.1 = f32[192,512]{1,0:T(8,128)S(1)} custom-call(f32[2,192,512]{2,1,0:T(8,128)S(1)} %bitcast.7, f32[192,512]{1,0:T(8,128)S(1)} %collective-permute-done.2.refs_1_, f32[192,512]{1,0:T(8,128)S(1)} %get-tuple-element.12.refs_2_.refs_3_, bf16[2,512,1024]{2,1,0:T(8,128)(2,1)S(1)} %get-tuple-element.13.refs_3_.refs_1_.refs_4_, ...), custom_call_target="tpu_custom_call" | custom-call | flops 805306368 | bytes 9965568 | tf_op jit(solution)/shard_map/third/pallas_call | solution.py:51
  29.5 2.4 %all-gather.2 = f32[384,512]{1,0:T(8,128)S(1)} all-gather(f32[192,512]{1,0:T(8,128)S(1)} %third.1), channel_id=4, replica_groups=mesh['outer'=16,'z'=16,'core'=2] {'core'}, dimensions={0}, use_global_device_ids=true | all-gather | bytes 1179648 | tf_op jit(solution)/shard_map/all_gather | solution.py:21
  31.9 0.1 part.1
  32.0 28.5 %all_to_all.15.refs_0_ = f32[16,24,128]{2,1,0:T(8,128)S(1)} all-to-all(f32[16,24,128]{2,1,0:T(8,128)S(1)} %part.1), channel_id=1, replica_groups=mesh['outer'=16,'z'=16,'core'=2] {'z'}, dimensions={0} | all-to-all | bytes 393216 | tf_op jit(solution)/shard_map/all_to_all | solution.py:226
  60.5 7.4 %collective-permute-start.3 = (f32[192,512]{1,0:T(8,128)S(1)}, f32[192,512]{1,0:T(8,128)S(1)}, u32[]{:S(2)}, u32[]{:S(2)}) collective-permute-start(f32[192,512]{1,0:T(8,128)S(1)} %third.1), channel_id=1, source_target_pairs={{1,2},{3,4},{5,6},{7,8},{9,10},{11,12},{13,14},{15,16},{17,18},{19... | collective-permute-start | bytes 1179656 | tf_op jit(solution)/shard_map/ppermute | solution.py:17
  68.0 14.1 %all_to_all.16.refs_0_ = f32[16,32,128]{2,1,0:T(8,128)S(1)} all-to-all(f32[16,32,128]{2,1,0:T(8,128)S(1)} %own.1), channel_id=1, replica_groups=mesh['outer'=16,'z'=16,'core'=2] {'outer'}, dimensions={0} | all-to-all | bytes 524288 | tf_op jit(solution)/shard_map/all_to_all | solution.py:235
  82.1 0.0 collective-permute-done.3.refs_1_.refs_2_
  82.1 0.1 scan.1
  82.1 22.3 %all_to_all.17 = f32[16,48,128]{2,1,0:T(8,128)S(1)} all-to-all(f32[16,48,128]{2,1,0:T(8,128)S(1)} %scan.1), channel_id=1, replica_groups=mesh['outer'=16,'z'=16,'core'=2] {'z'}, dimensions={0} | all-to-all | bytes 786432 | tf_op jit(solution)/shard_map/all_to_all | solution.py:237
  104.4 9.8 %all-gather.3 = f32[32,48,128]{2,1,0:T(8,128)S(1)} all-gather(f32[16,48,128]{2,1,0:T(8,128)S(1)} %all_to_all.17), channel_id=5, replica_groups=mesh['outer'=16,'z'=16,'core'=2] {'core'}, dimensions={0}, use_global_device_ids=true | all-gather | bytes 1179648 | tf_op jit(solution)/shard_map/all_gather | solution.py:21
  114.2 2.3 %last.1 = f32[1,192,512]{2,1,0:T(8,128)} custom-call(f32[2,16,48,128]{3,2,1,0:T(8,128)S(1)} %bitcast.9, f32[2,192,512]{2,1,0:T(8,128)S(1)} %bitcast.6, f32[192,512]{1,0:T(8,128)S(1)} %collective-permute-done.3.refs_1_.refs_2_, f32[192,512]{1,0:T(8,128)S(1)} %get-tuple-element.12.refs_2_.refs_3_, ...), custom_call_target="tpu_custom_call" | custom-call | flops 805306368 | bytes 10752000 | tf_op jit(solution)/shard_map/last/pallas_call | solution.py:51
  (1 shorter events, 0.0 us)
Async XLA Ops:
  0.0 7.4 %copy-start = (f32[1,192,512]{2,1,0:T(8,128)S(1)}, f32[1,192,512]{2,1,0:T(8,128)}, u32[]{:S(2)}) copy-start(f32[1,192,512]{2,1,0:T(8,128)} %param.7) | copy-start | bytes 1179652
  0.0 12.0 %collective-permute-start = (f32[192,512]{1,0:T(8,128)}, f32[192,512]{1,0:T(8,128)S(1)}, u32[]{:S(2)}, u32[]{:S(2)}) collective-permute-start(f32[192,512]{1,0:T(8,128)} %bitcast.11), channel_id=1, source_target_pairs={{1,2},{3,4},{5,6},{7,8},{9,10},{11,12},{13,14},{15,16},{17,18},{19... | collective-permute-start | bytes 1179656 | tf_op jit(solution)/shard_map/ppermute | solution.py:17
  13.5 9.8 %collective-permute-start.1 = (f32[192,512]{1,0:T(8,128)S(1)}, f32[192,512]{1,0:T(8,128)S(1)}, u32[]{:S(2)}, u32[]{:S(2)}) collective-permute-start(f32[192,512]{1,0:T(8,128)S(1)} %first.1), channel_id=1, source_target_pairs={{1,2},{3,4},{5,6},{7,8},{9,10},{11,12},{13,14},{15,16},{17,18},{19... | collective-permute-start | bytes 1179656 | tf_op jit(solution)/shard_map/ppermute | solution.py:17
  19.8 8.3 %collective-permute-start.2 = (f32[192,512]{1,0:T(8,128)S(1)}, f32[192,512]{1,0:T(8,128)S(1)}, u32[]{:S(2)}, u32[]{:S(2)}) collective-permute-start(f32[192,512]{1,0:T(8,128)S(1)} %second_odd.1.refs_0_), channel_id=1, source_target_pairs={{1,2},{3,4},{5,6},{7,8},{9,10},{11,12},{13,14},{15,16},{17,18},{19... | collective-permute-start | bytes 1179656 | tf_op jit(solution)/shard_map/ppermute | solution.py:17
  60.5 21.6 %collective-permute-start.3 = (f32[192,512]{1,0:T(8,128)S(1)}, f32[192,512]{1,0:T(8,128)S(1)}, u32[]{:S(2)}, u32[]{:S(2)}) collective-permute-start(f32[192,512]{1,0:T(8,128)S(1)} %third.1), channel_id=1, source_target_pairs={{1,2},{3,4},{5,6},{7,8},{9,10},{11,12},{13,14},{15,16},{17,18},{19... | collective-permute-start | bytes 1179656 | tf_op jit(solution)/shard_map/ppermute | solution.py:17

commit v4 on v3

--- a/solution.py
+++ b/solution.py
@@ -99,20 +99,21 @@
     return lax.axis_index(ALL) == 0
 
 
-def choose_kernel(pair, hop, start, weight_in, weight_out, norm_gain, out):
-    even = jnp.where(is_first(), start[...], hop[...])
-    state = jnp.where(is_odd(), pair[0], even)
-    out[...] = layers(state, weight_in, weight_out, norm_gain)
-
-
 def odd_kernel(pair, weight_in, weight_out, norm_gain, out):
-    out[...] = layers(pair[0], weight_in, weight_out, norm_gain)
-
-
-def even_kernel(ready, hop, start, weight_in, weight_out, norm_gain, out):
-    even = jnp.where(is_first(), start[...], hop[...])
-    state = layers(even, weight_in, weight_out, norm_gain)
-    out[...] = jnp.where(is_odd(), ready[...], state)
+    @pl.when(is_odd())
+    def _():
+        out[...] = layers(pair[0], weight_in, weight_out, norm_gain)
+
+
+def even_kernel(odd, hop, start, weight_in, weight_out, norm_gain, out):
+    @pl.when(is_odd())
+    def _():
+        out[...] = odd[...]
+
+    @pl.when(jnp.logical_not(is_odd()))
+    def _():
+        state = jnp.where(is_first(), start[...], hop[...])
+        out[...] = layers(state, weight_in, weight_out, norm_gain)
 
 
 def part_kernel(third, second, out):
@@ -209,23 +210,19 @@
     def block(body, args, name):
         return call(body, (tokens, width), args + params, name, flops)
 
-    guess_z = from_odd(guess[0])
-    guess_pair = from_pair(guess[0])
-    first = block(choose_kernel, (guess_pair, guess_z, start_state), "first")
-    first_z = from_odd(first)
-    first_pair = from_pair(first)
-    second_odd = block(odd_kernel, (first_pair,), "second_odd")
-    second_z = from_odd(second_odd)
-    second = block(even_kernel, (second_odd, first_z, start_state), "second")
-    second_pair = from_pair(second)
-    third = block(choose_kernel, (second_pair, second_z, start_state), "third")
-    third_pair = from_pair(third)
+    pairs = [from_pair(guess[0])]
+    hop = from_odd(guess[0])
+    for _ in range(3):
+        odd = block(odd_kernel, (pairs[-1],), "odd")
+        next_hop = from_odd(odd)
+        state = block(even_kernel, (odd, hop, start_state), "even")
+        pairs.append(from_pair(state))
+        hop = next_hop
+    second_pair, third_pair = pairs[2:]
 
     rows = tokens * width // LANES // places // cores
     part = call(part_kernel, (places, rows, LANES), (third_pair, second_pair), "part")
-    parts = lax.all_to_all(part, "z", 0, 0, tiled=True)
-    third, parts = lax.optimization_barrier((third, parts))
-    third_z = from_odd(third)
+    parts, hop = lax.optimization_barrier((lax.all_to_all(part, "z", 0, 0, tiled=True), hop))
     own = call(
         functools.partial(own_kernel, places * cores),
         (groups, rows + 8, LANES),
@@ -233,12 +230,12 @@
         "own",
     )
     heard = lax.all_to_all(own, "outer", 0, 0, tiled=True)
-    both = call(scan_kernel, (places, 2 * rows, LANES), (heard,), "scan", after=(third_z,))
+    both = call(scan_kernel, (places, 2 * rows, LANES), (heard,), "scan")
     both = from_pair(lax.all_to_all(both, "z", 0, 0, tiled=True))
     return call(
         last_kernel,
         (1, tokens, width),
-        (both, third_pair, third_z, start_state) + params,
+        (both, third_pair, hop, start_state) + params,
         "last",
         flops,
     )

time: 117 us -> 114 us (0.974)
  blocking collectives: 86.4 us -> 63.2 us
  starting transfers between devices: 18.4 us -> 29.4 us
  waiting for transfers between devices: 0.78 us -> 10.2 us
  Pallas kernels: 10.8 us -> 9.2 us
  local copies, waits for them, and re-layouts: 0.01 us -> 1.43 us
    all_to_all x1 -> x0, blocking collectives: 28.5 us -> none  [per_device(): parts = lax.all_to_all(part, 'z', 0, 0, tiled=True)]
    all_to_all x0 -> x1, starting transfers between devices: none -> 17.6 us  [per_device(): lax.all_to_all(part, 'z', 0, 0, tiled=True)]
    ppermute x4, waiting for transfers between devices: 0.78 us -> 10.2 us  [from_odd(): lax.ppermute(value, ALL, [(i, i + 1) for i in range(1, peers - 1, 2)])]
    ppermute x4, starting transfers between devices: 18.4 us -> 11.8 us  [from_odd(): lax.ppermute(value, ALL, [(i, i + 1) for i in range(1, peers - 1, 2)])]
    all_to_all x1, blocking collectives: 22.3 us -> 26.5 us  [per_device(): both = from_pair(lax.all_to_all(both, 'z', 0, 0, tiled=True))]
    pallas_call x8 -> x10, Pallas kernels: 8.5 us -> 6.88 us  [call(): pl.pallas_call(with_after, out_shape=jax.ShapeDtypeStruct(out_shape, jnp....]
    unnamed x2 -> x14, local copies, waits for them, and re-layouts: 0.01 us -> 1.43 us
  transfers between devices with their start and end apart: 4 -> 5, of which waited for: 1 -> 2; matrix products, arithmetic and copies ran while one was open for 0% -> 0% of each run, Pallas kernels for 5% -> 6%
where the time goes in v4:
time: 114 us
  blocking collectives  63.2 us (55%)
  starting transfers between devices  29.4 us (26%)
  waiting for transfers between devices  10.2 us (9%)
  Pallas kernels  9.2 us (8%)
  local copies, waits for them, and re-layouts  1.43 us (1%)
    all_to_all x1, blocking collectives, per_device(): both = from_pair(lax.all_to_all(both, 'z', 0, 0, tiled=True))  26.5 us
    all_gather x5, blocking collectives, from_pair(): return lax.all_gather(value, 'core', axis=0)  22.5 us
    all_to_all x1, starting transfers between devices, per_device(): lax.all_to_all(part, 'z', 0, 0, tiled=True)  17.6 us
    all_to_all x1, blocking collectives, per_device(): heard = lax.all_to_all(own, 'outer', 0, 0, tiled=True)  14.2 us
    ppermute x4, starting transfers between devices, from_odd(): lax.ppermute(value, ALL, [(i, i + 1) for i in range(1, peers - 1, 2)])  11.8 us
    ppermute x4, waiting for transfers between devices, from_odd(): lax.ppermute(value, ALL, [(i, i + 1) for i in range(1, peers - 1, 2)])  10.2 us
    pallas_call x10, Pallas kernels, call(): pl.pallas_call(with_after, out_shape=jax.ShapeDtypeStruct(out_shape, jnp....  6.88 us
    pallas_call x1, Pallas kernels, loaded(): pl.pallas_call(load_kernel, out_shape=[pltpu.VMEM(a.shape, a.dtype) for a...  2.32 us
  transfers between devices with their start and end apart: 5, of which 2 were waited for; matrix products, arithmetic and copies ran while one was open for 0% of the time, Pallas kernels for 6%

profile of v4, /device:TPU:1, one launch (start us, length us, event | category | flops | bytes accessed | tf_op | source)
XLA Modules:
  0.0 113.6 jit_solution(9210835041752883242)
XLA Ops:
  0.0 0.0 copy-start.6
  0.0 5.1 %collective-permute-start = (f32[192,512]{1,0:T(8,128)}, f32[192,512]{1,0:T(8,128)S(1)}, u32[]{:S(2)}, u32[]{:S(2)}) collective-permute-start(f32[192,512]{1,0:T(8,128)} %bitcast.11), channel_id=1, source_target_pairs={{1,2},{3,4},{5,6},{7,8},{9,10},{11,12},{13,14},{15,16},{17,18},{19... | collective-permute-start | bytes 1179656 | tf_op jit(solution)/shard_map/ppermute | solution.py:17
  5.1 2.3 %load.1 = (bf16[2,512,1024]{2,1,0:T(8,128)(2,1)S(1)}, bf16[2,1024,512]{2,1,0:T(8,128)(2,1)S(1)}, f32[2,512]{1,0:T(2,128)S(1)}, f32[192,512]{1,0:T(8,128)S(1)}, f32[1,512]{1,0:T(1,128)S(1)}) custom-call(bf16[2,512,1024]{2,1,0:T(8,128)(2,1)} %refs_0_.1, bf16[2,1024,512]{2,1,0:T(8,128)(2,1)} %refs_1_.1, f32[2,512]{1,0:T(2,128)} %refs_2_.1, f32[192,512]{1,0:T(8,128)} %refs_3_.1, ...), custom_call_target="tpu_custom_call" | custom-call | bytes 4593664 | tf_op jit(solution)/shard_map/load/pallas_call | solution.py:78
  7.4 0.0 copy-done.6
  7.4 0.0 copy-start
  7.4 4.6 %all_gather.27.refs_0_ = f32[2,192,512]{2,1,0:T(8,128)S(1)} all-gather(f32[1,192,512]{2,1,0:T(8,128)S(1)} %copy-done.6), channel_id=1, replica_groups=mesh['outer'=16,'z'=16,'core'=2] {'core'}, dimensions={0}, use_global_device_ids=true | all-gather | bytes 1179648 | tf_op jit(solution)/shard_map/all_gather | solution.py:21
  12.0 1.4 %odd.3.refs_0_ = f32[192,512]{1,0:T(8,128)S(1)} custom-call(f32[2,192,512]{2,1,0:T(8,128)S(1)} %all_gather.27.refs_0_, bf16[2,512,1024]{2,1,0:T(8,128)(2,1)S(1)} %get-tuple-element.12.refs_1_.refs_3_.refs_4_, bf16[2,1024,512]{2,1,0:T(8,128)(2,1)S(1)} %get-tuple-element.13.refs_2_.refs_4_.refs_5_, f32[2,512]{1,0:T(2,128)S(1)} %get-tuple-element.14.refs_3_.refs_5_.refs_6_), custom_call_target="tpu_custom_call" | custom-call | flops 805306368 | bytes 9179136 | tf_op jit(solution)/shard_map/odd/pallas_call | solution.py:51
  13.5 1.3 %collective-permute-start.1 = (f32[192,512]{1,0:T(8,128)S(1)}, f32[192,512]{1,0:T(8,128)S(1)}, u32[]{:S(2)}, u32[]{:S(2)}) collective-permute-start(f32[192,512]{1,0:T(8,128)S(1)} %odd.3.refs_0_), channel_id=1, source_target_pairs={{1,2},{3,4},{5,6},{7,8},{9,10},{11,12},{13,14},{15,16},{17,18},{19... | collective-permute-start | bytes 1179656 | tf_op jit(solution)/shard_map/ppermute | solution.py:17
  14.8 0.0 collective-permute-done.refs_1_
  14.9 2.4 %all-gather = f32[384,512]{1,0:T(8,128)S(1)} all-gather(f32[192,512]{1,0:T(8,128)S(1)} %even.3), channel_id=2, replica_groups=mesh['outer'=16,'z'=16,'core'=2] {'core'}, dimensions={0}, use_global_device_ids=true | all-gather | bytes 1179648 | tf_op jit(solution)/shard_map/all_gather | solution.py:21
  17.2 1.4 %odd.4.refs_0_ = f32[192,512]{1,0:T(8,128)S(1)} custom-call(f32[2,192,512]{2,1,0:T(8,128)S(1)} %bitcast.10, bf16[2,512,1024]{2,1,0:T(8,128)(2,1)S(1)} %get-tuple-element.12.refs_1_.refs_3_.refs_4_, bf16[2,1024,512]{2,1,0:T(8,128)(2,1)S(1)} %get-tuple-element.13.refs_2_.refs_4_.refs_5_, f32[2,512]{1,0:T(2,128)S(1)} %get-tuple-element.14.refs_3_.refs_5_.refs_6_), custom_call_target="tpu_custom_call" | custom-call | flops 805306368 | bytes 9179136 | tf_op jit(solution)/shard_map/odd/pallas_call | solution.py:51
  18.7 1.3 %collective-permute-start.2 = (f32[192,512]{1,0:T(8,128)S(1)}, f32[192,512]{1,0:T(8,128)S(1)}, u32[]{:S(2)}, u32[]{:S(2)}) collective-permute-start(f32[192,512]{1,0:T(8,128)S(1)} %odd.4.refs_0_), channel_id=1, source_target_pairs={{1,2},{3,4},{5,6},{7,8},{9,10},{11,12},{13,14},{15,16},{17,18},{19... | collective-permute-start | bytes 1179656 | tf_op jit(solution)/shard_map/ppermute | solution.py:17
  20.0 0.0 collective-permute-done.1.refs_1_
  20.1 2.4 %all-gather.1 = f32[384,512]{1,0:T(8,128)S(1)} all-gather(f32[192,512]{1,0:T(8,128)S(1)} %even.4), channel_id=3, replica_groups=mesh['outer'=16,'z'=16,'core'=2] {'core'}, dimensions={0}, use_global_device_ids=true | all-gather | bytes 1179648 | tf_op jit(solution)/shard_map/all_gather | solution.py:21
  22.4 1.4 %odd.5.refs_0_ = f32[192,512]{1,0:T(8,128)S(1)} custom-call(f32[2,192,512]{2,1,0:T(8,128)S(1)} %bitcast.7, bf16[2,512,1024]{2,1,0:T(8,128)(2,1)S(1)} %get-tuple-element.12.refs_1_.refs_3_.refs_4_, bf16[2,1024,512]{2,1,0:T(8,128)(2,1)S(1)} %get-tuple-element.13.refs_2_.refs_4_.refs_5_, f32[2,512]{1,0:T(2,128)S(1)} %get-tuple-element.14.refs_3_.refs_5_.refs_6_), custom_call_target="tpu_custom_call" | custom-call | flops 805306368 | bytes 9179136 | tf_op jit(solution)/shard_map/odd/pallas_call | solution.py:51
  23.9 0.0 copy-start.2
  23.9 0.8 collective-permute-done.2.refs_1_
  24.7 0.0 copy-done
  24.7 0.0 copy-done.2
  24.7 2.4 %all-gather.2 = f32[384,512]{1,0:T(8,128)S(1)} all-gather(f32[192,512]{1,0:T(8,128)S(1)} %even.5), channel_id=4, replica_groups=mesh['outer'=16,'z'=16,'core'=2] {'core'}, dimensions={0}, use_global_device_ids=true | all-gather | bytes 1179648 | tf_op jit(solution)/shard_map/all_gather | solution.py:21
  27.1 0.1 part.1
  27.2 0.0 copy-start.3
  27.2 0.7 copy-done.3
  27.9 17.6 %all-to-all-start = ((f32[16,24,128]{2,1,0:T(8,128)}), f32[16,24,128]{2,1,0:T(8,128)S(1)}, u32[]{:S(2)}, u32[]{:S(2)}) async-start(f32[16,24,128]{2,1,0:T(8,128)} %copy-done.3), calls=%async_computation | async-start | bytes 393216 | tf_op jit(solution)/shard_map/all_to_all | solution.py:225
  45.5 4.1 %collective-permute-start.3 = (f32[192,512]{1,0:T(8,128)}, f32[192,512]{1,0:T(8,128)S(1)}, u32[]{:S(2)}, u32[]{:S(2)}) collective-permute-start(f32[192,512]{1,0:T(8,128)} %copy-done.2), channel_id=1, source_target_pairs={{1,2},{3,4},{5,6},{7,8},{9,10},{11,12},{13,14},{15,16},{17,18},{19... | collective-permute-start | bytes 1179656 | tf_op jit(solution)/shard_map/ppermute | solution.py:17
  49.6 9.4 %collective-permute-done.3.refs_2_ = f32[192,512]{1,0:T(8,128)S(1)} collective-permute-done((f32[192,512]{1,0:T(8,128)}, f32[192,512]{1,0:T(8,128)S(1)}, u32[]{:S(2)}, u32[]{:S(2)}) %collective-permute-start.3) | collective-permute-done | bytes 393248 | tf_op jit(solution)/shard_map/ppermute | solution.py:17
  59.0 0.0 copy-start.4
  59.0 0.7 copy-done.4
  59.8 0.0 all-to-all-done.refs_0_
  59.8 0.0 copy-start.1
  59.8 0.0 copy-start.5
  59.8 14.2 %all_to_all.15.refs_0_ = f32[16,32,128]{2,1,0:T(8,128)S(1)} all-to-all(f32[16,32,128]{2,1,0:T(8,128)S(1)} %own.1), channel_id=1, replica_groups=mesh['outer'=16,'z'=16,'core'=2] {'outer'}, dimensions={0} | all-to-all | bytes 524288 | tf_op jit(solution)/shard_map/all_to_all | solution.py:232
  74.1 0.1 scan.1
  74.1 26.5 %all_to_all.16 = f32[16,48,128]{2,1,0:T(8,128)S(1)} all-to-all(f32[16,48,128]{2,1,0:T(8,128)S(1)} %scan.1), channel_id=1, replica_groups=mesh['outer'=16,'z'=16,'core'=2] {'z'}, dimensions={0} | all-to-all | bytes 786432 | tf_op jit(solution)/shard_map/all_to_all | solution.py:234
  100.6 10.8 %all-gather.3 = f32[32,48,128]{2,1,0:T(8,128)S(1)} all-gather(f32[16,48,128]{2,1,0:T(8,128)S(1)} %all_to_all.16), channel_id=5, replica_groups=mesh['outer'=16,'z'=16,'core'=2] {'core'}, dimensions={0}, use_global_device_ids=true | all-gather | bytes 1179648 | tf_op jit(solution)/shard_map/all_gather | solution.py:21
  111.4 0.0 copy-done.1
  111.4 0.0 copy-done.5
  111.4 2.3 %last.1 = f32[1,192,512]{2,1,0:T(8,128)} custom-call(f32[2,16,48,128]{3,2,1,0:T(8,128)S(1)} %bitcast.9, f32[2,192,512]{2,1,0:T(8,128)S(1)} %bitcast.6, f32[192,512]{1,0:T(8,128)S(1)} %copy-done.5, f32[192,512]{1,0:T(8,128)S(1)} %get-tuple-element.15.refs_2_.refs_3_, bf16[2,512,1024]{2,1,0:T(8,128)(2,1)S(1)} %get-tuple-element.12.refs_1_.refs_3_.refs_4_, ...), custom_call_target="tpu_custom_call" | custom-call | flops 805306368 | bytes 10752000 | tf_op jit(solution)/shard_map/last/pallas_call | solution.py:51
  (4 shorter events, 0.1 us)
Async XLA Ops:
  0.0 7.4 %copy-start.6 = (f32[1,192,512]{2,1,0:T(8,128)S(1)}, f32[1,192,512]{2,1,0:T(8,128)}, u32[]{:S(2)}) copy-start(f32[1,192,512]{2,1,0:T(8,128)} %param.7) | copy-start | bytes 1179652
  0.0 14.8 %collective-permute-start = (f32[192,512]{1,0:T(8,128)}, f32[192,512]{1,0:T(8,128)S(1)}, u32[]{:S(2)}, u32[]{:S(2)}) collective-permute-start(f32[192,512]{1,0:T(8,128)} %bitcast.11), channel_id=1, source_target_pairs={{1,2},{3,4},{5,6},{7,8},{9,10},{11,12},{13,14},{15,16},{17,18},{19... | collective-permute-start | bytes 1179656 | tf_op jit(solution)/shard_map/ppermute | solution.py:17
  7.4 17.3 %copy-start = (bf16[2,1024,512]{2,1,0:T(8,128)(2,1)}, bf16[2,1024,512]{2,1,0:T(8,128)(2,1)S(1)}, u32[]{:S(2)}) copy-start(bf16[2,1024,512]{2,1,0:T(8,128)(2,1)S(1)} %get-tuple-element.13.refs_2_.refs_4_.refs_5_) | copy-start | bytes 6291460
  13.5 6.5 %collective-permute-start.1 = (f32[192,512]{1,0:T(8,128)S(1)}, f32[192,512]{1,0:T(8,128)S(1)}, u32[]{:S(2)}, u32[]{:S(2)}) collective-permute-start(f32[192,512]{1,0:T(8,128)S(1)} %odd.3.refs_0_), channel_id=1, source_target_pairs={{1,2},{3,4},{5,6},{7,8},{9,10},{11,12},{13,14},{15,16},{17,18},{19... | collective-permute-start | bytes 1179656 | tf_op jit(solution)/shard_map/ppermute | solution.py:17
  18.7 6.0 %collective-permute-start.2 = (f32[192,512]{1,0:T(8,128)S(1)}, f32[192,512]{1,0:T(8,128)S(1)}, u32[]{:S(2)}, u32[]{:S(2)}) collective-permute-start(f32[192,512]{1,0:T(8,128)S(1)} %odd.4.refs_0_), channel_id=1, source_target_pairs={{1,2},{3,4},{5,6},{7,8},{9,10},{11,12},{13,14},{15,16},{17,18},{19... | collective-permute-start | bytes 1179656 | tf_op jit(solution)/shard_map/ppermute | solution.py:17
  23.9 0.8 copy-start.2
  27.2 0.7 copy-start.3
  27.9 31.9 %all-to-all-start = ((f32[16,24,128]{2,1,0:T(8,128)}), f32[16,24,128]{2,1,0:T(8,128)S(1)}, u32[]{:S(2)}, u32[]{:S(2)}) async-start(f32[16,24,128]{2,1,0:T(8,128)} %copy-done.3), calls=%async_computation | async-start | bytes 393216 | tf_op jit(solution)/shard_map/all_to_all | solution.py:225
  45.5 13.6 %collective-permute-start.3 = (f32[192,512]{1,0:T(8,128)}, f32[192,512]{1,0:T(8,128)S(1)}, u32[]{:S(2)}, u32[]{:S(2)}) collective-permute-start(f32[192,512]{1,0:T(8,128)} %copy-done.2), channel_id=1, source_target_pairs={{1,2},{3,4},{5,6},{7,8},{9,10},{11,12},{13,14},{15,16},{17,18},{19... | collective-permute-start | bytes 1179656 | tf_op jit(solution)/shard_map/ppermute | solution.py:17
  59.0 0.7 copy-start.4
  59.8 51.6 %copy-start.1 = (bf16[2,1024,512]{2,1,0:T(8,128)(2,1)S(1)}, bf16[2,1024,512]{2,1,0:T(8,128)(2,1)}, u32[]{:S(2)}) copy-start(bf16[2,1024,512]{2,1,0:T(8,128)(2,1)} %copy-done) | copy-start | bytes 6291460
  59.8 51.6 %copy-start.5 = (f32[192,512]{1,0:T(8,128)S(1)}, f32[192,512]{1,0:T(8,128)}, u32[]{:S(2)}) copy-start(f32[192,512]{1,0:T(8,128)} %copy-done.4) | copy-start | bytes 1179652

commit v5 on v4

--- a/solution.py
+++ b/solution.py
@@ -222,14 +222,14 @@
 
     rows = tokens * width // LANES // places // cores
     part = call(part_kernel, (places, rows, LANES), (third_pair, second_pair), "part")
-    parts, hop = lax.optimization_barrier((lax.all_to_all(part, "z", 0, 0, tiled=True), hop))
+    parts = lax.all_to_all(part, "z", 0, 0, tiled=True)
     own = call(
         functools.partial(own_kernel, places * cores),
         (groups, rows + 8, LANES),
         (parts, coarse_gain),
         "own",
     )
-    heard = lax.all_to_all(own, "outer", 0, 0, tiled=True)
+    heard, hop = lax.optimization_barrier((lax.all_to_all(own, "outer", 0, 0, tiled=True), hop))
     both = call(scan_kernel, (places, 2 * rows, LANES), (heard,), "scan")
     both = from_pair(lax.all_to_all(both, "z", 0, 0, tiled=True))
     return call(

time: 114 us -> 112 us (0.982)
  blocking collectives: 63.2 us -> 46.6 us
  starting transfers between devices: 29.4 us -> 36.9 us
  waiting for transfers between devices: 10.2 us -> 16.4 us
  Pallas kernels: 9.2 us -> 10.9 us
    all_to_all x1 -> x2, waiting for transfers between devices: 0.01 us -> 15.6 us  [the longest x1 8.07 us: per_device(): parts = lax.all_to_all(part, 'z', 0, 0, tiled=True)]
    all_to_all x1 -> x0, blocking collectives: 14.2 us -> none  [per_device(): heard = lax.all_to_all(own, 'outer', 0, 0, tiled=True)]
    ppermute x4, waiting for transfers between devices: 10.2 us -> 0.79 us  [from_odd(): lax.ppermute(value, ALL, [(i, i + 1) for i in range(1, peers - 1, 2)])]
    all_to_all x1 -> x2, starting transfers between devices: 17.6 us -> 24.4 us  [the longest x1 17.6 us: per_device(): parts = lax.all_to_all(part, 'z', 0, 0, tiled=True)]
    all_gather x5, blocking collectives: 22.5 us -> 20.7 us  [from_pair(): return lax.all_gather(value, 'core', axis=0)]
    pallas_call x10, Pallas kernels: 6.88 us -> 8.57 us  [call(): pl.pallas_call(with_after, out_shape=jax.ShapeDtypeStruct(out_shape, jnp....]
  transfers between devices with their start and end apart: 5 -> 6, of which waited for: 2 -> 3; matrix products, arithmetic and copies ran while one was open for 0% -> 0% of each run, Pallas kernels for 6% -> 7%
where the time goes in v5:
time: 112 us
  blocking collectives  46.6 us (42%)
  starting transfers between devices  36.9 us (33%)
  waiting for transfers between devices  16.4 us (15%)
  Pallas kernels  10.9 us (10%)
    all_to_all x1, blocking collectives, per_device(): both = from_pair(lax.all_to_all(both, 'z', 0, 0, tiled=True))  25.9 us
    all_gather x5, blocking collectives, from_pair(): return lax.all_gather(value, 'core', axis=0)  20.7 us
    all_to_all x1, starting transfers between devices, per_device(): parts = lax.all_to_all(part, 'z', 0, 0, tiled=True)  17.6 us
    ppermute x4, starting transfers between devices, from_odd(): lax.ppermute(value, ALL, [(i, i + 1) for i in range(1, peers - 1, 2)])  12.5 us
    pallas_call x10, Pallas kernels, call(): pl.pallas_call(with_after, out_shape=jax.ShapeDtypeStruct(out_shape, jnp....  8.57 us
    all_to_all x1, waiting for transfers between devices, per_device(): parts = lax.all_to_all(part, 'z', 0, 0, tiled=True)  8.07 us
    all_to_all x1, waiting for transfers between devices, per_device(): lax.all_to_all(own, 'outer', 0, 0, tiled=True)  7.53 us
    all_to_all x1, starting transfers between devices, per_device(): lax.all_to_all(own, 'outer', 0, 0, tiled=True)  6.75 us
  transfers between devices with their start and end apart: 6, of which 3 were waited for; matrix products, arithmetic and copies ran while one was open for 0% of the time, Pallas kernels for 7%

profile of v5, /device:TPU:1, one launch (start us, length us, event | category | flops | bytes accessed | tf_op | source)
XLA Modules:
  0.0 111.7 jit_solution(2750151276245426596)
XLA Ops:
  0.0 0.0 copy-start.4
  0.0 5.1 %collective-permute-start = (f32[192,512]{1,0:T(8,128)}, f32[192,512]{1,0:T(8,128)S(1)}, u32[]{:S(2)}, u32[]{:S(2)}) collective-permute-start(f32[192,512]{1,0:T(8,128)} %bitcast.11), channel_id=1, source_target_pairs={{1,2},{3,4},{5,6},{7,8},{9,10},{11,12},{13,14},{15,16},{17,18},{19... | collective-permute-start | bytes 1179656 | tf_op jit(solution)/shard_map/ppermute | solution.py:17
  5.1 2.3 %load.1 = (bf16[2,512,1024]{2,1,0:T(8,128)(2,1)S(1)}, bf16[2,1024,512]{2,1,0:T(8,128)(2,1)S(1)}, f32[2,512]{1,0:T(2,128)S(1)}, f32[192,512]{1,0:T(8,128)S(1)}, f32[1,512]{1,0:T(1,128)S(1)}) custom-call(bf16[2,512,1024]{2,1,0:T(8,128)(2,1)} %refs_0_.1, bf16[2,1024,512]{2,1,0:T(8,128)(2,1)} %refs_1_.1, f32[2,512]{1,0:T(2,128)} %refs_2_.1, f32[192,512]{1,0:T(8,128)} %refs_3_.1, ...), custom_call_target="tpu_custom_call" | custom-call | bytes 4593664 | tf_op jit(solution)/shard_map/load/pallas_call | solution.py:78
  7.4 0.0 copy-done.4
  7.4 0.0 copy-start
  7.4 4.6 %all_gather.27.refs_0_ = f32[2,192,512]{2,1,0:T(8,128)S(1)} all-gather(f32[1,192,512]{2,1,0:T(8,128)S(1)} %copy-done.4), channel_id=1, replica_groups=mesh['outer'=16,'z'=16,'core'=2] {'core'}, dimensions={0}, use_global_device_ids=true | all-gather | bytes 1179648 | tf_op jit(solution)/shard_map/all_gather | solution.py:21
  12.0 1.4 %odd.3.refs_0_ = f32[192,512]{1,0:T(8,128)S(1)} custom-call(f32[2,192,512]{2,1,0:T(8,128)S(1)} %all_gather.27.refs_0_, bf16[2,512,1024]{2,1,0:T(8,128)(2,1)S(1)} %get-tuple-element.12.refs_1_.refs_3_.refs_4_, bf16[2,1024,512]{2,1,0:T(8,128)(2,1)S(1)} %get-tuple-element.13.refs_2_.refs_4_.refs_5_, f32[2,512]{1,0:T(2,128)S(1)} %get-tuple-element.14.refs_3_.refs_5_.refs_6_), custom_call_target="tpu_custom_call" | custom-call | flops 805306368 | bytes 9179136 | tf_op jit(solution)/shard_map/odd/pallas_call | solution.py:51
  13.5 1.3 %collective-permute-start.1 = (f32[192,512]{1,0:T(8,128)S(1)}, f32[192,512]{1,0:T(8,128)S(1)}, u32[]{:S(2)}, u32[]{:S(2)}) collective-permute-start(f32[192,512]{1,0:T(8,128)S(1)} %odd.3.refs_0_), channel_id=1, source_target_pairs={{1,2},{3,4},{5,6},{7,8},{9,10},{11,12},{13,14},{15,16},{17,18},{19... | collective-permute-start | bytes 1179656 | tf_op jit(solution)/shard_map/ppermute | solution.py:17
  14.8 0.0 collective-permute-done.refs_1_
  14.9 2.4 %all-gather = f32[384,512]{1,0:T(8,128)S(1)} all-gather(f32[192,512]{1,0:T(8,128)S(1)} %even.3), channel_id=2, replica_groups=mesh['outer'=16,'z'=16,'core'=2] {'core'}, dimensions={0}, use_global_device_ids=true | all-gather | bytes 1179648 | tf_op jit(solution)/shard_map/all_gather | solution.py:21
  17.2 1.4 %odd.4.refs_0_ = f32[192,512]{1,0:T(8,128)S(1)} custom-call(f32[2,192,512]{2,1,0:T(8,128)S(1)} %bitcast.10, bf16[2,512,1024]{2,1,0:T(8,128)(2,1)S(1)} %get-tuple-element.12.refs_1_.refs_3_.refs_4_, bf16[2,1024,512]{2,1,0:T(8,128)(2,1)S(1)} %get-tuple-element.13.refs_2_.refs_4_.refs_5_, f32[2,512]{1,0:T(2,128)S(1)} %get-tuple-element.14.refs_3_.refs_5_.refs_6_), custom_call_target="tpu_custom_call" | custom-call | flops 805306368 | bytes 9179136 | tf_op jit(solution)/shard_map/odd/pallas_call | solution.py:51
  18.7 1.3 %collective-permute-start.2 = (f32[192,512]{1,0:T(8,128)S(1)}, f32[192,512]{1,0:T(8,128)S(1)}, u32[]{:S(2)}, u32[]{:S(2)}) collective-permute-start(f32[192,512]{1,0:T(8,128)S(1)} %odd.4.refs_0_), channel_id=1, source_target_pairs={{1,2},{3,4},{5,6},{7,8},{9,10},{11,12},{13,14},{15,16},{17,18},{19... | collective-permute-start | bytes 1179656 | tf_op jit(solution)/shard_map/ppermute | solution.py:17
  20.0 0.0 collective-permute-done.1.refs_1_
  20.1 2.4 %all-gather.1 = f32[384,512]{1,0:T(8,128)S(1)} all-gather(f32[192,512]{1,0:T(8,128)S(1)} %even.4), channel_id=3, replica_groups=mesh['outer'=16,'z'=16,'core'=2] {'core'}, dimensions={0}, use_global_device_ids=true | all-gather | bytes 1179648 | tf_op jit(solution)/shard_map/all_gather | solution.py:21
  22.4 1.4 %odd.5.refs_0_ = f32[192,512]{1,0:T(8,128)S(1)} custom-call(f32[2,192,512]{2,1,0:T(8,128)S(1)} %bitcast.7, bf16[2,512,1024]{2,1,0:T(8,128)(2,1)S(1)} %get-tuple-element.12.refs_1_.refs_3_.refs_4_, bf16[2,1024,512]{2,1,0:T(8,128)(2,1)S(1)} %get-tuple-element.13.refs_2_.refs_4_.refs_5_, f32[2,512]{1,0:T(2,128)S(1)} %get-tuple-element.14.refs_3_.refs_5_.refs_6_), custom_call_target="tpu_custom_call" | custom-call | flops 805306368 | bytes 9179136 | tf_op jit(solution)/shard_map/odd/pallas_call | solution.py:51
  23.9 0.0 copy-start.2
  23.9 0.8 collective-permute-done.2.refs_1_
  24.7 0.0 copy-done
  24.7 0.0 copy-done.2
  24.7 2.4 %all-gather.2 = f32[384,512]{1,0:T(8,128)S(1)} all-gather(f32[192,512]{1,0:T(8,128)S(1)} %even.5), channel_id=4, replica_groups=mesh['outer'=16,'z'=16,'core'=2] {'core'}, dimensions={0}, use_global_device_ids=true | all-gather | bytes 1179648 | tf_op jit(solution)/shard_map/all_gather | solution.py:21
  27.1 0.1 part.1
  27.2 0.0 copy-start.3
  27.2 0.7 copy-done.3
  27.9 17.6 %all-to-all-start = ((f32[16,24,128]{2,1,0:T(8,128)}), f32[16,24,128]{2,1,0:T(8,128)S(1)}, u32[]{:S(2)}, u32[]{:S(2)}) async-start(f32[16,24,128]{2,1,0:T(8,128)} %copy-done.3), calls=%async_computation | async-start | bytes 393216 | tf_op jit(solution)/shard_map/all_to_all | solution.py:225
  45.5 4.8 %collective-permute-start.3 = (f32[192,512]{1,0:T(8,128)}, f32[192,512]{1,0:T(8,128)}, u32[]{:S(2)}, u32[]{:S(2)}) collective-permute-start(f32[192,512]{1,0:T(8,128)} %copy-done.2), channel_id=1, source_target_pairs={{1,2},{3,4},{5,6},{7,8},{9,10},{11,12},{13,14},{15,16},{17,18},{19... | collective-permute-start | bytes 1179656 | tf_op jit(solution)/shard_map/ppermute | solution.py:17
  50.3 8.1 %all-to-all-done.refs_0_ = f32[16,24,128]{2,1,0:T(8,128)S(1)} async-done(((f32[16,24,128]{2,1,0:T(8,128)}), f32[16,24,128]{2,1,0:T(8,128)S(1)}, u32[]{:S(2)}, u32[]{:S(2)}) %all-to-all-start) | async-done | bytes 196640 | tf_op jit(solution)/shard_map/all_to_all | solution.py:225
  58.4 0.7 own.1
  59.1 6.8 %all-to-all-start.1 = ((f32[16,32,128]{2,1,0:T(8,128)}), f32[16,32,128]{2,1,0:T(8,128)S(1)}, u32[]{:S(2)}, u32[]{:S(2)}) async-start(f32[16,32,128]{2,1,0:T(8,128)} %own.1), calls=%async_computation.1 | async-start | bytes 524288 | tf_op jit(solution)/shard_map/all_to_all | solution.py:232
  65.9 0.0 collective-permute-done.3.refs_2_
  65.9 7.5 %all-to-all-done.1.refs_0_ = f32[16,32,128]{2,1,0:T(8,128)S(1)} async-done(((f32[16,32,128]{2,1,0:T(8,128)}), f32[16,32,128]{2,1,0:T(8,128)S(1)}, u32[]{:S(2)}, u32[]{:S(2)}) %all-to-all-start.1) | async-done | bytes 262176 | tf_op jit(solution)/shard_map/all_to_all | solution.py:232
  73.4 0.0 copy-start.1
  73.4 0.1 scan.1
  73.5 25.9 %all_to_all.15 = f32[16,48,128]{2,1,0:T(8,128)S(1)} all-to-all(f32[16,48,128]{2,1,0:T(8,128)S(1)} %scan.1), channel_id=1, replica_groups=mesh['outer'=16,'z'=16,'core'=2] {'z'}, dimensions={0} | all-to-all | bytes 786432 | tf_op jit(solution)/shard_map/all_to_all | solution.py:234
  99.4 9.0 %all-gather.3 = f32[32,48,128]{2,1,0:T(8,128)S(1)} all-gather(f32[16,48,128]{2,1,0:T(8,128)S(1)} %all_to_all.15), channel_id=5, replica_groups=mesh['outer'=16,'z'=16,'core'=2] {'core'}, dimensions={0}, use_global_device_ids=true | all-gather | bytes 1179648 | tf_op jit(solution)/shard_map/all_gather | solution.py:21
  108.4 0.0 copy-done.1
  108.5 3.2 %last.1 = f32[1,192,512]{2,1,0:T(8,128)} custom-call(f32[2,16,48,128]{3,2,1,0:T(8,128)S(1)} %bitcast.9, f32[2,192,512]{2,1,0:T(8,128)S(1)} %bitcast.6, f32[192,512]{1,0:T(8,128)} %collective-permute-done.3.refs_2_, f32[192,512]{1,0:T(8,128)S(1)} %get-tuple-element.15.refs_2_.refs_3_, bf16[2,512,1024]{2,1,0:T(8,128)(2,1)S(1)} %get-tuple-element.12.refs_1_.refs_3_.refs_4_, ...), custom_call_target="tpu_custom_call" | custom-call | flops 805306368 | bytes 10752000 | tf_op jit(solution)/shard_map/last/pallas_call | solution.py:51
  (3 shorter events, 0.1 us)
Async XLA Ops:
  0.0 7.4 %copy-start.4 = (f32[1,192,512]{2,1,0:T(8,128)S(1)}, f32[1,192,512]{2,1,0:T(8,128)}, u32[]{:S(2)}) copy-start(f32[1,192,512]{2,1,0:T(8,128)} %param.7) | copy-start | bytes 1179652
  0.0 14.8 %collective-permute-start = (f32[192,512]{1,0:T(8,128)}, f32[192,512]{1,0:T(8,128)S(1)}, u32[]{:S(2)}, u32[]{:S(2)}) collective-permute-start(f32[192,512]{1,0:T(8,128)} %bitcast.11), channel_id=1, source_target_pairs={{1,2},{3,4},{5,6},{7,8},{9,10},{11,12},{13,14},{15,16},{17,18},{19... | collective-permute-start | bytes 1179656 | tf_op jit(solution)/shard_map/ppermute | solution.py:17
  7.4 17.3 %copy-start = (bf16[2,1024,512]{2,1,0:T(8,128)(2,1)}, bf16[2,1024,512]{2,1,0:T(8,128)(2,1)S(1)}, u32[]{:S(2)}) copy-start(bf16[2,1024,512]{2,1,0:T(8,128)(2,1)S(1)} %get-tuple-element.13.refs_2_.refs_4_.refs_5_) | copy-start | bytes 6291460
  13.5 6.5 %collective-permute-start.1 = (f32[192,512]{1,0:T(8,128)S(1)}, f32[192,512]{1,0:T(8,128)S(1)}, u32[]{:S(2)}, u32[]{:S(2)}) collective-permute-start(f32[192,512]{1,0:T(8,128)S(1)} %odd.3.refs_0_), channel_id=1, source_target_pairs={{1,2},{3,4},{5,6},{7,8},{9,10},{11,12},{13,14},{15,16},{17,18},{19... | collective-permute-start | bytes 1179656 | tf_op jit(solution)/shard_map/ppermute | solution.py:17
  18.7 6.0 %collective-permute-start.2 = (f32[192,512]{1,0:T(8,128)S(1)}, f32[192,512]{1,0:T(8,128)S(1)}, u32[]{:S(2)}, u32[]{:S(2)}) collective-permute-start(f32[192,512]{1,0:T(8,128)S(1)} %odd.4.refs_0_), channel_id=1, source_target_pairs={{1,2},{3,4},{5,6},{7,8},{9,10},{11,12},{13,14},{15,16},{17,18},{19... | collective-permute-start | bytes 1179656 | tf_op jit(solution)/shard_map/ppermute | solution.py:17
  23.9 0.8 copy-start.2
  27.2 0.7 copy-start.3
  27.9 30.5 %all-to-all-start = ((f32[16,24,128]{2,1,0:T(8,128)}), f32[16,24,128]{2,1,0:T(8,128)S(1)}, u32[]{:S(2)}, u32[]{:S(2)}) async-start(f32[16,24,128]{2,1,0:T(8,128)} %copy-done.3), calls=%async_computation | async-start | bytes 393216 | tf_op jit(solution)/shard_map/all_to_all | solution.py:225
  45.5 20.4 %collective-permute-start.3 = (f32[192,512]{1,0:T(8,128)}, f32[192,512]{1,0:T(8,128)}, u32[]{:S(2)}, u32[]{:S(2)}) collective-permute-start(f32[192,512]{1,0:T(8,128)} %copy-done.2), channel_id=1, source_target_pairs={{1,2},{3,4},{5,6},{7,8},{9,10},{11,12},{13,14},{15,16},{17,18},{19... | collective-permute-start | bytes 1179656 | tf_op jit(solution)/shard_map/ppermute | solution.py:17
  59.1 14.3 %all-to-all-start.1 = ((f32[16,32,128]{2,1,0:T(8,128)}), f32[16,32,128]{2,1,0:T(8,128)S(1)}, u32[]{:S(2)}, u32[]{:S(2)}) async-start(f32[16,32,128]{2,1,0:T(8,128)} %own.1), calls=%async_computation.1 | async-start | bytes 524288 | tf_op jit(solution)/shard_map/all_to_all | solution.py:232
  73.4 35.0 %copy-start.1 = (bf16[2,1024,512]{2,1,0:T(8,128)(2,1)S(1)}, bf16[2,1024,512]{2,1,0:T(8,128)(2,1)}, u32[]{:S(2)}) copy-start(bf16[2,1024,512]{2,1,0:T(8,128)(2,1)} %copy-done) | copy-start | bytes 6291460

commit v6 on v5

--- a/solution.py
+++ b/solution.py
@@ -12,9 +12,9 @@
 LANES = 128
 
 
-def from_odd(value):
+def from_odd(value, by=1):
     peers = lax.axis_size(ALL)
-    return lax.ppermute(value, ALL, [(i, i + 1) for i in range(1, peers - 1, 2)])
+    return lax.ppermute(value, ALL, [(i, i + by) for i in range(1, peers - by, 2)])
 
 
 def from_pair(value):
@@ -28,7 +28,7 @@
     return half + half * jnp.tanh(inner)
 
 
-def layers(state, weight_in, weight_out, norm_gain):
+def layers(state, weight_in, weight_out, norm_gain, arriving=None):
     for level in range(weight_in.shape[0]):
         meansq = jnp.mean(state * state, axis=-1, keepdims=True)
         normed = (state * lax.rsqrt(meansq + 1e-06) * norm_gain[level : level + 1, :]).astype(
@@ -36,30 +36,29 @@
         )
         hidden = jnp.dot(normed, weight_in[level], preferred_element_type=jnp.float32)
         hidden = gelu(hidden).astype(jnp.bfloat16)
+        if arriving:
+            arriving[level].wait()
         state = state + step_size * jnp.dot(
             hidden, weight_out[level], preferred_element_type=jnp.float32
         )
     return state
 
 
-def call(body, out_shape, args, name, flops=0, after=()):
-    count = len(args)
-
-    def with_after(*refs):
-        body(*refs[:count], refs[-1])
-
+def call(body, out_shape, args, name, flops=0, kind=None, far=(), scratch=()):
+    far = tuple(pltpu.with_memory_space_constraint(a, pltpu.HBM) for a in far)
     return pl.pallas_call(
-        with_after,
-        out_shape=jax.ShapeDtypeStruct(out_shape, jnp.float32),
-        in_specs=[pl.BlockSpec(memory_space=pltpu.VMEM)] * count
-        + [pl.BlockSpec(memory_space=pl.ANY)] * len(after),
+        body,
+        out_shape=(kind or jax.ShapeDtypeStruct)(out_shape, jnp.float32),
+        in_specs=[pl.BlockSpec(memory_space=pl.ANY)] * len(far)
+        + [pl.BlockSpec(memory_space=pltpu.VMEM)] * len(args),
         out_specs=pl.BlockSpec(memory_space=pltpu.VMEM),
+        scratch_shapes=scratch,
         compiler_params=pltpu.CompilerParams(vmem_limit_bytes=16 << 20),
         cost_estimate=pl.CostEstimate(
             flops=flops, bytes_accessed=sum(a.size * 4 for a in args), transcendentals=0
         ),
         name=name,
-    )(*args, *after)
+    )(*far, *args)
 
 
 def load_kernel(*refs):
@@ -175,7 +174,17 @@
         out[place, rows:, :] = current
 
 
-def last_kernel(both, pair, hop, start, weight_in, weight_out, norm_gain, out):
+def last_kernel(
+    far_weight, far_hop, both, pair, start, weight_in, norm_gain, out, weight_out, hop, sem
+):
+    levels = weight_out.shape[0]
+    copies = [pltpu.make_async_copy(far_hop.at[1], hop, sem.at[levels])]
+    for level in range(levels):
+        copies.append(
+            pltpu.make_async_copy(far_weight.at[level], weight_out.at[level], sem.at[level])
+        )
+    for copy in copies:
+        copy.start()
     cores, places = both.shape[:2]
     rows, lanes = both.shape[2] // 2, both.shape[3]
     count = places * cores
@@ -191,10 +200,11 @@
                 earlier, current = both[core, at, 0:rows, :], both[core, at, rows:, :]
                 pieces.append(weight * current + (1.0 - weight) * earlier)
             columns.append(jnp.concatenate(pieces, axis=0))
+    copies[0].wait()
     moved = jnp.where(is_odd(), pair[0], hop[...])
     state = moved + jnp.concatenate(columns, axis=1)
     state = jnp.where(is_first(), start[...], state)
-    out[0] = layers(state, weight_in, weight_out, norm_gain)
+    out[0] = layers(state, weight_in, weight_out, norm_gain, copies[1:])
 
 
 def per_device(start_state, guess, weight_in, weight_out, norm_gain, coarse_gain):
@@ -212,16 +222,16 @@
 
     pairs = [from_pair(guess[0])]
     hop = from_odd(guess[0])
-    for _ in range(3):
+    for by in (1, 1, 2):
         odd = block(odd_kernel, (pairs[-1],), "odd")
-        next_hop = from_odd(odd)
+        next_hop = from_odd(odd, by)
         state = block(even_kernel, (odd, hop, start_state), "even")
         pairs.append(from_pair(state))
         hop = next_hop
     second_pair, third_pair = pairs[2:]
 
     rows = tokens * width // LANES // places // cores
-    part = call(part_kernel, (places, rows, LANES), (third_pair, second_pair), "part")
+    part = call(part_kernel, (places, rows, LANES), (third_pair, second_pair), "part", 0, pltpu.HBM)
     parts = lax.all_to_all(part, "z", 0, 0, tiled=True)
     own = call(
         functools.partial(own_kernel, places * cores),
@@ -230,14 +240,21 @@
         "own",
     )
     heard, hop = lax.optimization_barrier((lax.all_to_all(own, "outer", 0, 0, tiled=True), hop))
-    both = call(scan_kernel, (places, 2 * rows, LANES), (heard,), "scan")
+    both = call(scan_kernel, (places, 2 * rows, LANES), (heard,), "scan", 0, pltpu.HBM)
     both = from_pair(lax.all_to_all(both, "z", 0, 0, tiled=True))
+    hop = from_pair(hop)
     return call(
         last_kernel,
         (1, tokens, width),
-        (both, third_pair, hop, start_state) + params,
+        (both, third_pair, start_state, params[0], params[2]),
         "last",
         flops,
+        far=(weight_out, hop),
+        scratch=[
+            pltpu.VMEM(weight_out.shape, weight_out.dtype),
+            pltpu.VMEM((tokens, width), jnp.float32),
+            pltpu.SemaphoreType.DMA((weight_out.shape[0] + 1,)),
+        ],
     )
 
 

time: 112 us -> 113 us (level)
  blocking collectives: 46.6 us -> 29.9 us
  waiting for transfers between devices: 16.4 us -> 25.5 us
  starting transfers between devices: 36.9 us -> 44.6 us
  Pallas kernels: 10.9 us -> 12.6 us
    all_to_all x1 -> x0, blocking collectives: 25.9 us -> none  [per_device(): both = from_pair(lax.all_to_all(both, 'z', 0, 0, tiled=True))]
    all_gather x5 -> x6, blocking collectives: 20.7 us -> 29.9 us  [from_pair(): return lax.all_gather(value, 'core', axis=0)]
    all_to_all x0 -> x1, starting transfers between devices: none -> 8.51 us  [per_device(): both = from_pair(lax.all_to_all(both, 'z', 0, 0, tiled=True))]
    all_to_all x0 -> x1, waiting for transfers between devices: none -> 8.25 us  [per_device(): both = from_pair(lax.all_to_all(both, 'z', 0, 0, tiled=True))]
    pallas_call x10, Pallas kernels: 8.57 us -> 10.3 us  [call(): pl.pallas_call(body, out_shape=(kind or jax.ShapeDtypeStruct)(out_shape,...]
  transfers between devices with their start and end apart: 6 -> 7, of which waited for: 3 -> 4; matrix products, arithmetic and copies ran while one was open for 0% -> 0% of each run, Pallas kernels for 7% -> 7%
where the time goes in v6:
time: 113 us
  starting transfers between devices  44.6 us (39%)
  blocking collectives  29.9 us (26%)
  waiting for transfers between devices  25.5 us (23%)
  Pallas kernels  12.6 us (11%)
    all_gather x6, blocking collectives, from_pair(): return lax.all_gather(value, 'core', axis=0)  29.9 us
    all_to_all x1, starting transfers between devices, per_device(): parts = lax.all_to_all(part, 'z', 0, 0, tiled=True)  17.6 us
    ppermute x4, starting transfers between devices, from_odd(): lax.ppermute(value, ALL, [(i, i + by) for i in range(1, peers - by, 2)])  11.7 us
    pallas_call x10, Pallas kernels, call(): pl.pallas_call(body, out_shape=(kind or jax.ShapeDtypeStruct)(out_shape,...  10.3 us
    all_to_all x1, waiting for transfers between devices, per_device(): parts = lax.all_to_all(part, 'z', 0, 0, tiled=True)  8.88 us
    all_to_all x1, starting transfers between devices, per_device(): both = from_pair(lax.all_to_all(both, 'z', 0, 0, tiled=True))  8.51 us
    all_to_all x1, waiting for transfers between devices, per_device(): both = from_pair(lax.all_to_all(both, 'z', 0, 0, tiled=True))  8.25 us
    all_to_all x1, waiting for transfers between devices, per_device(): lax.all_to_all(own, 'outer', 0, 0, tiled=True)  7.53 us
  transfers between devices with their start and end apart: 7, of which 4 were waited for; matrix products, arithmetic and copies ran while one was open for 0% of the time, Pallas kernels for 7%

profile of v6, /device:TPU:1, one launch (start us, length us, event | category | flops | bytes accessed | tf_op | source)
XLA Modules:
  0.0 112.7 jit_solution(14762856494255121117)
XLA Ops:
  0.0 0.0 copy-start.1
  0.0 5.1 %collective-permute-start = (f32[192,512]{1,0:T(8,128)}, f32[192,512]{1,0:T(8,128)S(1)}, u32[]{:S(2)}, u32[]{:S(2)}) collective-permute-start(f32[192,512]{1,0:T(8,128)} %bitcast.13), channel_id=1, source_target_pairs={{1,2},{3,4},{5,6},{7,8},{9,10},{11,12},{13,14},{15,16},{17,18},{19... | collective-permute-start | bytes 1179656 | tf_op jit(solution)/shard_map/ppermute | solution.py:17
  5.1 2.3 %load.1 = (bf16[2,512,1024]{2,1,0:T(8,128)(2,1)S(1)}, bf16[2,1024,512]{2,1,0:T(8,128)(2,1)S(1)}, f32[2,512]{1,0:T(2,128)S(1)}, f32[192,512]{1,0:T(8,128)S(1)}, f32[1,512]{1,0:T(1,128)S(1)}) custom-call(bf16[2,512,1024]{2,1,0:T(8,128)(2,1)} %refs_0_.1, bf16[2,1024,512]{2,1,0:T(8,128)(2,1)} %far_weight.1, f32[2,512]{1,0:T(2,128)} %refs_2_.1, ...), custom_call_target="tpu_custom_call" | custom-call | bytes 4593664 | tf_op jit(solution)/shard_map/load/pallas_call | solution.py:77
  7.4 0.0 copy-done.1
  7.4 4.6 %all_gather.33.pair = f32[2,192,512]{2,1,0:T(8,128)S(1)} all-gather(f32[1,192,512]{2,1,0:T(8,128)S(1)} %copy-done.1), channel_id=1, replica_groups=mesh['outer'=16,'z'=16,'core'=2] {'core'}, dimensions={0}, use_global_device_ids=true | all-gather | bytes 1179648 | tf_op jit(solution)/shard_map/all_gather | solution.py:21
  12.0 1.4 %odd.3 = f32[192,512]{1,0:T(8,128)S(1)} custom-call(f32[2,192,512]{2,1,0:T(8,128)S(1)} %all_gather.33.pair, bf16[2,512,1024]{2,1,0:T(8,128)(2,1)S(1)} %get-tuple-element.12.weight_in, bf16[2,1024,512]{2,1,0:T(8,128)(2,1)S(1)} %get-tuple-element.13.weight_out, f32[2,512]{1,0:T(2,128)S(1)} %get-tuple-element.14.norm_gain), custom_call_target="tpu_custom_call" | custom-call | flops 805306368 | bytes 9179136 | tf_op jit(solution)/shard_map/odd/pallas_call | solution.py:49
  13.5 1.3 %collective-permute-start.1 = (f32[192,512]{1,0:T(8,128)S(1)}, f32[192,512]{1,0:T(8,128)S(1)}, u32[]{:S(2)}, u32[]{:S(2)}) collective-permute-start(f32[192,512]{1,0:T(8,128)S(1)} %odd.3), channel_id=1, source_target_pairs={{1,2},{3,4},{5,6},{7,8},{9,10},{11,12},{13,14},{15,16},{17,18},{19... | collective-permute-start | bytes 1179656 | tf_op jit(solution)/shard_map/ppermute | solution.py:17
  14.8 0.0 collective-permute-done.hop
  14.9 2.4 %all-gather = f32[384,512]{1,0:T(8,128)S(1)} all-gather(f32[192,512]{1,0:T(8,128)S(1)} %even.3), channel_id=2, replica_groups=mesh['outer'=16,'z'=16,'core'=2] {'core'}, dimensions={0}, use_global_device_ids=true | all-gather | bytes 1179648 | tf_op jit(solution)/shard_map/all_gather | solution.py:21
  17.2 1.4 %odd.4 = f32[192,512]{1,0:T(8,128)S(1)} custom-call(f32[2,192,512]{2,1,0:T(8,128)S(1)} %bitcast.11, bf16[2,512,1024]{2,1,0:T(8,128)(2,1)S(1)} %get-tuple-element.12.weight_in, bf16[2,1024,512]{2,1,0:T(8,128)(2,1)S(1)} %get-tuple-element.13.weight_out, f32[2,512]{1,0:T(2,128)S(1)} %get-tuple-element.14.norm_gain), custom_call_target="tpu_custom_call" | custom-call | flops 805306368 | bytes 9179136 | tf_op jit(solution)/shard_map/odd/pallas_call | solution.py:49
  18.7 1.3 %collective-permute-start.2 = (f32[192,512]{1,0:T(8,128)S(1)}, f32[192,512]{1,0:T(8,128)S(1)}, u32[]{:S(2)}, u32[]{:S(2)}) collective-permute-start(f32[192,512]{1,0:T(8,128)S(1)} %odd.4), channel_id=1, source_target_pairs={{1,2},{3,4},{5,6},{7,8},{9,10},{11,12},{13,14},{15,16},{17,18},{19... | collective-permute-start | bytes 1179656 | tf_op jit(solution)/shard_map/ppermute | solution.py:17
  20.0 0.0 collective-permute-done.1.hop
  20.1 2.4 %all-gather.1 = f32[384,512]{1,0:T(8,128)S(1)} all-gather(f32[192,512]{1,0:T(8,128)S(1)} %even.4), channel_id=3, replica_groups=mesh['outer'=16,'z'=16,'core'=2] {'core'}, dimensions={0}, use_global_device_ids=true | all-gather | bytes 1179648 | tf_op jit(solution)/shard_map/all_gather | solution.py:21
  22.4 1.4 %odd.5 = f32[192,512]{1,0:T(8,128)S(1)} custom-call(f32[2,192,512]{2,1,0:T(8,128)S(1)} %bitcast.8, bf16[2,512,1024]{2,1,0:T(8,128)(2,1)S(1)} %get-tuple-element.12.weight_in, bf16[2,1024,512]{2,1,0:T(8,128)(2,1)S(1)} %get-tuple-element.13.weight_out, f32[2,512]{1,0:T(2,128)S(1)} %get-tuple-element.14.norm_gain), custom_call_target="tpu_custom_call" | custom-call | flops 805306368 | bytes 9179136 | tf_op jit(solution)/shard_map/odd/pallas_call | solution.py:49
  23.9 0.0 copy-start
  23.9 0.8 collective-permute-done.2.hop
  24.7 0.0 copy-done
  24.7 2.4 %all-gather.2 = f32[384,512]{1,0:T(8,128)S(1)} all-gather(f32[192,512]{1,0:T(8,128)S(1)} %even.5), channel_id=4, replica_groups=mesh['outer'=16,'z'=16,'core'=2] {'core'}, dimensions={0}, use_global_device_ids=true | all-gather | bytes 1179648 | tf_op jit(solution)/shard_map/all_gather | solution.py:21
  27.1 0.8 part.1
  27.8 17.6 %all-to-all-start = ((f32[16,24,128]{2,1,0:T(8,128)}), f32[16,24,128]{2,1,0:T(8,128)S(1)}, u32[]{:S(2)}, u32[]{:S(2)}) async-start(f32[16,24,128]{2,1,0:T(8,128)} %part.1), calls=%async_computation | async-start | bytes 393216 | tf_op jit(solution)/shard_map/all_to_all | solution.py:235
  45.5 4.0 %collective-permute-start.3 = (f32[192,512]{1,0:T(8,128)}, f32[192,512]{1,0:T(8,128)}, u32[]{:S(2)}, u32[]{:S(2)}) collective-permute-start(f32[192,512]{1,0:T(8,128)} %copy-done), channel_id=1, source_target_pairs={{1,3},{3,5},{5,7},{7,9},{9,11},{11,13},{13,15},{15,17},{17,19},{19... | collective-permute-start | bytes 1179656 | tf_op jit(solution)/shard_map/ppermute | solution.py:17
  49.5 8.9 %all-to-all-done.parts = f32[16,24,128]{2,1,0:T(8,128)S(1)} async-done(((f32[16,24,128]{2,1,0:T(8,128)}), f32[16,24,128]{2,1,0:T(8,128)S(1)}, u32[]{:S(2)}, u32[]{:S(2)}) %all-to-all-start) | async-done | bytes 196640 | tf_op jit(solution)/shard_map/all_to_all | solution.py:235
  58.4 0.7 own.1
  59.1 6.8 %all-to-all-start.1 = ((f32[16,32,128]{2,1,0:T(8,128)}), f32[16,32,128]{2,1,0:T(8,128)S(1)}, u32[]{:S(2)}, u32[]{:S(2)}) async-start(f32[16,32,128]{2,1,0:T(8,128)} %own.1), calls=%async_computation.1 | async-start | bytes 524288 | tf_op jit(solution)/shard_map/all_to_all | solution.py:242
  65.9 0.0 collective-permute-done.3
  65.9 7.5 %all-to-all-done.1.heard = f32[16,32,128]{2,1,0:T(8,128)S(1)} async-done(((f32[16,32,128]{2,1,0:T(8,128)}), f32[16,32,128]{2,1,0:T(8,128)S(1)}, u32[]{:S(2)}, u32[]{:S(2)}) %all-to-all-start.1) | async-done | bytes 262176 | tf_op jit(solution)/shard_map/all_to_all | solution.py:242
  73.5 0.8 scan.1
  74.3 8.5 %all-to-all-start.2 = ((f32[16,48,128]{2,1,0:T(8,128)}), f32[16,48,128]{2,1,0:T(8,128)}, u32[]{:S(2)}, u32[]{:S(2)}) async-start(f32[16,48,128]{2,1,0:T(8,128)} %scan.1), calls=%async_computation.2 | async-start | bytes 786432 | tf_op jit(solution)/shard_map/all_to_all | solution.py:244
  82.8 7.1 %all-gather.3 = f32[384,512]{1,0:T(8,128)} all-gather(f32[192,512]{1,0:T(8,128)} %collective-permute-done.3), channel_id=5, replica_groups=mesh['outer'=16,'z'=16,'core'=2] {'core'}, dimensions={0}, use_global_device_ids=true | all-gather | bytes 1179648 | tf_op jit(solution)/shard_map/all_gather | solution.py:21
  89.9 8.3 %all-to-all-done.2 = f32[16,48,128]{2,1,0:T(8,128)} async-done(((f32[16,48,128]{2,1,0:T(8,128)}), f32[16,48,128]{2,1,0:T(8,128)}, u32[]{:S(2)}, u32[]{:S(2)}) %all-to-all-start.2) | async-done | bytes 393248 | tf_op jit(solution)/shard_map/all_to_all | solution.py:244
  98.2 11.0 %all-gather.4 = f32[32,48,128]{2,1,0:T(8,128)S(1)} all-gather(f32[16,48,128]{2,1,0:T(8,128)} %all-to-all-done.2), channel_id=6, replica_groups=mesh['outer'=16,'z'=16,'core'=2] {'core'}, dimensions={0}, use_global_device_ids=true | all-gather | bytes 1179648 | tf_op jit(solution)/shard_map/all_gather | solution.py:21
  109.2 3.6 %last.1 = f32[1,192,512]{2,1,0:T(8,128)} custom-call(bf16[2,1024,512]{2,1,0:T(8,128)(2,1)} %far_weight.1, f32[2,192,512]{2,1,0:T(8,128)} %bitcast.12, f32[2,16,48,128]{3,2,1,0:T(8,128)S(1)} %bitcast.10, f32[2,192,512]{2,1,0:T(8,128)S(1)} %bitcast.7, f32[192,512]{1,0:T(8,128)S(1)} %get-tuple-element.15.start, ...), custom_call_target="tpu_custom_call" | custom-call | flops 805306368 | bytes 6164480 | tf_op jit(solution)/shard_map/last/pallas_call | solution.py:49
  (3 shorter events, 0.1 us)
Async XLA Ops:
  0.0 7.4 %copy-start.1 = (f32[1,192,512]{2,1,0:T(8,128)S(1)}, f32[1,192,512]{2,1,0:T(8,128)}, u32[]{:S(2)}) copy-start(f32[1,192,512]{2,1,0:T(8,128)} %param.7) | copy-start | bytes 1179652
  0.0 14.8 %collective-permute-start = (f32[192,512]{1,0:T(8,128)}, f32[192,512]{1,0:T(8,128)S(1)}, u32[]{:S(2)}, u32[]{:S(2)}) collective-permute-start(f32[192,512]{1,0:T(8,128)} %bitcast.13), channel_id=1, source_target_pairs={{1,2},{3,4},{5,6},{7,8},{9,10},{11,12},{13,14},{15,16},{17,18},{19... | collective-permute-start | bytes 1179656 | tf_op jit(solution)/shard_map/ppermute | solution.py:17
  13.5 6.5 %collective-permute-start.1 = (f32[192,512]{1,0:T(8,128)S(1)}, f32[192,512]{1,0:T(8,128)S(1)}, u32[]{:S(2)}, u32[]{:S(2)}) collective-permute-start(f32[192,512]{1,0:T(8,128)S(1)} %odd.3), channel_id=1, source_target_pairs={{1,2},{3,4},{5,6},{7,8},{9,10},{11,12},{13,14},{15,16},{17,18},{19... | collective-permute-start | bytes 1179656 | tf_op jit(solution)/shard_map/ppermute | solution.py:17
  18.7 6.0 %collective-permute-start.2 = (f32[192,512]{1,0:T(8,128)S(1)}, f32[192,512]{1,0:T(8,128)S(1)}, u32[]{:S(2)}, u32[]{:S(2)}) collective-permute-start(f32[192,512]{1,0:T(8,128)S(1)} %odd.4), channel_id=1, source_target_pairs={{1,2},{3,4},{5,6},{7,8},{9,10},{11,12},{13,14},{15,16},{17,18},{19... | collective-permute-start | bytes 1179656 | tf_op jit(solution)/shard_map/ppermute | solution.py:17
  23.9 0.8 copy-start
  27.8 30.5 %all-to-all-start = ((f32[16,24,128]{2,1,0:T(8,128)}), f32[16,24,128]{2,1,0:T(8,128)S(1)}, u32[]{:S(2)}, u32[]{:S(2)}) async-start(f32[16,24,128]{2,1,0:T(8,128)} %part.1), calls=%async_computation | async-start | bytes 393216 | tf_op jit(solution)/shard_map/all_to_all | solution.py:235
  45.5 20.4 %collective-permute-start.3 = (f32[192,512]{1,0:T(8,128)}, f32[192,512]{1,0:T(8,128)}, u32[]{:S(2)}, u32[]{:S(2)}) collective-permute-start(f32[192,512]{1,0:T(8,128)} %copy-done), channel_id=1, source_target_pairs={{1,3},{3,5},{5,7},{7,9},{9,11},{11,13},{13,15},{15,17},{17,19},{19... | collective-permute-start | bytes 1179656 | tf_op jit(solution)/shard_map/ppermute | solution.py:17
  59.1 14.3 %all-to-all-start.1 = ((f32[16,32,128]{2,1,0:T(8,128)}), f32[16,32,128]{2,1,0:T(8,128)S(1)}, u32[]{:S(2)}, u32[]{:S(2)}) async-start(f32[16,32,128]{2,1,0:T(8,128)} %own.1), calls=%async_computation.1 | async-start | bytes 524288 | tf_op jit(solution)/shard_map/all_to_all | solution.py:242
  74.3 23.9 %all-to-all-start.2 = ((f32[16,48,128]{2,1,0:T(8,128)}), f32[16,48,128]{2,1,0:T(8,128)}, u32[]{:S(2)}, u32[]{:S(2)}) async-start(f32[16,48,128]{2,1,0:T(8,128)} %scan.1), calls=%async_computation.2 | async-start | bytes 786432 | tf_op jit(solution)/shard_map/all_to_all | solution.py:244

commit v7 on v6

--- a/solution.py
+++ b/solution.py
@@ -8,13 +8,14 @@
 from jax.sharding import Mesh, PartitionSpec as P
 
 step_size = 0.5
-ALL = ("outer", "z", "core")
+ALL = ("outer", "far", "near", "core")
+PLACES = ("far", "near")
 LANES = 128
 
 
-def from_odd(value, by=1):
+def from_odd(value):
     peers = lax.axis_size(ALL)
-    return lax.ppermute(value, ALL, [(i, i + by) for i in range(1, peers - by, 2)])
+    return lax.ppermute(value, ALL, [(i, i + 1) for i in range(1, peers - 1, 2)])
 
 
 def from_pair(value):
@@ -44,11 +45,13 @@
     return state
 
 
-def call(body, out_shape, args, name, flops=0, kind=None, far=(), scratch=()):
+def call(
+    body, out_shape, args, name, flops=0, kind=jax.ShapeDtypeStruct, far=(), scratch=()
+):
     far = tuple(pltpu.with_memory_space_constraint(a, pltpu.HBM) for a in far)
     return pl.pallas_call(
         body,
-        out_shape=(kind or jax.ShapeDtypeStruct)(out_shape, jnp.float32),
+        out_shape=kind(out_shape, jnp.float32),
         in_specs=[pl.BlockSpec(memory_space=pl.ANY)] * len(far)
         + [pl.BlockSpec(memory_space=pltpu.VMEM)] * len(args),
         out_specs=pl.BlockSpec(memory_space=pltpu.VMEM),
@@ -139,7 +142,7 @@
 def gain_piece(gain, lanes):
     pieces = gain.shape[1] // lanes
     across = pieces // 2
-    place = lax.axis_index("core") * across + lax.rem(lax.axis_index("z"), across)
+    place = lax.axis_index("core") * across + lax.rem(lax.axis_index(PLACES), across)
     value = gain[:, 0:lanes]
     for at in range(1, pieces):
         value = jnp.where(place == at, gain[:, at * lanes : (at + 1) * lanes], value)
@@ -175,20 +178,20 @@
 
 
 def last_kernel(
-    far_weight, far_hop, both, pair, start, weight_in, norm_gain, out, weight_out, hop, sem
+    far_weight, both, pair, hop, start, weight_in, norm_gain, out, weight_out, arrived
 ):
-    levels = weight_out.shape[0]
-    copies = [pltpu.make_async_copy(far_hop.at[1], hop, sem.at[levels])]
-    for level in range(levels):
-        copies.append(
-            pltpu.make_async_copy(far_weight.at[level], weight_out.at[level], sem.at[level])
-        )
-    for copy in copies:
+    arriving = [
+        pltpu.make_async_copy(far_weight.at[level], weight_out.at[level], arrived.at[level])
+        for level in range(weight_out.shape[0])
+    ]
+    for copy in arriving:
         copy.start()
-    cores, places = both.shape[:2]
+    cores = pair.shape[0]
+    nears = both.shape[0] // cores
+    places = nears * both.shape[1]
     rows, lanes = both.shape[2] // 2, both.shape[3]
     count = places * cores
-    place = lax.axis_index("z") * cores + lax.axis_index("core")
+    place = lax.axis_index(PLACES) * cores + lax.axis_index("core")
     weight = place.astype(jnp.float32) / count
     across = hop.shape[1] // lanes // cores
     columns = []
@@ -197,19 +200,19 @@
             pieces = []
             for down in range(places // across):
                 at = down * across + side
-                earlier, current = both[core, at, 0:rows, :], both[core, at, rows:, :]
+                device, far = at % nears * cores + core, at // nears
+                earlier, current = both[device, far, 0:rows, :], both[device, far, rows:, :]
                 pieces.append(weight * current + (1.0 - weight) * earlier)
             columns.append(jnp.concatenate(pieces, axis=0))
-    copies[0].wait()
     moved = jnp.where(is_odd(), pair[0], hop[...])
     state = moved + jnp.concatenate(columns, axis=1)
     state = jnp.where(is_first(), start[...], state)
-    out[0] = layers(state, weight_in, weight_out, norm_gain, copies[1:])
+    out[0] = layers(state, weight_in, weight_out, norm_gain, arriving)
 
 
 def per_device(start_state, guess, weight_in, weight_out, norm_gain, coarse_gain):
     tokens, width = start_state.shape
-    places, groups = lax.axis_size("z"), lax.axis_size("outer")
+    places, groups = lax.axis_size(PLACES), lax.axis_size("outer")
     cores = lax.axis_size("core")
     *params, start_state, coarse_gain = loaded(
         (weight_in, weight_out, norm_gain, start_state, coarse_gain)
@@ -222,9 +225,9 @@
 
     pairs = [from_pair(guess[0])]
     hop = from_odd(guess[0])
-    for by in (1, 1, 2):
+    for _ in range(3):
         odd = block(odd_kernel, (pairs[-1],), "odd")
-        next_hop = from_odd(odd, by)
+        next_hop = from_odd(odd)
         state = block(even_kernel, (odd, hop, start_state), "even")
         pairs.append(from_pair(state))
         hop = next_hop
@@ -232,35 +235,37 @@
 
     rows = tokens * width // LANES // places // cores
     part = call(part_kernel, (places, rows, LANES), (third_pair, second_pair), "part", 0, pltpu.HBM)
-    parts = lax.all_to_all(part, "z", 0, 0, tiled=True)
+    parts = lax.all_to_all(part, PLACES, 0, 0, tiled=True)
     own = call(
         functools.partial(own_kernel, places * cores),
         (groups, rows + 8, LANES),
         (parts, coarse_gain),
         "own",
+        0,
+        pltpu.HBM,
     )
     heard, hop = lax.optimization_barrier((lax.all_to_all(own, "outer", 0, 0, tiled=True), hop))
-    both = call(scan_kernel, (places, 2 * rows, LANES), (heard,), "scan", 0, pltpu.HBM)
-    both = from_pair(lax.all_to_all(both, "z", 0, 0, tiled=True))
-    hop = from_pair(hop)
+    copies = lax.axis_size("far")
+    both = call(scan_kernel, (copies, 2 * rows, LANES), (heard,), "scan")
+    both = lax.all_to_all(both, "far", 0, 0, tiled=True)
+    both = lax.all_gather(both, ("near", "core"), axis=0)
     return call(
         last_kernel,
         (1, tokens, width),
-        (both, third_pair, start_state, params[0], params[2]),
+        (both, third_pair, hop, start_state, params[0], params[2]),
         "last",
         flops,
-        far=(weight_out, hop),
+        far=(weight_out,),
         scratch=[
             pltpu.VMEM(weight_out.shape, weight_out.dtype),
-            pltpu.VMEM((tokens, width), jnp.float32),
-            pltpu.SemaphoreType.DMA((weight_out.shape[0] + 1,)),
+            pltpu.SemaphoreType.DMA((weight_out.shape[0],)),
         ],
     )
 
 
 def solution(mesh):
     groups, inner = mesh.devices.shape
-    fine = Mesh(mesh.devices.reshape(groups, inner // 2, 2), ALL)
+    fine = Mesh(mesh.devices.reshape(groups, inner // 4, 2, 2), ALL)
     split = P(ALL, None, None)
     return jax.shard_map(
         per_device,

time: 113 us -> 113 us (level)
  blocking collectives: 29.9 us -> 46.4 us
  waiting for transfers between devices: 25.5 us -> 16.4 us
  starting transfers between devices: 44.6 us -> 36.9 us
    all_to_all x0 -> x1, blocking collectives: none -> 22.5 us  [per_device(): both = lax.all_to_all(both, 'far', 0, 0, tiled=True)]
    all_gather x6 -> x4, blocking collectives: 29.9 us -> 11.7 us  [from_pair(): return lax.all_gather(value, 'core', axis=0)]
    all_gather x0 -> x1, blocking collectives: none -> 12.2 us  [per_device(): both = lax.all_gather(both, ('near', 'core'), axis=0)]
    all_to_all x2 -> x1, waiting for transfers between devices: 17.1 us -> 8.07 us  [per_device(): parts = lax.all_to_all(part, PLACES, 0, 0, tiled=True)]
    all_to_all x2 -> x1, starting transfers between devices: 26.1 us -> 17.6 us  [per_device(): parts = lax.all_to_all(part, PLACES, 0, 0, tiled=True)]
  transfers between devices with their start and end apart: 7 -> 6, of which waited for: 4 -> 3; matrix products, arithmetic and copies ran while one was open for 0% -> 0% of each run, Pallas kernels for 7% -> 7%
where the time goes in v7:
time: 113 us; the launch traced here: 112 us
  blocking collectives  46.4 us (41%)
  starting transfers between devices  36.9 us (33%)
  waiting for transfers between devices  16.4 us (15%)
  Pallas kernels  12.5 us (11%)
    all_to_all x1, blocking collectives, per_device(): both = lax.all_to_all(both, 'far', 0, 0, tiled=True)  22.5 us
    all_to_all x1, starting transfers between devices, per_device(): parts = lax.all_to_all(part, PLACES, 0, 0, tiled=True)  17.6 us
    ppermute x4, starting transfers between devices, from_odd(): lax.ppermute(value, ALL, [(i, i + 1) for i in range(1, peers - 1, 2)])  12.5 us
    all_gather x1, blocking collectives, per_device(): both = lax.all_gather(both, ('near', 'core'), axis=0)  12.2 us
    all_gather x4, blocking collectives, from_pair(): return lax.all_gather(value, 'core', axis=0)  11.7 us
    pallas_call x10, Pallas kernels, call(): pl.pallas_call(body, out_shape=kind(out_shape, jnp.float32), in_specs=[pl...  10.2 us
    all_to_all x1, waiting for transfers between devices, per_device(): parts = lax.all_to_all(part, PLACES, 0, 0, tiled=True)  8.07 us
    all_to_all x1, waiting for transfers between devices, per_device(): lax.all_to_all(own, 'outer', 0, 0, tiled=True)  7.53 us
  transfers between devices with their start and end apart: 6, of which 3 were waited for; matrix products, arithmetic and copies ran while one was open for 0% of the time, Pallas kernels for 7%

profile of v7, /device:TPU:1, one launch (start us, length us, event | category | flops | bytes accessed | tf_op | source)
XLA Modules:
  0.0 112.4 jit_solution(5554066139802154475)
XLA Ops:
  0.0 0.0 copy-start.1
  0.0 5.1 %collective-permute-start = (f32[192,512]{1,0:T(8,128)}, f32[192,512]{1,0:T(8,128)S(1)}, u32[]{:S(2)}, u32[]{:S(2)}) collective-permute-start(f32[192,512]{1,0:T(8,128)} %bitcast.11), channel_id=1, source_target_pairs={{1,2},{3,4},{5,6},{7,8},{9,10},{11,12},{13,14},{15,16},{17,18},{19... | collective-permute-start | bytes 1179656 | tf_op jit(solution)/shard_map/ppermute | solution.py:18
  5.1 2.3 %load.1 = (bf16[2,512,1024]{2,1,0:T(8,128)(2,1)S(1)}, bf16[2,1024,512]{2,1,0:T(8,128)(2,1)S(1)}, f32[2,512]{1,0:T(2,128)S(1)}, f32[192,512]{1,0:T(8,128)S(1)}, f32[1,512]{1,0:T(1,128)S(1)}) custom-call(bf16[2,512,1024]{2,1,0:T(8,128)(2,1)} %refs_0_.1, bf16[2,1024,512]{2,1,0:T(8,128)(2,1)} %far_weight.1, f32[2,512]{1,0:T(2,128)} %refs_2_.1, ...), custom_call_target="tpu_custom_call" | custom-call | bytes 4593664 | tf_op jit(solution)/shard_map/load/pallas_call | solution.py:80
  7.4 0.0 copy-done.1
  7.4 4.6 %all_gather.27.pair = f32[2,192,512]{2,1,0:T(8,128)S(1)} all-gather(f32[1,192,512]{2,1,0:T(8,128)S(1)} %copy-done.1), channel_id=1, replica_groups=mesh['outer'=16,'far'=8,'near'=2,'core'=2] {'core'}, dimensions={0}, use_global_device_ids=true | all-gather | bytes 1179648 | tf_op jit(solution)/shard_map/all_gather | solution.py:22
  12.0 1.4 %odd.3 = f32[192,512]{1,0:T(8,128)S(1)} custom-call(f32[2,192,512]{2,1,0:T(8,128)S(1)} %all_gather.27.pair, bf16[2,512,1024]{2,1,0:T(8,128)(2,1)S(1)} %get-tuple-element.12.weight_in, bf16[2,1024,512]{2,1,0:T(8,128)(2,1)S(1)} %get-tuple-element.13.weight_out, f32[2,512]{1,0:T(2,128)S(1)} %get-tuple-element.14.norm_gain), custom_call_target="tpu_custom_call" | custom-call | flops 805306368 | bytes 9179136 | tf_op jit(solution)/shard_map/odd/pallas_call | solution.py:52
  13.5 1.3 %collective-permute-start.1 = (f32[192,512]{1,0:T(8,128)S(1)}, f32[192,512]{1,0:T(8,128)S(1)}, u32[]{:S(2)}, u32[]{:S(2)}) collective-permute-start(f32[192,512]{1,0:T(8,128)S(1)} %odd.3), channel_id=1, source_target_pairs={{1,2},{3,4},{5,6},{7,8},{9,10},{11,12},{13,14},{15,16},{17,18},{19... | collective-permute-start | bytes 1179656 | tf_op jit(solution)/shard_map/ppermute | solution.py:18
  14.8 0.0 collective-permute-done.hop
  14.9 2.4 %all-gather = f32[384,512]{1,0:T(8,128)S(1)} all-gather(f32[192,512]{1,0:T(8,128)S(1)} %even.3), channel_id=2, replica_groups=mesh['outer'=16,'far'=8,'near'=2,'core'=2] {'core'}, dimensions={0}, use_global_device_ids=true | all-gather | bytes 1179648 | tf_op jit(solution)/shard_map/all_gather | solution.py:22
  17.2 1.4 %odd.4 = f32[192,512]{1,0:T(8,128)S(1)} custom-call(f32[2,192,512]{2,1,0:T(8,128)S(1)} %bitcast.9, bf16[2,512,1024]{2,1,0:T(8,128)(2,1)S(1)} %get-tuple-element.12.weight_in, bf16[2,1024,512]{2,1,0:T(8,128)(2,1)S(1)} %get-tuple-element.13.weight_out, f32[2,512]{1,0:T(2,128)S(1)} %get-tuple-element.14.norm_gain), custom_call_target="tpu_custom_call" | custom-call | flops 805306368 | bytes 9179136 | tf_op jit(solution)/shard_map/odd/pallas_call | solution.py:52
  18.7 1.3 %collective-permute-start.2 = (f32[192,512]{1,0:T(8,128)S(1)}, f32[192,512]{1,0:T(8,128)S(1)}, u32[]{:S(2)}, u32[]{:S(2)}) collective-permute-start(f32[192,512]{1,0:T(8,128)S(1)} %odd.4), channel_id=1, source_target_pairs={{1,2},{3,4},{5,6},{7,8},{9,10},{11,12},{13,14},{15,16},{17,18},{19... | collective-permute-start | bytes 1179656 | tf_op jit(solution)/shard_map/ppermute | solution.py:18
  20.0 0.0 collective-permute-done.1.hop
  20.1 2.4 %all-gather.1 = f32[384,512]{1,0:T(8,128)S(1)} all-gather(f32[192,512]{1,0:T(8,128)S(1)} %even.4), channel_id=3, replica_groups=mesh['outer'=16,'far'=8,'near'=2,'core'=2] {'core'}, dimensions={0}, use_global_device_ids=true | all-gather | bytes 1179648 | tf_op jit(solution)/shard_map/all_gather | solution.py:22
  22.4 1.4 %odd.5 = f32[192,512]{1,0:T(8,128)S(1)} custom-call(f32[2,192,512]{2,1,0:T(8,128)S(1)} %bitcast.7, bf16[2,512,1024]{2,1,0:T(8,128)(2,1)S(1)} %get-tuple-element.12.weight_in, bf16[2,1024,512]{2,1,0:T(8,128)(2,1)S(1)} %get-tuple-element.13.weight_out, f32[2,512]{1,0:T(2,128)S(1)} %get-tuple-element.14.norm_gain), custom_call_target="tpu_custom_call" | custom-call | flops 805306368 | bytes 9179136 | tf_op jit(solution)/shard_map/odd/pallas_call | solution.py:52
  23.9 0.0 copy-start
  23.9 0.8 collective-permute-done.2.hop
  24.7 0.0 copy-done
  24.7 2.4 %all-gather.2 = f32[384,512]{1,0:T(8,128)S(1)} all-gather(f32[192,512]{1,0:T(8,128)S(1)} %even.5), channel_id=4, replica_groups=mesh['outer'=16,'far'=8,'near'=2,'core'=2] {'core'}, dimensions={0}, use_global_device_ids=true | all-gather | bytes 1179648 | tf_op jit(solution)/shard_map/all_gather | solution.py:22
  27.1 0.8 part.1
  27.8 17.6 %all-to-all-start = ((f32[16,24,128]{2,1,0:T(8,128)}), f32[16,24,128]{2,1,0:T(8,128)S(1)}, u32[]{:S(2)}, u32[]{:S(2)}) async-start(f32[16,24,128]{2,1,0:T(8,128)} %part.1), calls=%async_computation | async-start | bytes 393216 | tf_op jit(solution)/shard_map/all_to_all | solution.py:238
  45.5 4.8 %collective-permute-start.3 = (f32[192,512]{1,0:T(8,128)}, f32[192,512]{1,0:T(8,128)}, u32[]{:S(2)}, u32[]{:S(2)}) collective-permute-start(f32[192,512]{1,0:T(8,128)} %copy-done), channel_id=1, source_target_pairs={{1,2},{3,4},{5,6},{7,8},{9,10},{11,12},{13,14},{15,16},{17,18},{19... | collective-permute-start | bytes 1179656 | tf_op jit(solution)/shard_map/ppermute | solution.py:18
  50.3 8.1 %all-to-all-done.parts = f32[16,24,128]{2,1,0:T(8,128)S(1)} async-done(((f32[16,24,128]{2,1,0:T(8,128)}), f32[16,24,128]{2,1,0:T(8,128)S(1)}, u32[]{:S(2)}, u32[]{:S(2)}) %all-to-all-start) | async-done | bytes 196640 | tf_op jit(solution)/shard_map/all_to_all | solution.py:238
  58.4 0.7 own.1
  59.1 6.8 %all-to-all-start.1 = ((f32[16,32,128]{2,1,0:T(8,128)}), f32[16,32,128]{2,1,0:T(8,128)S(1)}, u32[]{:S(2)}, u32[]{:S(2)}) async-start(f32[16,32,128]{2,1,0:T(8,128)} %own.1), calls=%async_computation.1 | async-start | bytes 524288 | tf_op jit(solution)/shard_map/all_to_all | solution.py:247
  65.9 0.0 collective-permute-done.3.hop
  65.9 7.5 %all-to-all-done.1.heard = f32[16,32,128]{2,1,0:T(8,128)S(1)} async-done(((f32[16,32,128]{2,1,0:T(8,128)}), f32[16,32,128]{2,1,0:T(8,128)S(1)}, u32[]{:S(2)}, u32[]{:S(2)}) %all-to-all-start.1) | async-done | bytes 262176 | tf_op jit(solution)/shard_map/all_to_all | solution.py:247
  73.4 0.1 scan.1
  73.5 22.5 %all_to_all.15 = f32[8,48,128]{2,1,0:T(8,128)S(1)} all-to-all(f32[8,48,128]{2,1,0:T(8,128)S(1)} %scan.1), channel_id=1, replica_groups=mesh['outer'=16,'far'=8,'near'=2,'core'=2] {'far'}, dimensions={0} | all-to-all | bytes 393216 | tf_op jit(solution)/shard_map/all_to_all | solution.py:250
  96.0 12.2 %all-gather.3 = f32[32,48,128]{2,1,0:T(8,128)S(1)} all-gather(f32[8,48,128]{2,1,0:T(8,128)S(1)} %all_to_all.15), channel_id=5, replica_groups=mesh['outer'=16,'far'=8,'near'=2,'core'=2] {'near','core'}, dimensions={0}, use_global_device_ids=true | all-gather | bytes 983040 | tf_op jit(solution)/shard_map/all_gather | solution.py:251
  108.2 4.2 %last.1 = f32[1,192,512]{2,1,0:T(8,128)} custom-call(bf16[2,1024,512]{2,1,0:T(8,128)(2,1)} %far_weight.1, f32[4,8,48,128]{3,2,1,0:T(8,128)S(1)} %bitcast.10, f32[2,192,512]{2,1,0:T(8,128)S(1)} %bitcast.6, f32[192,512]{1,0:T(8,128)} %collective-permute-done.3.hop, f32[192,512]{1,0:T(8,128)S(1)} %get-tuple-element.15.start, ...), custom_call_target="tpu_custom_call" | custom-call | flops 805306368 | bytes 6557696 | tf_op jit(solution)/shard_map/last/pallas_call | solution.py:52
  (3 shorter events, 0.1 us)
Async XLA Ops:
  0.0 7.4 %copy-start.1 = (f32[1,192,512]{2,1,0:T(8,128)S(1)}, f32[1,192,512]{2,1,0:T(8,128)}, u32[]{:S(2)}) copy-start(f32[1,192,512]{2,1,0:T(8,128)} %param.7) | copy-start | bytes 1179652
  0.0 14.8 %collective-permute-start = (f32[192,512]{1,0:T(8,128)}, f32[192,512]{1,0:T(8,128)S(1)}, u32[]{:S(2)}, u32[]{:S(2)}) collective-permute-start(f32[192,512]{1,0:T(8,128)} %bitcast.11), channel_id=1, source_target_pairs={{1,2},{3,4},{5,6},{7,8},{9,10},{11,12},{13,14},{15,16},{17,18},{19... | collective-permute-start | bytes 1179656 | tf_op jit(solution)/shard_map/ppermute | solution.py:18
  13.5 6.5 %collective-permute-start.1 = (f32[192,512]{1,0:T(8,128)S(1)}, f32[192,512]{1,0:T(8,128)S(1)}, u32[]{:S(2)}, u32[]{:S(2)}) collective-permute-start(f32[192,512]{1,0:T(8,128)S(1)} %odd.3), channel_id=1, source_target_pairs={{1,2},{3,4},{5,6},{7,8},{9,10},{11,12},{13,14},{15,16},{17,18},{19... | collective-permute-start | bytes 1179656 | tf_op jit(solution)/shard_map/ppermute | solution.py:18
  18.7 6.0 %collective-permute-start.2 = (f32[192,512]{1,0:T(8,128)S(1)}, f32[192,512]{1,0:T(8,128)S(1)}, u32[]{:S(2)}, u32[]{:S(2)}) collective-permute-start(f32[192,512]{1,0:T(8,128)S(1)} %odd.4), channel_id=1, source_target_pairs={{1,2},{3,4},{5,6},{7,8},{9,10},{11,12},{13,14},{15,16},{17,18},{19... | collective-permute-start | bytes 1179656 | tf_op jit(solution)/shard_map/ppermute | solution.py:18
  23.9 0.8 copy-start
  27.8 30.5 %all-to-all-start = ((f32[16,24,128]{2,1,0:T(8,128)}), f32[16,24,128]{2,1,0:T(8,128)S(1)}, u32[]{:S(2)}, u32[]{:S(2)}) async-start(f32[16,24,128]{2,1,0:T(8,128)} %part.1), calls=%async_computation | async-start | bytes 393216 | tf_op jit(solution)/shard_map/all_to_all | solution.py:238
  45.5 20.4 %collective-permute-start.3 = (f32[192,512]{1,0:T(8,128)}, f32[192,512]{1,0:T(8,128)}, u32[]{:S(2)}, u32[]{:S(2)}) collective-permute-start(f32[192,512]{1,0:T(8,128)} %copy-done), channel_id=1, source_target_pairs={{1,2},{3,4},{5,6},{7,8},{9,10},{11,12},{13,14},{15,16},{17,18},{19... | collective-permute-start | bytes 1179656 | tf_op jit(solution)/shard_map/ppermute | solution.py:18
  59.1 14.3 %all-to-all-start.1 = ((f32[16,32,128]{2,1,0:T(8,128)}), f32[16,32,128]{2,1,0:T(8,128)S(1)}, u32[]{:S(2)}, u32[]{:S(2)}) async-start(f32[16,32,128]{2,1,0:T(8,128)} %own.1), calls=%async_computation.1 | async-start | bytes 524288 | tf_op jit(solution)/shard_map/all_to_all | solution.py:247

commit v8 on v7

--- a/solution.py
+++ b/solution.py
@@ -29,7 +29,7 @@
     return half + half * jnp.tanh(inner)
 
 
-def layers(state, weight_in, weight_out, norm_gain, arriving=None):
+def layers(state, weight_in, weight_out, norm_gain):
     for level in range(weight_in.shape[0]):
         meansq = jnp.mean(state * state, axis=-1, keepdims=True)
         normed = (state * lax.rsqrt(meansq + 1e-06) * norm_gain[level : level + 1, :]).astype(
@@ -37,8 +37,6 @@
         )
         hidden = jnp.dot(normed, weight_in[level], preferred_element_type=jnp.float32)
         hidden = gelu(hidden).astype(jnp.bfloat16)
-        if arriving:
-            arriving[level].wait()
         state = state + step_size * jnp.dot(
             hidden, weight_out[level], preferred_element_type=jnp.float32
         )
@@ -178,18 +176,13 @@
 
 
 def last_kernel(
-    far_weight, both, pair, hop, start, weight_in, norm_gain, out, weight_out, arrived
+    far_hop, both, pair, start, weight_in, weight_out, norm_gain, out, hop, arrived
 ):
-    arriving = [
-        pltpu.make_async_copy(far_weight.at[level], weight_out.at[level], arrived.at[level])
-        for level in range(weight_out.shape[0])
-    ]
-    for copy in arriving:
-        copy.start()
-    cores = pair.shape[0]
-    nears = both.shape[0] // cores
-    places = nears * both.shape[1]
-    rows, lanes = both.shape[2] // 2, both.shape[3]
+    arriving = pltpu.make_async_copy(far_hop, hop, arrived)
+    arriving.start()
+    cores, nears = both.shape[:2]
+    places = nears * both.shape[2]
+    rows, lanes = both.shape[3] // 2, both.shape[4]
     count = places * cores
     place = lax.axis_index(PLACES) * cores + lax.axis_index("core")
     weight = place.astype(jnp.float32) / count
@@ -200,14 +193,15 @@
             pieces = []
             for down in range(places // across):
                 at = down * across + side
-                device, far = at % nears * cores + core, at // nears
-                earlier, current = both[device, far, 0:rows, :], both[device, far, rows:, :]
+                near, far = at % nears, at // nears
+                earlier, current = both[core, near, far, 0:rows, :], both[core, near, far, rows:, :]
                 pieces.append(weight * current + (1.0 - weight) * earlier)
             columns.append(jnp.concatenate(pieces, axis=0))
+    arriving.wait()
     moved = jnp.where(is_odd(), pair[0], hop[...])
     state = moved + jnp.concatenate(columns, axis=1)
     state = jnp.where(is_first(), start[...], state)
-    out[0] = layers(state, weight_in, weight_out, norm_gain, arriving)
+    out[0] = layers(state, weight_in, weight_out, norm_gain)
 
 
 def per_device(start_state, guess, weight_in, weight_out, norm_gain, coarse_gain):
@@ -248,18 +242,15 @@
     copies = lax.axis_size("far")
     both = call(scan_kernel, (copies, 2 * rows, LANES), (heard,), "scan")
     both = lax.all_to_all(both, "far", 0, 0, tiled=True)
-    both = lax.all_gather(both, ("near", "core"), axis=0)
+    both = lax.all_gather(lax.all_gather(both, "near", axis=0), "core", axis=0)
     return call(
         last_kernel,
         (1, tokens, width),
-        (both, third_pair, hop, start_state, params[0], params[2]),
+        (both, third_pair, start_state) + params,
         "last",
         flops,
-        far=(weight_out,),
-        scratch=[
-            pltpu.VMEM(weight_out.shape, weight_out.dtype),
-            pltpu.SemaphoreType.DMA((weight_out.shape[0],)),
-        ],
+        far=(hop,),
+        scratch=[pltpu.VMEM(hop.shape, hop.dtype), pltpu.SemaphoreType.DMA(())],
     )
 
 

time: 113 us -> 113 us (level)
    all_gather x1 -> x2, blocking collectives: 12.2 us -> 13.2 us  [per_device(): both = lax.all_gather(lax.all_gather(both, 'near', axis=0), 'core', axis=0)]
where the time goes in v8:
time: 113 us; the launch traced here: 112 us
  blocking collectives  47.5 us (42%)
  starting transfers between devices  36.9 us (33%)
  waiting for transfers between devices  16.4 us (15%)
  Pallas kernels  11.5 us (10%)
    all_to_all x1, blocking collectives, per_device(): both = lax.all_to_all(both, 'far', 0, 0, tiled=True)  22.6 us
    all_to_all x1, starting transfers between devices, per_device(): parts = lax.all_to_all(part, PLACES, 0, 0, tiled=True)  17.6 us
    all_gather x2, blocking collectives, per_device(): both = lax.all_gather(lax.all_gather(both, 'near', axis=0), 'core', axis=0)  13.2 us
    ppermute x4, starting transfers between devices, from_odd(): lax.ppermute(value, ALL, [(i, i + 1) for i in range(1, peers - 1, 2)])  12.5 us
    all_gather x4, blocking collectives, from_pair(): return lax.all_gather(value, 'core', axis=0)  11.7 us
    pallas_call x10, Pallas kernels, call(): pl.pallas_call(body, out_shape=kind(out_shape, jnp.float32), in_specs=[pl...  9.2 us
    all_to_all x1, waiting for transfers between devices, per_device(): parts = lax.all_to_all(part, PLACES, 0, 0, tiled=True)  8.08 us
    all_to_all x1, waiting for transfers between devices, per_device(): lax.all_to_all(own, 'outer', 0, 0, tiled=True)  7.53 us
  transfers between devices with their start and end apart: 6, of which 3 were waited for; matrix products, arithmetic and copies ran while one was open for 0% of the time, Pallas kernels for 7%

profile of v8, /device:TPU:1, one launch (start us, length us, event | category | flops | bytes accessed | tf_op | source)
XLA Modules:
  0.0 112.5 jit_solution(15451706870616612164)
XLA Ops:
  0.0 0.0 copy-start.3
  0.0 5.1 %collective-permute-start = (f32[192,512]{1,0:T(8,128)}, f32[192,512]{1,0:T(8,128)S(1)}, u32[]{:S(2)}, u32[]{:S(2)}) collective-permute-start(f32[192,512]{1,0:T(8,128)} %bitcast.13), channel_id=1, source_target_pairs={{1,2},{3,4},{5,6},{7,8},{9,10},{11,12},{13,14},{15,16},{17,18},{19... | collective-permute-start | bytes 1179656 | tf_op jit(solution)/shard_map/ppermute | solution.py:18
  5.1 2.3 %load.1 = (bf16[2,512,1024]{2,1,0:T(8,128)(2,1)S(1)}, bf16[2,1024,512]{2,1,0:T(8,128)(2,1)S(1)}, f32[2,512]{1,0:T(2,128)S(1)}, f32[192,512]{1,0:T(8,128)S(1)}, f32[1,512]{1,0:T(1,128)S(1)}) custom-call(bf16[2,512,1024]{2,1,0:T(8,128)(2,1)} %refs_0_.1, bf16[2,1024,512]{2,1,0:T(8,128)(2,1)} %refs_1_.1, f32[2,512]{1,0:T(2,128)} %refs_2_.1, f32[192,512]{1,0:T(8,128)} %refs_3_.1, ...), custom_call_target="tpu_custom_call" | custom-call | bytes 4593664 | tf_op jit(solution)/shard_map/load/pallas_call | solution.py:78
  7.4 0.0 copy-done.3
  7.4 0.0 copy-start
  7.4 4.6 %all_gather.33.pair = f32[2,192,512]{2,1,0:T(8,128)S(1)} all-gather(f32[1,192,512]{2,1,0:T(8,128)S(1)} %copy-done.3), channel_id=1, replica_groups=mesh['outer'=16,'far'=8,'near'=2,'core'=2] {'core'}, dimensions={0}, use_global_device_ids=true | all-gather | bytes 1179648 | tf_op jit(solution)/shard_map/all_gather | solution.py:22
  12.0 1.4 %odd.3 = f32[192,512]{1,0:T(8,128)S(1)} custom-call(f32[2,192,512]{2,1,0:T(8,128)S(1)} %all_gather.33.pair, bf16[2,512,1024]{2,1,0:T(8,128)(2,1)S(1)} %get-tuple-element.12.weight_in, bf16[2,1024,512]{2,1,0:T(8,128)(2,1)S(1)} %get-tuple-element.13.weight_out, f32[2,512]{1,0:T(2,128)S(1)} %get-tuple-element.14.norm_gain), custom_call_target="tpu_custom_call" | custom-call | flops 805306368 | bytes 9179136 | tf_op jit(solution)/shard_map/odd/pallas_call | solution.py:50
  13.5 1.3 %collective-permute-start.1 = (f32[192,512]{1,0:T(8,128)S(1)}, f32[192,512]{1,0:T(8,128)S(1)}, u32[]{:S(2)}, u32[]{:S(2)}) collective-permute-start(f32[192,512]{1,0:T(8,128)S(1)} %odd.3), channel_id=1, source_target_pairs={{1,2},{3,4},{5,6},{7,8},{9,10},{11,12},{13,14},{15,16},{17,18},{19... | collective-permute-start | bytes 1179656 | tf_op jit(solution)/shard_map/ppermute | solution.py:18
  14.8 0.0 collective-permute-done.hop
  14.9 2.4 %all-gather = f32[384,512]{1,0:T(8,128)S(1)} all-gather(f32[192,512]{1,0:T(8,128)S(1)} %even.3), channel_id=2, replica_groups=mesh['outer'=16,'far'=8,'near'=2,'core'=2] {'core'}, dimensions={0}, use_global_device_ids=true | all-gather | bytes 1179648 | tf_op jit(solution)/shard_map/all_gather | solution.py:22
  17.2 1.4 %odd.4 = f32[192,512]{1,0:T(8,128)S(1)} custom-call(f32[2,192,512]{2,1,0:T(8,128)S(1)} %bitcast.11, bf16[2,512,1024]{2,1,0:T(8,128)(2,1)S(1)} %get-tuple-element.12.weight_in, bf16[2,1024,512]{2,1,0:T(8,128)(2,1)S(1)} %get-tuple-element.13.weight_out, f32[2,512]{1,0:T(2,128)S(1)} %get-tuple-element.14.norm_gain), custom_call_target="tpu_custom_call" | custom-call | flops 805306368 | bytes 9179136 | tf_op jit(solution)/shard_map/odd/pallas_call | solution.py:50
  18.7 1.3 %collective-permute-start.2 = (f32[192,512]{1,0:T(8,128)S(1)}, f32[192,512]{1,0:T(8,128)S(1)}, u32[]{:S(2)}, u32[]{:S(2)}) collective-permute-start(f32[192,512]{1,0:T(8,128)S(1)} %odd.4), channel_id=1, source_target_pairs={{1,2},{3,4},{5,6},{7,8},{9,10},{11,12},{13,14},{15,16},{17,18},{19... | collective-permute-start | bytes 1179656 | tf_op jit(solution)/shard_map/ppermute | solution.py:18
  20.0 0.0 collective-permute-done.1.hop
  20.1 2.4 %all-gather.1 = f32[384,512]{1,0:T(8,128)S(1)} all-gather(f32[192,512]{1,0:T(8,128)S(1)} %even.4), channel_id=3, replica_groups=mesh['outer'=16,'far'=8,'near'=2,'core'=2] {'core'}, dimensions={0}, use_global_device_ids=true | all-gather | bytes 1179648 | tf_op jit(solution)/shard_map/all_gather | solution.py:22
  22.4 1.4 %odd.5 = f32[192,512]{1,0:T(8,128)S(1)} custom-call(f32[2,192,512]{2,1,0:T(8,128)S(1)} %bitcast.8, bf16[2,512,1024]{2,1,0:T(8,128)(2,1)S(1)} %get-tuple-element.12.weight_in, bf16[2,1024,512]{2,1,0:T(8,128)(2,1)S(1)} %get-tuple-element.13.weight_out, f32[2,512]{1,0:T(2,128)S(1)} %get-tuple-element.14.norm_gain), custom_call_target="tpu_custom_call" | custom-call | flops 805306368 | bytes 9179136 | tf_op jit(solution)/shard_map/odd/pallas_call | solution.py:50
  23.9 0.0 copy-start.2
  23.9 0.8 collective-permute-done.2.hop
  24.7 0.0 copy-done
  24.7 0.0 copy-done.2
  24.7 2.4 %all-gather.2 = f32[384,512]{1,0:T(8,128)S(1)} all-gather(f32[192,512]{1,0:T(8,128)S(1)} %even.5), channel_id=4, replica_groups=mesh['outer'=16,'far'=8,'near'=2,'core'=2] {'core'}, dimensions={0}, use_global_device_ids=true | all-gather | bytes 1179648 | tf_op jit(solution)/shard_map/all_gather | solution.py:22
  27.1 0.8 part.1
  27.9 17.6 %all-to-all-start = ((f32[16,24,128]{2,1,0:T(8,128)}), f32[16,24,128]{2,1,0:T(8,128)S(1)}, u32[]{:S(2)}, u32[]{:S(2)}) async-start(f32[16,24,128]{2,1,0:T(8,128)} %part.1), calls=%async_computation | async-start | bytes 393216 | tf_op jit(solution)/shard_map/all_to_all | solution.py:232
  45.5 4.8 %collective-permute-start.3 = (f32[192,512]{1,0:T(8,128)}, f32[192,512]{1,0:T(8,128)}, u32[]{:S(2)}, u32[]{:S(2)}) collective-permute-start(f32[192,512]{1,0:T(8,128)} %copy-done.2), channel_id=1, source_target_pairs={{1,2},{3,4},{5,6},{7,8},{9,10},{11,12},{13,14},{15,16},{17,18},{19... | collective-permute-start | bytes 1179656 | tf_op jit(solution)/shard_map/ppermute | solution.py:18
  50.3 8.1 %all-to-all-done.parts = f32[16,24,128]{2,1,0:T(8,128)S(1)} async-done(((f32[16,24,128]{2,1,0:T(8,128)}), f32[16,24,128]{2,1,0:T(8,128)S(1)}, u32[]{:S(2)}, u32[]{:S(2)}) %all-to-all-start) | async-done | bytes 196640 | tf_op jit(solution)/shard_map/all_to_all | solution.py:232
  58.4 0.7 own.1
  59.1 6.8 %all-to-all-start.1 = ((f32[16,32,128]{2,1,0:T(8,128)}), f32[16,32,128]{2,1,0:T(8,128)S(1)}, u32[]{:S(2)}, u32[]{:S(2)}) async-start(f32[16,32,128]{2,1,0:T(8,128)} %own.1), calls=%async_computation.1 | async-start | bytes 524288 | tf_op jit(solution)/shard_map/all_to_all | solution.py:241
  65.9 0.0 collective-permute-done.3.far_hop
  65.9 7.5 %all-to-all-done.1.heard = f32[16,32,128]{2,1,0:T(8,128)S(1)} async-done(((f32[16,32,128]{2,1,0:T(8,128)}), f32[16,32,128]{2,1,0:T(8,128)S(1)}, u32[]{:S(2)}, u32[]{:S(2)}) %all-to-all-start.1) | async-done | bytes 262176 | tf_op jit(solution)/shard_map/all_to_all | solution.py:241
  73.4 0.0 copy-start.1
  73.4 0.1 scan.1
  73.5 22.6 %all_to_all.15 = f32[8,48,128]{2,1,0:T(8,128)S(1)} all-to-all(f32[8,48,128]{2,1,0:T(8,128)S(1)} %scan.1), channel_id=1, replica_groups=mesh['outer'=16,'far'=8,'near'=2,'core'=2] {'far'}, dimensions={0} | all-to-all | bytes 393216 | tf_op jit(solution)/shard_map/all_to_all | solution.py:244
  96.1 5.2 %all-gather.3 = f32[16,48,128]{2,1,0:T(8,128)S(1)} all-gather(f32[8,48,128]{2,1,0:T(8,128)S(1)} %all_to_all.15), channel_id=5, replica_groups=mesh['outer'=16,'far'=8,'near'=2,'core'=2] {'near'}, dimensions={0}, use_global_device_ids=true | all-gather | bytes 589824 | tf_op jit(solution)/shard_map/all_gather | solution.py:245
  101.3 8.0 %all-gather.4 = f32[4,8,48,128]{3,2,1,0:T(8,128)S(1)} all-gather(f32[2,8,48,128]{3,2,1,0:T(8,128)S(1)} %bitcast.12), channel_id=6, replica_groups=mesh['outer'=16,'far'=8,'near'=2,'core'=2] {'core'}, dimensions={0}, use_global_device_ids=true | all-gather | bytes 1179648 | tf_op jit(solution)/shard_map/all_gather | solution.py:245
  109.3 0.0 copy-done.1
  109.3 3.2 %last.1 = f32[1,192,512]{2,1,0:T(8,128)} custom-call(f32[192,512]{1,0:T(8,128)} %collective-permute-done.3.far_hop, f32[2,2,8,48,128]{4,3,2,1,0:T(8,128)S(1)} %bitcast.10, f32[2,192,512]{2,1,0:T(8,128)S(1)} %bitcast.7, f32[192,512]{1,0:T(8,128)S(1)} %get-tuple-element.15.start, bf16[2,512,1024]{2,1,0:T(8,128)(2,1)S(1)} %get-tuple-element.12.weight_in, ...), custom_call_target="tpu_custom_call" | custom-call | flops 805306368 | bytes 10358784 | tf_op jit(solution)/shard_map/last/pallas_call | solution.py:50
  (3 shorter events, 0.1 us)
Async XLA Ops:
  0.0 7.4 %copy-start.3 = (f32[1,192,512]{2,1,0:T(8,128)S(1)}, f32[1,192,512]{2,1,0:T(8,128)}, u32[]{:S(2)}) copy-start(f32[1,192,512]{2,1,0:T(8,128)} %param.7) | copy-start | bytes 1179652
  0.0 14.8 %collective-permute-start = (f32[192,512]{1,0:T(8,128)}, f32[192,512]{1,0:T(8,128)S(1)}, u32[]{:S(2)}, u32[]{:S(2)}) collective-permute-start(f32[192,512]{1,0:T(8,128)} %bitcast.13), channel_id=1, source_target_pairs={{1,2},{3,4},{5,6},{7,8},{9,10},{11,12},{13,14},{15,16},{17,18},{19... | collective-permute-start | bytes 1179656 | tf_op jit(solution)/shard_map/ppermute | solution.py:18
  7.4 17.3 %copy-start = (bf16[2,1024,512]{2,1,0:T(8,128)(2,1)}, bf16[2,1024,512]{2,1,0:T(8,128)(2,1)S(1)}, u32[]{:S(2)}) copy-start(bf16[2,1024,512]{2,1,0:T(8,128)(2,1)S(1)} %get-tuple-element.13.weight_out) | copy-start | bytes 6291460
  13.5 6.5 %collective-permute-start.1 = (f32[192,512]{1,0:T(8,128)S(1)}, f32[192,512]{1,0:T(8,128)S(1)}, u32[]{:S(2)}, u32[]{:S(2)}) collective-permute-start(f32[192,512]{1,0:T(8,128)S(1)} %odd.3), channel_id=1, source_target_pairs={{1,2},{3,4},{5,6},{7,8},{9,10},{11,12},{13,14},{15,16},{17,18},{19... | collective-permute-start | bytes 1179656 | tf_op jit(solution)/shard_map/ppermute | solution.py:18
  18.7 6.0 %collective-permute-start.2 = (f32[192,512]{1,0:T(8,128)S(1)}, f32[192,512]{1,0:T(8,128)S(1)}, u32[]{:S(2)}, u32[]{:S(2)}) collective-permute-start(f32[192,512]{1,0:T(8,128)S(1)} %odd.4), channel_id=1, source_target_pairs={{1,2},{3,4},{5,6},{7,8},{9,10},{11,12},{13,14},{15,16},{17,18},{19... | collective-permute-start | bytes 1179656 | tf_op jit(solution)/shard_map/ppermute | solution.py:18
  23.9 0.8 copy-start.2
  27.9 30.5 %all-to-all-start = ((f32[16,24,128]{2,1,0:T(8,128)}), f32[16,24,128]{2,1,0:T(8,128)S(1)}, u32[]{:S(2)}, u32[]{:S(2)}) async-start(f32[16,24,128]{2,1,0:T(8,128)} %part.1), calls=%async_computation | async-start | bytes 393216 | tf_op jit(solution)/shard_map/all_to_all | solution.py:232
  45.5 20.4 %collective-permute-start.3 = (f32[192,512]{1,0:T(8,128)}, f32[192,512]{1,0:T(8,128)}, u32[]{:S(2)}, u32[]{:S(2)}) collective-permute-start(f32[192,512]{1,0:T(8,128)} %copy-done.2), channel_id=1, source_target_pairs={{1,2},{3,4},{5,6},{7,8},{9,10},{11,12},{13,14},{15,16},{17,18},{19... | collective-permute-start | bytes 1179656 | tf_op jit(solution)/shard_map/ppermute | solution.py:18
  59.1 14.3 %all-to-all-start.1 = ((f32[16,32,128]{2,1,0:T(8,128)}), f32[16,32,128]{2,1,0:T(8,128)S(1)}, u32[]{:S(2)}, u32[]{:S(2)}) async-start(f32[16,32,128]{2,1,0:T(8,128)} %own.1), calls=%async_computation.1 | async-start | bytes 524288 | tf_op jit(solution)/shard_map/all_to_all | solution.py:241
  73.4 35.9 %copy-start.1 = (bf16[2,1024,512]{2,1,0:T(8,128)(2,1)S(1)}, bf16[2,1024,512]{2,1,0:T(8,128)(2,1)}, u32[]{:S(2)}) copy-start(bf16[2,1024,512]{2,1,0:T(8,128)(2,1)} %copy-done) | copy-start | bytes 6291460

commit v9 on v7

--- a/solution.py
+++ b/solution.py
@@ -177,15 +177,7 @@
         out[place, rows:, :] = current
 
 
-def last_kernel(
-    far_weight, both, pair, hop, start, weight_in, norm_gain, out, weight_out, arrived
-):
-    arriving = [
-        pltpu.make_async_copy(far_weight.at[level], weight_out.at[level], arrived.at[level])
-        for level in range(weight_out.shape[0])
-    ]
-    for copy in arriving:
-        copy.start()
+def last_kernel(both, pair, hop, start, weight_in, weight_out, norm_gain, out):
     cores = pair.shape[0]
     nears = both.shape[0] // cores
     places = nears * both.shape[1]
@@ -207,7 +199,7 @@
     moved = jnp.where(is_odd(), pair[0], hop[...])
     state = moved + jnp.concatenate(columns, axis=1)
     state = jnp.where(is_first(), start[...], state)
-    out[0] = layers(state, weight_in, weight_out, norm_gain, arriving)
+    out[0] = layers(state, weight_in, weight_out, norm_gain)
 
 
 def per_device(start_state, guess, weight_in, weight_out, norm_gain, coarse_gain):
@@ -246,20 +238,15 @@
     )
     heard, hop = lax.optimization_barrier((lax.all_to_all(own, "outer", 0, 0, tiled=True), hop))
     copies = lax.axis_size("far")
-    both = call(scan_kernel, (copies, 2 * rows, LANES), (heard,), "scan")
+    both = call(scan_kernel, (copies, 2 * rows, LANES), (heard,), "scan", 12 * flops)
     both = lax.all_to_all(both, "far", 0, 0, tiled=True)
     both = lax.all_gather(both, ("near", "core"), axis=0)
     return call(
         last_kernel,
         (1, tokens, width),
-        (both, third_pair, hop, start_state, params[0], params[2]),
+        (both, third_pair, hop, start_state) + params,
         "last",
         flops,
-        far=(weight_out,),
-        scratch=[
-            pltpu.VMEM(weight_out.shape, weight_out.dtype),
-            pltpu.SemaphoreType.DMA((weight_out.shape[0],)),
-        ],
     )
 
 

time: 113 us -> 112 us (level)
  no operation moved by 1% of the time
where the time goes in v9:
time: 112 us
  blocking collectives  46.5 us (42%)
  starting transfers between devices  36.9 us (33%)
  waiting for transfers between devices  16.4 us (15%)
  Pallas kernels  11.6 us (10%)
    all_to_all x1, blocking collectives, per_device(): both = lax.all_to_all(both, 'far', 0, 0, tiled=True)  22.6 us
    all_to_all x1, starting transfers between devices, per_device(): parts = lax.all_to_all(part, PLACES, 0, 0, tiled=True)  17.6 us
    ppermute x4, starting transfers between devices, from_odd(): lax.ppermute(value, ALL, [(i, i + 1) for i in range(1, peers - 1, 2)])  12.5 us
    all_gather x1, blocking collectives, per_device(): both = lax.all_gather(both, ('near', 'core'), axis=0)  12.2 us
    all_gather x4, blocking collectives, from_pair(): return lax.all_gather(value, 'core', axis=0)  11.7 us
    pallas_call x10, Pallas kernels, call(): pl.pallas_call(body, out_shape=kind(out_shape, jnp.float32), in_specs=[pl...  9.26 us
    all_to_all x1, waiting for transfers between devices, per_device(): parts = lax.all_to_all(part, PLACES, 0, 0, tiled=True)  8.08 us
    all_to_all x1, waiting for transfers between devices, per_device(): lax.all_to_all(own, 'outer', 0, 0, tiled=True)  7.53 us
  transfers between devices with their start and end apart: 6, of which 3 were waited for; matrix products, arithmetic and copies ran while one was open for 0% of the time, Pallas kernels for 7%

profile of v9, /device:TPU:1, one launch (start us, length us, event | category | flops | bytes accessed | tf_op | source)
XLA Modules:
  0.0 111.6 jit_solution(14564177852214172906)
XLA Ops:
  0.0 0.0 copy-start.3
  0.0 5.1 %collective-permute-start = (f32[192,512]{1,0:T(8,128)}, f32[192,512]{1,0:T(8,128)S(1)}, u32[]{:S(2)}, u32[]{:S(2)}) collective-permute-start(f32[192,512]{1,0:T(8,128)} %bitcast.11), channel_id=1, source_target_pairs={{1,2},{3,4},{5,6},{7,8},{9,10},{11,12},{13,14},{15,16},{17,18},{19... | collective-permute-start | bytes 1179656 | tf_op jit(solution)/shard_map/ppermute | solution.py:18
  5.1 2.3 %load.1 = (bf16[2,512,1024]{2,1,0:T(8,128)(2,1)S(1)}, bf16[2,1024,512]{2,1,0:T(8,128)(2,1)S(1)}, f32[2,512]{1,0:T(2,128)S(1)}, f32[192,512]{1,0:T(8,128)S(1)}, f32[1,512]{1,0:T(1,128)S(1)}) custom-call(bf16[2,512,1024]{2,1,0:T(8,128)(2,1)} %refs_0_.1, bf16[2,1024,512]{2,1,0:T(8,128)(2,1)} %refs_1_.1, f32[2,512]{1,0:T(2,128)} %refs_2_.1, f32[192,512]{1,0:T(8,128)} %refs_3_.1, ...), custom_call_target="tpu_custom_call" | custom-call | bytes 4593664 | tf_op jit(solution)/shard_map/load/pallas_call | solution.py:80
  7.4 0.0 copy-done.3
  7.4 0.0 copy-start
  7.4 4.6 %all_gather.27.pair = f32[2,192,512]{2,1,0:T(8,128)S(1)} all-gather(f32[1,192,512]{2,1,0:T(8,128)S(1)} %copy-done.3), channel_id=1, replica_groups=mesh['outer'=16,'far'=8,'near'=2,'core'=2] {'core'}, dimensions={0}, use_global_device_ids=true | all-gather | bytes 1179648 | tf_op jit(solution)/shard_map/all_gather | solution.py:22
  12.0 1.4 %odd.3 = f32[192,512]{1,0:T(8,128)S(1)} custom-call(f32[2,192,512]{2,1,0:T(8,128)S(1)} %all_gather.27.pair, bf16[2,512,1024]{2,1,0:T(8,128)(2,1)S(1)} %get-tuple-element.12.weight_in, bf16[2,1024,512]{2,1,0:T(8,128)(2,1)S(1)} %get-tuple-element.13.weight_out, f32[2,512]{1,0:T(2,128)S(1)} %get-tuple-element.14.norm_gain), custom_call_target="tpu_custom_call" | custom-call | flops 805306368 | bytes 9179136 | tf_op jit(solution)/shard_map/odd/pallas_call | solution.py:52
  13.5 1.3 %collective-permute-start.1 = (f32[192,512]{1,0:T(8,128)S(1)}, f32[192,512]{1,0:T(8,128)S(1)}, u32[]{:S(2)}, u32[]{:S(2)}) collective-permute-start(f32[192,512]{1,0:T(8,128)S(1)} %odd.3), channel_id=1, source_target_pairs={{1,2},{3,4},{5,6},{7,8},{9,10},{11,12},{13,14},{15,16},{17,18},{19... | collective-permute-start | bytes 1179656 | tf_op jit(solution)/shard_map/ppermute | solution.py:18
  14.8 0.0 collective-permute-done.hop
  14.9 2.4 %all-gather = f32[384,512]{1,0:T(8,128)S(1)} all-gather(f32[192,512]{1,0:T(8,128)S(1)} %even.3), channel_id=2, replica_groups=mesh['outer'=16,'far'=8,'near'=2,'core'=2] {'core'}, dimensions={0}, use_global_device_ids=true | all-gather | bytes 1179648 | tf_op jit(solution)/shard_map/all_gather | solution.py:22
  17.2 1.4 %odd.4 = f32[192,512]{1,0:T(8,128)S(1)} custom-call(f32[2,192,512]{2,1,0:T(8,128)S(1)} %bitcast.9, bf16[2,512,1024]{2,1,0:T(8,128)(2,1)S(1)} %get-tuple-element.12.weight_in, bf16[2,1024,512]{2,1,0:T(8,128)(2,1)S(1)} %get-tuple-element.13.weight_out, f32[2,512]{1,0:T(2,128)S(1)} %get-tuple-element.14.norm_gain), custom_call_target="tpu_custom_call" | custom-call | flops 805306368 | bytes 9179136 | tf_op jit(solution)/shard_map/odd/pallas_call | solution.py:52
  18.7 1.3 %collective-permute-start.2 = (f32[192,512]{1,0:T(8,128)S(1)}, f32[192,512]{1,0:T(8,128)S(1)}, u32[]{:S(2)}, u32[]{:S(2)}) collective-permute-start(f32[192,512]{1,0:T(8,128)S(1)} %odd.4), channel_id=1, source_target_pairs={{1,2},{3,4},{5,6},{7,8},{9,10},{11,12},{13,14},{15,16},{17,18},{19... | collective-permute-start | bytes 1179656 | tf_op jit(solution)/shard_map/ppermute | solution.py:18
  20.0 0.0 collective-permute-done.1.hop
  20.1 2.4 %all-gather.1 = f32[384,512]{1,0:T(8,128)S(1)} all-gather(f32[192,512]{1,0:T(8,128)S(1)} %even.4), channel_id=3, replica_groups=mesh['outer'=16,'far'=8,'near'=2,'core'=2] {'core'}, dimensions={0}, use_global_device_ids=true | all-gather | bytes 1179648 | tf_op jit(solution)/shard_map/all_gather | solution.py:22
  22.4 1.4 %odd.5 = f32[192,512]{1,0:T(8,128)S(1)} custom-call(f32[2,192,512]{2,1,0:T(8,128)S(1)} %bitcast.7, bf16[2,512,1024]{2,1,0:T(8,128)(2,1)S(1)} %get-tuple-element.12.weight_in, bf16[2,1024,512]{2,1,0:T(8,128)(2,1)S(1)} %get-tuple-element.13.weight_out, f32[2,512]{1,0:T(2,128)S(1)} %get-tuple-element.14.norm_gain), custom_call_target="tpu_custom_call" | custom-call | flops 805306368 | bytes 9179136 | tf_op jit(solution)/shard_map/odd/pallas_call | solution.py:52
  23.9 0.0 copy-start.2
  23.9 0.8 collective-permute-done.2.hop
  24.7 0.0 copy-done
  24.7 0.0 copy-done.2
  24.7 2.4 %all-gather.2 = f32[384,512]{1,0:T(8,128)S(1)} all-gather(f32[192,512]{1,0:T(8,128)S(1)} %even.5), channel_id=4, replica_groups=mesh['outer'=16,'far'=8,'near'=2,'core'=2] {'core'}, dimensions={0}, use_global_device_ids=true | all-gather | bytes 1179648 | tf_op jit(solution)/shard_map/all_gather | solution.py:22
  27.1 0.8 part.1
  27.9 17.6 %all-to-all-start = ((f32[16,24,128]{2,1,0:T(8,128)}), f32[16,24,128]{2,1,0:T(8,128)S(1)}, u32[]{:S(2)}, u32[]{:S(2)}) async-start(f32[16,24,128]{2,1,0:T(8,128)} %part.1), calls=%async_computation | async-start | bytes 393216 | tf_op jit(solution)/shard_map/all_to_all | solution.py:230
  45.5 4.8 %collective-permute-start.3 = (f32[192,512]{1,0:T(8,128)}, f32[192,512]{1,0:T(8,128)}, u32[]{:S(2)}, u32[]{:S(2)}) collective-permute-start(f32[192,512]{1,0:T(8,128)} %copy-done.2), channel_id=1, source_target_pairs={{1,2},{3,4},{5,6},{7,8},{9,10},{11,12},{13,14},{15,16},{17,18},{19... | collective-permute-start | bytes 1179656 | tf_op jit(solution)/shard_map/ppermute | solution.py:18
  50.3 8.1 %all-to-all-done.parts = f32[16,24,128]{2,1,0:T(8,128)S(1)} async-done(((f32[16,24,128]{2,1,0:T(8,128)}), f32[16,24,128]{2,1,0:T(8,128)S(1)}, u32[]{:S(2)}, u32[]{:S(2)}) %all-to-all-start) | async-done | bytes 196640 | tf_op jit(solution)/shard_map/all_to_all | solution.py:230
  58.4 0.7 own.1
  59.1 6.8 %all-to-all-start.1 = ((f32[16,32,128]{2,1,0:T(8,128)}), f32[16,32,128]{2,1,0:T(8,128)S(1)}, u32[]{:S(2)}, u32[]{:S(2)}) async-start(f32[16,32,128]{2,1,0:T(8,128)} %own.1), calls=%async_computation.1 | async-start | bytes 524288 | tf_op jit(solution)/shard_map/all_to_all | solution.py:239
  65.9 0.0 collective-permute-done.3.hop
  65.9 7.5 %all-to-all-done.1.heard = f32[16,32,128]{2,1,0:T(8,128)S(1)} async-done(((f32[16,32,128]{2,1,0:T(8,128)}), f32[16,32,128]{2,1,0:T(8,128)S(1)}, u32[]{:S(2)}, u32[]{:S(2)}) %all-to-all-start.1) | async-done | bytes 262176 | tf_op jit(solution)/shard_map/all_to_all | solution.py:239
  73.4 0.0 copy-start.1
  73.4 0.1 scan.1
  73.5 22.6 %all_to_all.15 = f32[8,48,128]{2,1,0:T(8,128)S(1)} all-to-all(f32[8,48,128]{2,1,0:T(8,128)S(1)} %scan.1), channel_id=1, replica_groups=mesh['outer'=16,'far'=8,'near'=2,'core'=2] {'far'}, dimensions={0} | all-to-all | bytes 393216 | tf_op jit(solution)/shard_map/all_to_all | solution.py:242
  96.1 12.2 %all-gather.3 = f32[32,48,128]{2,1,0:T(8,128)S(1)} all-gather(f32[8,48,128]{2,1,0:T(8,128)S(1)} %all_to_all.15), channel_id=5, replica_groups=mesh['outer'=16,'far'=8,'near'=2,'core'=2] {'near','core'}, dimensions={0}, use_global_device_ids=true | all-gather | bytes 983040 | tf_op jit(solution)/shard_map/all_gather | solution.py:243
  108.3 0.0 copy-done.1
  108.3 3.3 %last.1 = f32[1,192,512]{2,1,0:T(8,128)} custom-call(f32[4,8,48,128]{3,2,1,0:T(8,128)S(1)} %bitcast.10, f32[2,192,512]{2,1,0:T(8,128)S(1)} %bitcast.6, f32[192,512]{1,0:T(8,128)} %collective-permute-done.3.hop, f32[192,512]{1,0:T(8,128)S(1)} %get-tuple-element.15.start, bf16[2,512,1024]{2,1,0:T(8,128)(2,1)S(1)} %get-tuple-element.12.weight_in, ...), custom_call_target="tpu_custom_call" | custom-call | flops 805306368 | bytes 10752000 | tf_op jit(solution)/shard_map/last/pallas_call | solution.py:52
  (3 shorter events, 0.1 us)
Async XLA Ops:
  0.0 7.4 %copy-start.3 = (f32[1,192,512]{2,1,0:T(8,128)S(1)}, f32[1,192,512]{2,1,0:T(8,128)}, u32[]{:S(2)}) copy-start(f32[1,192,512]{2,1,0:T(8,128)} %param.7) | copy-start | bytes 1179652
  0.0 14.8 %collective-permute-start = (f32[192,512]{1,0:T(8,128)}, f32[192,512]{1,0:T(8,128)S(1)}, u32[]{:S(2)}, u32[]{:S(2)}) collective-permute-start(f32[192,512]{1,0:T(8,128)} %bitcast.11), channel_id=1, source_target_pairs={{1,2},{3,4},{5,6},{7,8},{9,10},{11,12},{13,14},{15,16},{17,18},{19... | collective-permute-start | bytes 1179656 | tf_op jit(solution)/shard_map/ppermute | solution.py:18
  7.4 17.3 %copy-start = (bf16[2,1024,512]{2,1,0:T(8,128)(2,1)}, bf16[2,1024,512]{2,1,0:T(8,128)(2,1)S(1)}, u32[]{:S(2)}) copy-start(bf16[2,1024,512]{2,1,0:T(8,128)(2,1)S(1)} %get-tuple-element.13.weight_out) | copy-start | bytes 6291460
  13.5 6.5 %collective-permute-start.1 = (f32[192,512]{1,0:T(8,128)S(1)}, f32[192,512]{1,0:T(8,128)S(1)}, u32[]{:S(2)}, u32[]{:S(2)}) collective-permute-start(f32[192,512]{1,0:T(8,128)S(1)} %odd.3), channel_id=1, source_target_pairs={{1,2},{3,4},{5,6},{7,8},{9,10},{11,12},{13,14},{15,16},{17,18},{19... | collective-permute-start | bytes 1179656 | tf_op jit(solution)/shard_map/ppermute | solution.py:18
  18.7 6.0 %collective-permute-start.2 = (f32[192,512]{1,0:T(8,128)S(1)}, f32[192,512]{1,0:T(8,128)S(1)}, u32[]{:S(2)}, u32[]{:S(2)}) collective-permute-start(f32[192,512]{1,0:T(8,128)S(1)} %odd.4), channel_id=1, source_target_pairs={{1,2},{3,4},{5,6},{7,8},{9,10},{11,12},{13,14},{15,16},{17,18},{19... | collective-permute-start | bytes 1179656 | tf_op jit(solution)/shard_map/ppermute | solution.py:18
  23.9 0.8 copy-start.2
  27.9 30.5 %all-to-all-start = ((f32[16,24,128]{2,1,0:T(8,128)}), f32[16,24,128]{2,1,0:T(8,128)S(1)}, u32[]{:S(2)}, u32[]{:S(2)}) async-start(f32[16,24,128]{2,1,0:T(8,128)} %part.1), calls=%async_computation | async-start | bytes 393216 | tf_op jit(solution)/shard_map/all_to_all | solution.py:230
  45.5 20.4 %collective-permute-start.3 = (f32[192,512]{1,0:T(8,128)}, f32[192,512]{1,0:T(8,128)}, u32[]{:S(2)}, u32[]{:S(2)}) collective-permute-start(f32[192,512]{1,0:T(8,128)} %copy-done.2), channel_id=1, source_target_pairs={{1,2},{3,4},{5,6},{7,8},{9,10},{11,12},{13,14},{15,16},{17,18},{19... | collective-permute-start | bytes 1179656 | tf_op jit(solution)/shard_map/ppermute | solution.py:18
  59.1 14.3 %all-to-all-start.1 = ((f32[16,32,128]{2,1,0:T(8,128)}), f32[16,32,128]{2,1,0:T(8,128)S(1)}, u32[]{:S(2)}, u32[]{:S(2)}) async-start(f32[16,32,128]{2,1,0:T(8,128)} %own.1), calls=%async_computation.1 | async-start | bytes 524288 | tf_op jit(solution)/shard_map/all_to_all | solution.py:239
  73.4 34.9 %copy-start.1 = (bf16[2,1024,512]{2,1,0:T(8,128)(2,1)S(1)}, bf16[2,1024,512]{2,1,0:T(8,128)(2,1)}, u32[]{:S(2)}) copy-start(bf16[2,1024,512]{2,1,0:T(8,128)(2,1)} %copy-done) | copy-start | bytes 6291460

commit v10 on v9

--- a/solution.py
+++ b/solution.py
@@ -149,6 +149,10 @@
     return value
 
 
+def moved_kernel(pair, hop, out):
+    out[...] = jnp.where(is_odd(), pair[0], hop[...])
+
+
 def own_kernel(count, parts, gain, out):
     places, rows, lanes = parts.shape
     own = parts[0]
@@ -177,15 +181,15 @@
         out[place, rows:, :] = current
 
 
-def last_kernel(both, pair, hop, start, weight_in, weight_out, norm_gain, out):
-    cores = pair.shape[0]
+def last_kernel(both, moved, start, weight_in, weight_out, norm_gain, out):
+    cores = 2
     nears = both.shape[0] // cores
     places = nears * both.shape[1]
     rows, lanes = both.shape[2] // 2, both.shape[3]
     count = places * cores
     place = lax.axis_index(PLACES) * cores + lax.axis_index("core")
     weight = place.astype(jnp.float32) / count
-    across = hop.shape[1] // lanes // cores
+    across = moved.shape[1] // lanes // cores
     columns = []
     for core in range(cores):
         for side in range(across):
@@ -196,8 +200,7 @@
                 earlier, current = both[device, far, 0:rows, :], both[device, far, rows:, :]
                 pieces.append(weight * current + (1.0 - weight) * earlier)
             columns.append(jnp.concatenate(pieces, axis=0))
-    moved = jnp.where(is_odd(), pair[0], hop[...])
-    state = moved + jnp.concatenate(columns, axis=1)
+    state = moved[...] + jnp.concatenate(columns, axis=1)
     state = jnp.where(is_first(), start[...], state)
     out[0] = layers(state, weight_in, weight_out, norm_gain)
 
@@ -236,7 +239,9 @@
         0,
         pltpu.HBM,
     )
-    heard, hop = lax.optimization_barrier((lax.all_to_all(own, "outer", 0, 0, tiled=True), hop))
+    moved = call(moved_kernel, (tokens, width), (third_pair, hop), "moved")
+    heard = lax.all_to_all(own, "outer", 0, 0, tiled=True)
+    heard, moved = lax.optimization_barrier((heard, moved))
     copies = lax.axis_size("far")
     both = call(scan_kernel, (copies, 2 * rows, LANES), (heard,), "scan", 12 * flops)
     both = lax.all_to_all(both, "far", 0, 0, tiled=True)
@@ -244,7 +249,7 @@
     return call(
         last_kernel,
         (1, tokens, width),
-        (both, third_pair, hop, start_state) + params,
+        (both, moved, start_state) + params,
         "last",
         flops,
     )

time: 112 us -> 111 us (level)
  waiting for transfers between devices: 16.4 us -> 14.6 us
    all_to_all x1, waiting for transfers between devices: 7.53 us -> 5.74 us  [per_device(): heard = lax.all_to_all(own, 'outer', 0, 0, tiled=True)]
    pallas_call x10 -> x11, Pallas kernels: 9.26 us -> 9.27 us  [call(): pl.pallas_call(body, out_shape=kind(out_shape, jnp.float32), in_specs=[pl...]
  transfers between devices with their start and end apart: 6 -> 6, of which waited for: 3 -> 3; matrix products, arithmetic and copies ran while one was open for 0% -> 0% of each run, Pallas kernels for 7% -> 8%
where the time goes in v10:
time: 111 us
  blocking collectives  46.5 us (42%)
  starting transfers between devices  36.9 us (33%)
  waiting for transfers between devices  14.6 us (13%)
  Pallas kernels  11.6 us (10%)
    all_to_all x1, blocking collectives, per_device(): both = lax.all_to_all(both, 'far', 0, 0, tiled=True)  22.6 us
    all_to_all x1, starting transfers between devices, per_device(): parts = lax.all_to_all(part, PLACES, 0, 0, tiled=True)  17.6 us
    ppermute x4, starting transfers between devices, from_odd(): lax.ppermute(value, ALL, [(i, i + 1) for i in range(1, peers - 1, 2)])  12.5 us
    all_gather x1, blocking collectives, per_device(): both = lax.all_gather(both, ('near', 'core'), axis=0)  12.2 us
    all_gather x4, blocking collectives, from_pair(): return lax.all_gather(value, 'core', axis=0)  11.7 us
    pallas_call x11, Pallas kernels, call(): pl.pallas_call(body, out_shape=kind(out_shape, jnp.float32), in_specs=[pl...  9.27 us
    all_to_all x1, waiting for transfers between devices, per_device(): parts = lax.all_to_all(part, PLACES, 0, 0, tiled=True)  8.07 us
    all_to_all x1, starting transfers between devices, per_device(): heard = lax.all_to_all(own, 'outer', 0, 0, tiled=True)  6.75 us
  transfers between devices with their start and end apart: 6, of which 3 were waited for; matrix products, arithmetic and copies ran while one was open for 0% of the time, Pallas kernels for 8%

profile of v10, /device:TPU:1, one launch (start us, length us, event | category | flops | bytes accessed | tf_op | source)
XLA Modules:
  0.0 110.5 jit_solution(9335590519852949426)
XLA Ops:
  0.0 0.0 copy-start.5
  0.0 5.1 %collective-permute-start = (f32[192,512]{1,0:T(8,128)}, f32[192,512]{1,0:T(8,128)S(1)}, u32[]{:S(2)}, u32[]{:S(2)}) collective-permute-start(f32[192,512]{1,0:T(8,128)} %bitcast.11), channel_id=1, source_target_pairs={{1,2},{3,4},{5,6},{7,8},{9,10},{11,12},{13,14},{15,16},{17,18},{19... | collective-permute-start | bytes 1179656 | tf_op jit(solution)/shard_map/ppermute | solution.py:18
  5.1 2.3 %load.1 = (bf16[2,512,1024]{2,1,0:T(8,128)(2,1)S(1)}, bf16[2,1024,512]{2,1,0:T(8,128)(2,1)S(1)}, f32[2,512]{1,0:T(2,128)S(1)}, f32[192,512]{1,0:T(8,128)S(1)}, f32[1,512]{1,0:T(1,128)S(1)}) custom-call(bf16[2,512,1024]{2,1,0:T(8,128)(2,1)} %refs_0_.1, bf16[2,1024,512]{2,1,0:T(8,128)(2,1)} %refs_1_.1, f32[2,512]{1,0:T(2,128)} %refs_2_.1, f32[192,512]{1,0:T(8,128)} %refs_3_.1, ...), custom_call_target="tpu_custom_call" | custom-call | bytes 4593664 | tf_op jit(solution)/shard_map/load/pallas_call | solution.py:80
  7.4 0.0 copy-done.5
  7.4 0.0 copy-start
  7.4 4.6 %all_gather.27.pair = f32[2,192,512]{2,1,0:T(8,128)S(1)} all-gather(f32[1,192,512]{2,1,0:T(8,128)S(1)} %copy-done.5), channel_id=1, replica_groups=mesh['outer'=16,'far'=8,'near'=2,'core'=2] {'core'}, dimensions={0}, use_global_device_ids=true | all-gather | bytes 1179648 | tf_op jit(solution)/shard_map/all_gather | solution.py:22
  12.0 1.4 %odd.3 = f32[192,512]{1,0:T(8,128)S(1)} custom-call(f32[2,192,512]{2,1,0:T(8,128)S(1)} %all_gather.27.pair, bf16[2,512,1024]{2,1,0:T(8,128)(2,1)S(1)} %get-tuple-element.12.weight_in, bf16[2,1024,512]{2,1,0:T(8,128)(2,1)S(1)} %get-tuple-element.13.weight_out, f32[2,512]{1,0:T(2,128)S(1)} %get-tuple-element.14.norm_gain), custom_call_target="tpu_custom_call" | custom-call | flops 805306368 | bytes 9179136 | tf_op jit(solution)/shard_map/odd/pallas_call | solution.py:52
  13.5 1.3 %collective-permute-start.1 = (f32[192,512]{1,0:T(8,128)S(1)}, f32[192,512]{1,0:T(8,128)S(1)}, u32[]{:S(2)}, u32[]{:S(2)}) collective-permute-start(f32[192,512]{1,0:T(8,128)S(1)} %odd.3), channel_id=1, source_target_pairs={{1,2},{3,4},{5,6},{7,8},{9,10},{11,12},{13,14},{15,16},{17,18},{19... | collective-permute-start | bytes 1179656 | tf_op jit(solution)/shard_map/ppermute | solution.py:18
  14.8 0.0 collective-permute-done.hop
  14.9 2.4 %all-gather = f32[384,512]{1,0:T(8,128)S(1)} all-gather(f32[192,512]{1,0:T(8,128)S(1)} %even.3), channel_id=2, replica_groups=mesh['outer'=16,'far'=8,'near'=2,'core'=2] {'core'}, dimensions={0}, use_global_device_ids=true | all-gather | bytes 1179648 | tf_op jit(solution)/shard_map/all_gather | solution.py:22
  17.2 1.4 %odd.4 = f32[192,512]{1,0:T(8,128)S(1)} custom-call(f32[2,192,512]{2,1,0:T(8,128)S(1)} %bitcast.9, bf16[2,512,1024]{2,1,0:T(8,128)(2,1)S(1)} %get-tuple-element.12.weight_in, bf16[2,1024,512]{2,1,0:T(8,128)(2,1)S(1)} %get-tuple-element.13.weight_out, f32[2,512]{1,0:T(2,128)S(1)} %get-tuple-element.14.norm_gain), custom_call_target="tpu_custom_call" | custom-call | flops 805306368 | bytes 9179136 | tf_op jit(solution)/shard_map/odd/pallas_call | solution.py:52
  18.7 1.3 %collective-permute-start.2 = (f32[192,512]{1,0:T(8,128)S(1)}, f32[192,512]{1,0:T(8,128)S(1)}, u32[]{:S(2)}, u32[]{:S(2)}) collective-permute-start(f32[192,512]{1,0:T(8,128)S(1)} %odd.4), channel_id=1, source_target_pairs={{1,2},{3,4},{5,6},{7,8},{9,10},{11,12},{13,14},{15,16},{17,18},{19... | collective-permute-start | bytes 1179656 | tf_op jit(solution)/shard_map/ppermute | solution.py:18
  20.0 0.0 collective-permute-done.1.hop
  20.1 2.4 %all-gather.1 = f32[384,512]{1,0:T(8,128)S(1)} all-gather(f32[192,512]{1,0:T(8,128)S(1)} %even.4), channel_id=3, replica_groups=mesh['outer'=16,'far'=8,'near'=2,'core'=2] {'core'}, dimensions={0}, use_global_device_ids=true | all-gather | bytes 1179648 | tf_op jit(solution)/shard_map/all_gather | solution.py:22
  22.4 1.4 %odd.5 = f32[192,512]{1,0:T(8,128)S(1)} custom-call(f32[2,192,512]{2,1,0:T(8,128)S(1)} %bitcast.5, bf16[2,512,1024]{2,1,0:T(8,128)(2,1)S(1)} %get-tuple-element.12.weight_in, bf16[2,1024,512]{2,1,0:T(8,128)(2,1)S(1)} %get-tuple-element.13.weight_out, f32[2,512]{1,0:T(2,128)S(1)} %get-tuple-element.14.norm_gain), custom_call_target="tpu_custom_call" | custom-call | flops 805306368 | bytes 9179136 | tf_op jit(solution)/shard_map/odd/pallas_call | solution.py:52
  23.9 0.0 copy-start.2
  23.9 0.8 collective-permute-done.2.hop
  24.7 0.0 copy-done
  24.7 0.0 copy-done.2
  24.7 2.4 %all-gather.2 = f32[384,512]{1,0:T(8,128)S(1)} all-gather(f32[192,512]{1,0:T(8,128)S(1)} %even.5), channel_id=4, replica_groups=mesh['outer'=16,'far'=8,'near'=2,'core'=2] {'core'}, dimensions={0}, use_global_device_ids=true | all-gather | bytes 1179648 | tf_op jit(solution)/shard_map/all_gather | solution.py:22
  27.1 0.8 part.1
  27.9 17.6 %all-to-all-start = ((f32[16,24,128]{2,1,0:T(8,128)}), f32[16,24,128]{2,1,0:T(8,128)S(1)}, u32[]{:S(2)}, u32[]{:S(2)}) async-start(f32[16,24,128]{2,1,0:T(8,128)} %part.1), calls=%async_computation | async-start | bytes 393216 | tf_op jit(solution)/shard_map/all_to_all | solution.py:233
  45.4 4.8 %collective-permute-start.3 = (f32[192,512]{1,0:T(8,128)}, f32[192,512]{1,0:T(8,128)}, u32[]{:S(2)}, u32[]{:S(2)}) collective-permute-start(f32[192,512]{1,0:T(8,128)} %copy-done.2), channel_id=1, source_target_pairs={{1,2},{3,4},{5,6},{7,8},{9,10},{11,12},{13,14},{15,16},{17,18},{19... | collective-permute-start | bytes 1179656 | tf_op jit(solution)/shard_map/ppermute | solution.py:18
  50.3 8.1 %all-to-all-done.parts = f32[16,24,128]{2,1,0:T(8,128)S(1)} async-done(((f32[16,24,128]{2,1,0:T(8,128)}), f32[16,24,128]{2,1,0:T(8,128)S(1)}, u32[]{:S(2)}, u32[]{:S(2)}) %all-to-all-start) | async-done | bytes 196640 | tf_op jit(solution)/shard_map/all_to_all | solution.py:233
  58.3 0.7 own.1
  59.1 6.8 %all-to-all-start.1 = ((f32[16,32,128]{2,1,0:T(8,128)}), f32[16,32,128]{2,1,0:T(8,128)S(1)}, u32[]{:S(2)}, u32[]{:S(2)}) async-start(f32[16,32,128]{2,1,0:T(8,128)} %own.1), calls=%async_computation.1 | async-start | bytes 524288 | tf_op jit(solution)/shard_map/all_to_all | solution.py:243
  65.8 0.0 collective-permute-done.3.hop
  65.9 1.0 moved.1
  66.9 0.0 copy-start.3
  66.9 0.7 copy-done.3
  67.7 5.7 %all-to-all-done.1.heard = f32[16,32,128]{2,1,0:T(8,128)S(1)} async-done(((f32[16,32,128]{2,1,0:T(8,128)}), f32[16,32,128]{2,1,0:T(8,128)S(1)}, u32[]{:S(2)}, u32[]{:S(2)}) %all-to-all-start.1) | async-done | bytes 262176 | tf_op jit(solution)/shard_map/all_to_all | solution.py:243
  73.4 0.0 copy-start.1
  73.4 0.0 copy-start.4
  73.4 0.1 scan.1
  73.4 22.6 %all_to_all.15 = f32[8,48,128]{2,1,0:T(8,128)S(1)} all-to-all(f32[8,48,128]{2,1,0:T(8,128)S(1)} %scan.1), channel_id=1, replica_groups=mesh['outer'=16,'far'=8,'near'=2,'core'=2] {'far'}, dimensions={0} | all-to-all | bytes 393216 | tf_op jit(solution)/shard_map/all_to_all | solution.py:247
  96.1 12.2 %all-gather.3 = f32[32,48,128]{2,1,0:T(8,128)S(1)} all-gather(f32[8,48,128]{2,1,0:T(8,128)S(1)} %all_to_all.15), channel_id=5, replica_groups=mesh['outer'=16,'far'=8,'near'=2,'core'=2] {'near','core'}, dimensions={0}, use_global_device_ids=true | all-gather | bytes 983040 | tf_op jit(solution)/shard_map/all_gather | solution.py:248
  108.3 0.0 copy-done.1
  108.3 0.0 copy-done.4
  108.3 2.3 %last.1 = f32[1,192,512]{2,1,0:T(8,128)} custom-call(f32[4,8,48,128]{3,2,1,0:T(8,128)S(1)} %bitcast.10, f32[192,512]{1,0:T(8,128)S(1)} %copy-done.4, f32[192,512]{1,0:T(8,128)S(1)} %get-tuple-element.15.start, bf16[2,512,1024]{2,1,0:T(8,128)(2,1)S(1)} %get-tuple-element.12.weight_in, bf16[2,1024,512]{2,1,0:T(8,128)(2,1)S(1)} %copy-done.1, ...), custom_call_target="tpu_custom_call" | custom-call | flops 805306368 | bytes 9965568 | tf_op jit(solution)/shard_map/last/pallas_call | solution.py:52
  (3 shorter events, 0.1 us)
Async XLA Ops:
  0.0 7.4 %copy-start.5 = (f32[1,192,512]{2,1,0:T(8,128)S(1)}, f32[1,192,512]{2,1,0:T(8,128)}, u32[]{:S(2)}) copy-start(f32[1,192,512]{2,1,0:T(8,128)} %param.7) | copy-start | bytes 1179652
  0.0 14.8 %collective-permute-start = (f32[192,512]{1,0:T(8,128)}, f32[192,512]{1,0:T(8,128)S(1)}, u32[]{:S(2)}, u32[]{:S(2)}) collective-permute-start(f32[192,512]{1,0:T(8,128)} %bitcast.11), channel_id=1, source_target_pairs={{1,2},{3,4},{5,6},{7,8},{9,10},{11,12},{13,14},{15,16},{17,18},{19... | collective-permute-start | bytes 1179656 | tf_op jit(solution)/shard_map/ppermute | solution.py:18
  7.4 17.3 %copy-start = (bf16[2,1024,512]{2,1,0:T(8,128)(2,1)}, bf16[2,1024,512]{2,1,0:T(8,128)(2,1)S(1)}, u32[]{:S(2)}) copy-start(bf16[2,1024,512]{2,1,0:T(8,128)(2,1)S(1)} %get-tuple-element.13.weight_out) | copy-start | bytes 6291460
  13.5 6.5 %collective-permute-start.1 = (f32[192,512]{1,0:T(8,128)S(1)}, f32[192,512]{1,0:T(8,128)S(1)}, u32[]{:S(2)}, u32[]{:S(2)}) collective-permute-start(f32[192,512]{1,0:T(8,128)S(1)} %odd.3), channel_id=1, source_target_pairs={{1,2},{3,4},{5,6},{7,8},{9,10},{11,12},{13,14},{15,16},{17,18},{19... | collective-permute-start | bytes 1179656 | tf_op jit(solution)/shard_map/ppermute | solution.py:18
  18.7 6.0 %collective-permute-start.2 = (f32[192,512]{1,0:T(8,128)S(1)}, f32[192,512]{1,0:T(8,128)S(1)}, u32[]{:S(2)}, u32[]{:S(2)}) collective-permute-start(f32[192,512]{1,0:T(8,128)S(1)} %odd.4), channel_id=1, source_target_pairs={{1,2},{3,4},{5,6},{7,8},{9,10},{11,12},{13,14},{15,16},{17,18},{19... | collective-permute-start | bytes 1179656 | tf_op jit(solution)/shard_map/ppermute | solution.py:18
  23.9 0.8 copy-start.2
  27.9 30.5 %all-to-all-start = ((f32[16,24,128]{2,1,0:T(8,128)}), f32[16,24,128]{2,1,0:T(8,128)S(1)}, u32[]{:S(2)}, u32[]{:S(2)}) async-start(f32[16,24,128]{2,1,0:T(8,128)} %part.1), calls=%async_computation | async-start | bytes 393216 | tf_op jit(solution)/shard_map/all_to_all | solution.py:233
  45.4 20.4 %collective-permute-start.3 = (f32[192,512]{1,0:T(8,128)}, f32[192,512]{1,0:T(8,128)}, u32[]{:S(2)}, u32[]{:S(2)}) collective-permute-start(f32[192,512]{1,0:T(8,128)} %copy-done.2), channel_id=1, source_target_pairs={{1,2},{3,4},{5,6},{7,8},{9,10},{11,12},{13,14},{15,16},{17,18},{19... | collective-permute-start | bytes 1179656 | tf_op jit(solution)/shard_map/ppermute | solution.py:18
  59.1 14.3 %all-to-all-start.1 = ((f32[16,32,128]{2,1,0:T(8,128)}), f32[16,32,128]{2,1,0:T(8,128)S(1)}, u32[]{:S(2)}, u32[]{:S(2)}) async-start(f32[16,32,128]{2,1,0:T(8,128)} %own.1), calls=%async_computation.1 | async-start | bytes 524288 | tf_op jit(solution)/shard_map/all_to_all | solution.py:243
  66.9 0.7 copy-start.3
  73.4 34.9 %copy-start.1 = (bf16[2,1024,512]{2,1,0:T(8,128)(2,1)S(1)}, bf16[2,1024,512]{2,1,0:T(8,128)(2,1)}, u32[]{:S(2)}) copy-start(bf16[2,1024,512]{2,1,0:T(8,128)(2,1)} %copy-done) | copy-start | bytes 6291460
  73.4 34.9 %copy-start.4 = (f32[192,512]{1,0:T(8,128)S(1)}, f32[192,512]{1,0:T(8,128)}, u32[]{:S(2)}) copy-start(f32[192,512]{1,0:T(8,128)} %copy-done.3) | copy-start | bytes 1179652

commit v11 on v10

--- a/solution.py
+++ b/solution.py
@@ -149,8 +149,9 @@
     return value
 
 
-def moved_kernel(pair, hop, out):
-    out[...] = jnp.where(is_odd(), pair[0], hop[...])
+def moved_kernel(pair, hop, start, out):
+    even = jnp.where(is_first(), start[...], hop[...])
+    out[...] = jnp.where(is_odd(), pair[0], even)
 
 
 def own_kernel(count, parts, gain, out):
@@ -181,7 +182,7 @@
         out[place, rows:, :] = current
 
 
-def last_kernel(both, moved, start, weight_in, weight_out, norm_gain, out):
+def last_kernel(both, moved, weight_in, weight_out, norm_gain, out):
     cores = 2
     nears = both.shape[0] // cores
     places = nears * both.shape[1]
@@ -201,7 +202,6 @@
                 pieces.append(weight * current + (1.0 - weight) * earlier)
             columns.append(jnp.concatenate(pieces, axis=0))
     state = moved[...] + jnp.concatenate(columns, axis=1)
-    state = jnp.where(is_first(), start[...], state)
     out[0] = layers(state, weight_in, weight_out, norm_gain)
 
 
@@ -239,7 +239,7 @@
         0,
         pltpu.HBM,
     )
-    moved = call(moved_kernel, (tokens, width), (third_pair, hop), "moved")
+    moved = call(moved_kernel, (tokens, width), (third_pair, hop, start_state), "moved")
     heard = lax.all_to_all(own, "outer", 0, 0, tiled=True)
     heard, moved = lax.optimization_barrier((heard, moved))
     copies = lax.axis_size("far")
@@ -249,7 +249,7 @@
     return call(
         last_kernel,
         (1, tokens, width),
-        (both, moved, start_state) + params,
+        (both, moved) + params,
         "last",
         flops,
     )

time: 111 us -> 111 us (level)
  no operation moved by 1% of the time
where the time goes in v11:
time: 111 us
  blocking collectives  46.5 us (42%)
  starting transfers between devices  36.9 us (33%)
  waiting for transfers between devices  14.6 us (13%)
  Pallas kernels  11.6 us (10%)
    all_to_all x1, blocking collectives, per_device(): both = lax.all_to_all(both, 'far', 0, 0, tiled=True)  22.6 us
    all_to_all x1, starting transfers between devices, per_device(): parts = lax.all_to_all(part, PLACES, 0, 0, tiled=True)  17.6 us
    ppermute x4, starting transfers between devices, from_odd(): lax.ppermute(value, ALL, [(i, i + 1) for i in range(1, peers - 1, 2)])  12.5 us
    all_gather x1, blocking collectives, per_device(): both = lax.all_gather(both, ('near', 'core'), axis=0)  12.2 us
    all_gather x4, blocking collectives, from_pair(): return lax.all_gather(value, 'core', axis=0)  11.7 us
    pallas_call x11, Pallas kernels, call(): pl.pallas_call(body, out_shape=kind(out_shape, jnp.float32), in_specs=[pl...  9.26 us
    all_to_all x1, waiting for transfers between devices, per_device(): parts = lax.all_to_all(part, PLACES, 0, 0, tiled=True)  8.07 us
    all_to_all x1, starting transfers between devices, per_device(): heard = lax.all_to_all(own, 'outer', 0, 0, tiled=True)  6.75 us
  transfers between devices with their start and end apart: 6, of which 3 were waited for; matrix products, arithmetic and copies ran while one was open for 0% of the time, Pallas kernels for 8%

profile of v11, /device:TPU:1, one launch (start us, length us, event | category | flops | bytes accessed | tf_op | source)
XLA Modules:
  0.0 110.5 jit_solution(17637818839648788210)
XLA Ops:
  0.0 0.0 copy-start.5
  0.0 5.1 %collective-permute-start = (f32[192,512]{1,0:T(8,128)}, f32[192,512]{1,0:T(8,128)S(1)}, u32[]{:S(2)}, u32[]{:S(2)}) collective-permute-start(f32[192,512]{1,0:T(8,128)} %bitcast.11), channel_id=1, source_target_pairs={{1,2},{3,4},{5,6},{7,8},{9,10},{11,12},{13,14},{15,16},{17,18},{19... | collective-permute-start | bytes 1179656 | tf_op jit(solution)/shard_map/ppermute | solution.py:18
  5.1 2.3 %load.1 = (bf16[2,512,1024]{2,1,0:T(8,128)(2,1)S(1)}, bf16[2,1024,512]{2,1,0:T(8,128)(2,1)S(1)}, f32[2,512]{1,0:T(2,128)S(1)}, f32[192,512]{1,0:T(8,128)S(1)}, f32[1,512]{1,0:T(1,128)S(1)}) custom-call(bf16[2,512,1024]{2,1,0:T(8,128)(2,1)} %refs_0_.1, bf16[2,1024,512]{2,1,0:T(8,128)(2,1)} %refs_1_.1, f32[2,512]{1,0:T(2,128)} %refs_2_.1, f32[192,512]{1,0:T(8,128)} %refs_3_.1, ...), custom_call_target="tpu_custom_call" | custom-call | bytes 4593664 | tf_op jit(solution)/shard_map/load/pallas_call | solution.py:80
  7.4 0.0 copy-done.5
  7.4 0.0 copy-start
  7.4 4.6 %all_gather.27.pair = f32[2,192,512]{2,1,0:T(8,128)S(1)} all-gather(f32[1,192,512]{2,1,0:T(8,128)S(1)} %copy-done.5), channel_id=1, replica_groups=mesh['outer'=16,'far'=8,'near'=2,'core'=2] {'core'}, dimensions={0}, use_global_device_ids=true | all-gather | bytes 1179648 | tf_op jit(solution)/shard_map/all_gather | solution.py:22
  12.0 1.4 %odd.3 = f32[192,512]{1,0:T(8,128)S(1)} custom-call(f32[2,192,512]{2,1,0:T(8,128)S(1)} %all_gather.27.pair, bf16[2,512,1024]{2,1,0:T(8,128)(2,1)S(1)} %get-tuple-element.12.weight_in, bf16[2,1024,512]{2,1,0:T(8,128)(2,1)S(1)} %get-tuple-element.13.weight_out, f32[2,512]{1,0:T(2,128)S(1)} %get-tuple-element.14.norm_gain), custom_call_target="tpu_custom_call" | custom-call | flops 805306368 | bytes 9179136 | tf_op jit(solution)/shard_map/odd/pallas_call | solution.py:52
  13.5 1.3 %collective-permute-start.1 = (f32[192,512]{1,0:T(8,128)S(1)}, f32[192,512]{1,0:T(8,128)S(1)}, u32[]{:S(2)}, u32[]{:S(2)}) collective-permute-start(f32[192,512]{1,0:T(8,128)S(1)} %odd.3), channel_id=1, source_target_pairs={{1,2},{3,4},{5,6},{7,8},{9,10},{11,12},{13,14},{15,16},{17,18},{19... | collective-permute-start | bytes 1179656 | tf_op jit(solution)/shard_map/ppermute | solution.py:18
  14.8 0.0 collective-permute-done.hop
  14.9 2.4 %all-gather = f32[384,512]{1,0:T(8,128)S(1)} all-gather(f32[192,512]{1,0:T(8,128)S(1)} %even.3), channel_id=2, replica_groups=mesh['outer'=16,'far'=8,'near'=2,'core'=2] {'core'}, dimensions={0}, use_global_device_ids=true | all-gather | bytes 1179648 | tf_op jit(solution)/shard_map/all_gather | solution.py:22
  17.2 1.4 %odd.4 = f32[192,512]{1,0:T(8,128)S(1)} custom-call(f32[2,192,512]{2,1,0:T(8,128)S(1)} %bitcast.9, bf16[2,512,1024]{2,1,0:T(8,128)(2,1)S(1)} %get-tuple-element.12.weight_in, bf16[2,1024,512]{2,1,0:T(8,128)(2,1)S(1)} %get-tuple-element.13.weight_out, f32[2,512]{1,0:T(2,128)S(1)} %get-tuple-element.14.norm_gain), custom_call_target="tpu_custom_call" | custom-call | flops 805306368 | bytes 9179136 | tf_op jit(solution)/shard_map/odd/pallas_call | solution.py:52
  18.7 1.3 %collective-permute-start.2 = (f32[192,512]{1,0:T(8,128)S(1)}, f32[192,512]{1,0:T(8,128)S(1)}, u32[]{:S(2)}, u32[]{:S(2)}) collective-permute-start(f32[192,512]{1,0:T(8,128)S(1)} %odd.4), channel_id=1, source_target_pairs={{1,2},{3,4},{5,6},{7,8},{9,10},{11,12},{13,14},{15,16},{17,18},{19... | collective-permute-start | bytes 1179656 | tf_op jit(solution)/shard_map/ppermute | solution.py:18
  20.0 0.0 collective-permute-done.1.hop
  20.1 2.4 %all-gather.1 = f32[384,512]{1,0:T(8,128)S(1)} all-gather(f32[192,512]{1,0:T(8,128)S(1)} %even.4), channel_id=3, replica_groups=mesh['outer'=16,'far'=8,'near'=2,'core'=2] {'core'}, dimensions={0}, use_global_device_ids=true | all-gather | bytes 1179648 | tf_op jit(solution)/shard_map/all_gather | solution.py:22
  22.4 1.4 %odd.5 = f32[192,512]{1,0:T(8,128)S(1)} custom-call(f32[2,192,512]{2,1,0:T(8,128)S(1)} %bitcast.5, bf16[2,512,1024]{2,1,0:T(8,128)(2,1)S(1)} %get-tuple-element.12.weight_in, bf16[2,1024,512]{2,1,0:T(8,128)(2,1)S(1)} %get-tuple-element.13.weight_out, f32[2,512]{1,0:T(2,128)S(1)} %get-tuple-element.14.norm_gain), custom_call_target="tpu_custom_call" | custom-call | flops 805306368 | bytes 9179136 | tf_op jit(solution)/shard_map/odd/pallas_call | solution.py:52
  23.9 0.0 copy-start.2
  23.9 0.8 collective-permute-done.2.hop
  24.7 0.0 copy-done
  24.7 0.0 copy-done.2
  24.7 2.4 %all-gather.2 = f32[384,512]{1,0:T(8,128)S(1)} all-gather(f32[192,512]{1,0:T(8,128)S(1)} %even.5), channel_id=4, replica_groups=mesh['outer'=16,'far'=8,'near'=2,'core'=2] {'core'}, dimensions={0}, use_global_device_ids=true | all-gather | bytes 1179648 | tf_op jit(solution)/shard_map/all_gather | solution.py:22
  27.1 0.8 part.1
  27.9 17.6 %all-to-all-start = ((f32[16,24,128]{2,1,0:T(8,128)}), f32[16,24,128]{2,1,0:T(8,128)S(1)}, u32[]{:S(2)}, u32[]{:S(2)}) async-start(f32[16,24,128]{2,1,0:T(8,128)} %part.1), calls=%async_computation | async-start | bytes 393216 | tf_op jit(solution)/shard_map/all_to_all | solution.py:233
  45.4 4.8 %collective-permute-start.3 = (f32[192,512]{1,0:T(8,128)}, f32[192,512]{1,0:T(8,128)}, u32[]{:S(2)}, u32[]{:S(2)}) collective-permute-start(f32[192,512]{1,0:T(8,128)} %copy-done.2), channel_id=1, source_target_pairs={{1,2},{3,4},{5,6},{7,8},{9,10},{11,12},{13,14},{15,16},{17,18},{19... | collective-permute-start | bytes 1179656 | tf_op jit(solution)/shard_map/ppermute | solution.py:18
  50.3 8.1 %all-to-all-done.parts = f32[16,24,128]{2,1,0:T(8,128)S(1)} async-done(((f32[16,24,128]{2,1,0:T(8,128)}), f32[16,24,128]{2,1,0:T(8,128)S(1)}, u32[]{:S(2)}, u32[]{:S(2)}) %all-to-all-start) | async-done | bytes 196640 | tf_op jit(solution)/shard_map/all_to_all | solution.py:233
  58.3 0.7 own.1
  59.1 6.8 %all-to-all-start.1 = ((f32[16,32,128]{2,1,0:T(8,128)}), f32[16,32,128]{2,1,0:T(8,128)S(1)}, u32[]{:S(2)}, u32[]{:S(2)}) async-start(f32[16,32,128]{2,1,0:T(8,128)} %own.1), calls=%async_computation.1 | async-start | bytes 524288 | tf_op jit(solution)/shard_map/all_to_all | solution.py:243
  65.8 0.0 collective-permute-done.3.hop
  65.9 1.1 moved.1
  66.9 0.0 copy-start.3
  66.9 0.7 copy-done.3
  67.7 5.7 %all-to-all-done.1.heard = f32[16,32,128]{2,1,0:T(8,128)S(1)} async-done(((f32[16,32,128]{2,1,0:T(8,128)}), f32[16,32,128]{2,1,0:T(8,128)S(1)}, u32[]{:S(2)}, u32[]{:S(2)}) %all-to-all-start.1) | async-done | bytes 262176 | tf_op jit(solution)/shard_map/all_to_all | solution.py:243
  73.4 0.0 copy-start.1
  73.4 0.0 copy-start.4
  73.4 0.1 scan.1
  73.4 22.6 %all_to_all.15 = f32[8,48,128]{2,1,0:T(8,128)S(1)} all-to-all(f32[8,48,128]{2,1,0:T(8,128)S(1)} %scan.1), channel_id=1, replica_groups=mesh['outer'=16,'far'=8,'near'=2,'core'=2] {'far'}, dimensions={0} | all-to-all | bytes 393216 | tf_op jit(solution)/shard_map/all_to_all | solution.py:247
  96.1 12.2 %all-gather.3 = f32[32,48,128]{2,1,0:T(8,128)S(1)} all-gather(f32[8,48,128]{2,1,0:T(8,128)S(1)} %all_to_all.15), channel_id=5, replica_groups=mesh['outer'=16,'far'=8,'near'=2,'core'=2] {'near','core'}, dimensions={0}, use_global_device_ids=true | all-gather | bytes 983040 | tf_op jit(solution)/shard_map/all_gather | solution.py:248
  108.3 0.0 copy-done.1
  108.3 0.0 copy-done.4
  108.3 2.2 %last.1 = f32[1,192,512]{2,1,0:T(8,128)} custom-call(f32[4,8,48,128]{3,2,1,0:T(8,128)S(1)} %bitcast.10, f32[192,512]{1,0:T(8,128)S(1)} %copy-done.4, bf16[2,512,1024]{2,1,0:T(8,128)(2,1)S(1)} %get-tuple-element.12.weight_in, bf16[2,1024,512]{2,1,0:T(8,128)(2,1)S(1)} %copy-done.1, f32[2,512]{1,0:T(2,128)S(1)} %get-tuple-element.14.norm_gain), custom_call_target="tpu_custom_call" | custom-call | flops 805306368 | bytes 9572352 | tf_op jit(solution)/shard_map/last/pallas_call | solution.py:52
  (3 shorter events, 0.1 us)
Async XLA Ops:
  0.0 7.4 %copy-start.5 = (f32[1,192,512]{2,1,0:T(8,128)S(1)}, f32[1,192,512]{2,1,0:T(8,128)}, u32[]{:S(2)}) copy-start(f32[1,192,512]{2,1,0:T(8,128)} %param.7) | copy-start | bytes 1179652
  0.0 14.8 %collective-permute-start = (f32[192,512]{1,0:T(8,128)}, f32[192,512]{1,0:T(8,128)S(1)}, u32[]{:S(2)}, u32[]{:S(2)}) collective-permute-start(f32[192,512]{1,0:T(8,128)} %bitcast.11), channel_id=1, source_target_pairs={{1,2},{3,4},{5,6},{7,8},{9,10},{11,12},{13,14},{15,16},{17,18},{19... | collective-permute-start | bytes 1179656 | tf_op jit(solution)/shard_map/ppermute | solution.py:18
  7.4 17.3 %copy-start = (bf16[2,1024,512]{2,1,0:T(8,128)(2,1)}, bf16[2,1024,512]{2,1,0:T(8,128)(2,1)S(1)}, u32[]{:S(2)}) copy-start(bf16[2,1024,512]{2,1,0:T(8,128)(2,1)S(1)} %get-tuple-element.13.weight_out) | copy-start | bytes 6291460
  13.5 6.5 %collective-permute-start.1 = (f32[192,512]{1,0:T(8,128)S(1)}, f32[192,512]{1,0:T(8,128)S(1)}, u32[]{:S(2)}, u32[]{:S(2)}) collective-permute-start(f32[192,512]{1,0:T(8,128)S(1)} %odd.3), channel_id=1, source_target_pairs={{1,2},{3,4},{5,6},{7,8},{9,10},{11,12},{13,14},{15,16},{17,18},{19... | collective-permute-start | bytes 1179656 | tf_op jit(solution)/shard_map/ppermute | solution.py:18
  18.7 6.0 %collective-permute-start.2 = (f32[192,512]{1,0:T(8,128)S(1)}, f32[192,512]{1,0:T(8,128)S(1)}, u32[]{:S(2)}, u32[]{:S(2)}) collective-permute-start(f32[192,512]{1,0:T(8,128)S(1)} %odd.4), channel_id=1, source_target_pairs={{1,2},{3,4},{5,6},{7,8},{9,10},{11,12},{13,14},{15,16},{17,18},{19... | collective-permute-start | bytes 1179656 | tf_op jit(solution)/shard_map/ppermute | solution.py:18
  23.9 0.8 copy-start.2
  27.9 30.5 %all-to-all-start = ((f32[16,24,128]{2,1,0:T(8,128)}), f32[16,24,128]{2,1,0:T(8,128)S(1)}, u32[]{:S(2)}, u32[]{:S(2)}) async-start(f32[16,24,128]{2,1,0:T(8,128)} %part.1), calls=%async_computation | async-start | bytes 393216 | tf_op jit(solution)/shard_map/all_to_all | solution.py:233
  45.4 20.4 %collective-permute-start.3 = (f32[192,512]{1,0:T(8,128)}, f32[192,512]{1,0:T(8,128)}, u32[]{:S(2)}, u32[]{:S(2)}) collective-permute-start(f32[192,512]{1,0:T(8,128)} %copy-done.2), channel_id=1, source_target_pairs={{1,2},{3,4},{5,6},{7,8},{9,10},{11,12},{13,14},{15,16},{17,18},{19... | collective-permute-start | bytes 1179656 | tf_op jit(solution)/shard_map/ppermute | solution.py:18
  59.1 14.3 %all-to-all-start.1 = ((f32[16,32,128]{2,1,0:T(8,128)}), f32[16,32,128]{2,1,0:T(8,128)S(1)}, u32[]{:S(2)}, u32[]{:S(2)}) async-start(f32[16,32,128]{2,1,0:T(8,128)} %own.1), calls=%async_computation.1 | async-start | bytes 524288 | tf_op jit(solution)/shard_map/all_to_all | solution.py:243
  66.9 0.7 copy-start.3
  73.4 34.9 %copy-start.1 = (bf16[2,1024,512]{2,1,0:T(8,128)(2,1)S(1)}, bf16[2,1024,512]{2,1,0:T(8,128)(2,1)}, u32[]{:S(2)}) copy-start(bf16[2,1024,512]{2,1,0:T(8,128)(2,1)} %copy-done) | copy-start | bytes 6291460
  73.4 34.9 %copy-start.4 = (f32[192,512]{1,0:T(8,128)S(1)}, f32[192,512]{1,0:T(8,128)}, u32[]{:S(2)}) copy-start(f32[192,512]{1,0:T(8,128)} %copy-done.3) | copy-start | bytes 1179652
